TPU v7x, 32 devices: a whole 2x2x4 slice. The times are simulated.
32 devices in a mesh: expert: 4 (over y, x), fsdp: 8 (over z, core).
Axes of the slice: x: 2, y: 2, z: 4, core: 2. Of those that a mesh axis runs over, the one named last changes fastest.
Arguments:
- branch_wo: bfloat16 [4, 4096, 4096], P('expert', 'fsdp'), may hold values from -3 to 3
- context: bfloat16 [1024, 4096], P('fsdp', 'expert'), may hold values from -6 to 6
- residual: bfloat16 [1024, 4096], P('fsdp', 'expert'), may hold values from -160 to 160
- norm_gain: bfloat16 [4096], P('expert'), may hold values from 0.25 to 1.75
- router_w: bfloat16 [4096, 4], P('expert'), may hold values from -0.1875 to 0.1875
- gate_w: bfloat16 [4, 4096, 8192], P('expert', None, 'fsdp'), may hold values from -0.09375 to 0.09375
- up_w: bfloat16 [4, 4096, 8192], P('expert', None, 'fsdp'), may hold values from -0.09375 to 0.09375
- expert_ids: int32 [1024, 2], P('fsdp'), may hold values from 0 to 3, as said below
- slot_ids: int32 [1024, 2], P('fsdp'), may hold values from 0 to 95, as said below
- cot_hidden: bfloat16 [4, 768, 8192], P('expert', None, 'fsdp'), may hold values from -1.1953125 to 1.1953125
Outputs:
- merged_wo: bfloat16 [4096, 4096], P('fsdp', 'expert')
- hidden: bfloat16 [4, 768, 8192], P('expert', None, 'fsdp')
- grad_gate: bfloat16 [4, 4096, 8192], P('expert', None, 'fsdp')
- grad_up: bfloat16 [4, 4096, 8192], P('expert', None, 'fsdp')
Inputs may be any that keep to these rules, and one draw needn't show every extreme that they name: expert_ids[t, 0] and expert_ids[t, 1] differ. Within each aligned block of 128 tokens (the tokens of one index of fsdp) no expert is named more than 96 times, and some expert is named exactly 96 times in every block. Within each aligned block of 128 tokens the pairs (expert_ids[t, k], slot_ids[t, k]) are all different, and an expert named c times in the block uses exactly the slots 0 to c - 1.
All inputs are finite; a program needn't handle non-finite values.
Results may differ from a plain program's by a relative error of at most 0.015.
Values may be sent and summed in bfloat16 or wider, within the bound.
No kernel may reach another device: no remote copies, remote signals or barrier semaphores. Data moves between devices by JAX's collectives and lax.ppermute only.
A program may use at most 128 MiB of HBM per device.

v0:
```python
import jax
import jax.numpy as jnp
from jax import lax
from jax.sharding import PartitionSpec as P


def per_device(
    branch_wo,
    context,
    residual,
    norm_gain,
    router_w,
    gate_w,
    up_w,
    expert_ids,
    slot_ids,
    cot_hidden,
):
    experts = lax.axis_size("expert")
    my_index = lax.axis_index("expert")
    columns = context.shape[1]
    width_all = columns * experts
    capacity = cot_hidden.shape[1] // lax.axis_size("fsdp")
    local_branch = branch_wo[0].astype(jnp.float32)
    summed = lax.psum_scatter(
        local_branch.astype(jnp.bfloat16), "expert", scatter_dimension=1, tiled=True
    ).astype(jnp.float32)
    merged = (summed / experts).astype(jnp.bfloat16)
    full_context = lax.all_gather(context, "expert", axis=1, tiled=True)
    attention = jnp.dot(
        full_context,
        lax.all_gather(merged, "fsdp", axis=0, tiled=True),
        preferred_element_type=jnp.float32,
    )
    hstate = residual.astype(jnp.float32) + attention
    scaled = hstate * norm_gain.astype(jnp.float32)
    partial_logits = jnp.dot(scaled, router_w.astype(jnp.float32), precision=lax.Precision.HIGHEST)
    squares, logits = lax.psum((jnp.sum(hstate * hstate, axis=1), partial_logits), "expert")
    inverse = lax.rsqrt(squares / width_all + 1e-05)
    normed = (scaled * inverse[:, None]).astype(jnp.bfloat16)
    logits = logits * inverse[:, None]
    expert_range = jnp.arange(experts, dtype=jnp.int32)
    selected = (expert_ids[:, :, None] == expert_range[None, None, :]).astype(jnp.float32)
    picked = jnp.sum(selected * logits[:, None, :], axis=2)
    probs = jax.nn.sigmoid(picked - picked[:, ::-1])
    codes = expert_ids * capacity + slot_ids
    targets = jnp.arange(experts * capacity, dtype=jnp.int32)
    one_hot = jnp.any(codes[None, :, :] == targets[:, None, None], axis=2).astype(jnp.bfloat16)
    sent = jnp.dot(one_hot, normed, preferred_element_type=jnp.float32).astype(jnp.bfloat16)
    sent = sent.reshape(experts, capacity, columns)
    own_slots = my_index * capacity + jnp.arange(capacity, dtype=jnp.int32)
    matches = codes[None, :, :] == own_slots[:, None, None]
    slot_local = jnp.sum(jnp.where(matches, probs[None, :, :], 0.0), axis=(1, 2)).astype(
        jnp.bfloat16
    )
    arrived = lax.all_to_all(sent, "expert", split_axis=0, concat_axis=2, tiled=True)
    rows_local = arrived[0]
    gate_weight = gate_w[0]
    up_weight = up_w[0]
    all_rows, slot_weight = (
        lax.all_gather(rows_local, "fsdp", axis=0, tiled=True),
        lax.all_gather(slot_local, "fsdp", axis=0, tiled=True),
    )
    gate_pre = jnp.dot(all_rows, gate_weight, preferred_element_type=jnp.float32)
    up_pre = jnp.dot(all_rows, up_weight, preferred_element_type=jnp.float32)
    sig_gate = jax.nn.sigmoid(gate_pre)
    act_gate = gate_pre * sig_gate
    weight_col = slot_weight.astype(jnp.float32)[:, None]
    hidden = (weight_col * act_gate * up_pre).astype(jnp.bfloat16)
    d_pre = cot_hidden[0].astype(jnp.float32) * weight_col
    d_gate = (d_pre * up_pre * sig_gate * (1.0 + gate_pre * (1.0 - sig_gate))).astype(jnp.bfloat16)
    d_up = (d_pre * act_gate).astype(jnp.bfloat16)
    contract = (((0,), (0,)), ((), ()))
    grad_gate = lax.dot_general(all_rows, d_gate, contract, preferred_element_type=jnp.float32)
    grad_up = lax.dot_general(all_rows, d_up, contract, preferred_element_type=jnp.float32)
    return (
        merged,
        hidden[None],
        grad_gate.astype(jnp.bfloat16)[None],
        grad_up.astype(jnp.bfloat16)[None],
    )


def solution(mesh):
    placed = (
        P("expert", "fsdp", None),
        P("fsdp", "expert"),
        P("fsdp", "expert"),
        P("expert"),
        P("expert", None),
        P("expert", None, "fsdp"),
        P("expert", None, "fsdp"),
        P("fsdp", None),
        P("fsdp", None),
        P("expert", None, "fsdp"),
    )
    return jax.shard_map(
        per_device,
        mesh=mesh,
        in_specs=placed,
        out_specs=(
            P("fsdp", "expert"),
            P("expert", None, "fsdp"),
            P("expert", None, "fsdp"),
            P("expert", None, "fsdp"),
        ),
        check_vma=False,
    )
```

profile of v0, /device:TPU:0, one launch (start us, length us, event | category | flops | bytes accessed | tf_op | source)
XLA Modules:
  0.0 321.9 jit_solution(1076995394852777832)
XLA Ops:
  7.2 0.0 copy-start
  7.2 0.0 reduce-scatter.2.cloned.1.call-start
  7.2 0.0 copy-start.4
  7.2 0.0 copy-start.2
  7.3 0.0 copy-start.3
  7.3 0.0 copy-start.5
  7.3 0.6 reduce-scatter.2.cloned.1.call-update
  7.9 0.0 all-gather.6.cloned.1.call-start
  8.0 0.7 all-gather.6.cloned.1.call-update
  8.7 0.0 all-gather.4.cloned.1.call-start
  8.7 57.7 %reduce-scatter.2.cloned.1.call-done = bf16[512,1024]{1,0:T(8,128)(2,1)} async-done(((bf16[512,4096]{1,0:T(8,128)(2,1)}), bf16[512,1024]{1,0:T(8,128)(2,1)}) %reduce-scatter.2.cloned.1.call-update) | async-done | bytes 1048592 | tf_op jit(solution)/shard_map/reduce_scatter | solution.py:25
  66.4 2.4 multiply_convert_fusion.1
  68.8 0.0 all-gather.4.cloned.1.call-update
  68.8 0.0 all-gather.8.cloned.1.call-start
  68.9 0.0 copy-done.4
  68.9 0.0 copy-done.2
  68.9 0.2 copy.31
  69.1 0.0 copy-done.3
  69.1 0.0 copy-done.5
  69.2 25.9 %all-gather.6.cloned.1.call-done = bf16[128,4096]{1,0:T(8,128)(2,1)} async-done(((bf16[128,1024]{1,0:T(8,128)(2,1)}), bf16[128,4096]{1,0:T(8,128)(2,1)}) %all-gather.6.cloned.1.call-update) | async-done | bytes 1048592 | tf_op jit(solution)/shard_map/all_gather | solution.py:29
  95.0 84.4 %all-gather.4.cloned.1.call-done = bf16[4096,1024]{1,0:T(8,128)(2,1)} async-done(((bf16[512,1024]{1,0:T(8,128)(2,1)}), bf16[4096,1024]{1,0:T(8,128)(2,1)}) %all-gather.4.cloned.1.call-update) | async-done | bytes 8388624 | tf_op jit(solution)/shard_map/all_gather | solution.py:32
  179.4 6.1 %multiply_reduce_fusion = (f32[128]{0:T(128)S(1)}, f32[128,1024]{0,1:T(8,128)S(1)}) fusion(bf16[4096,1024]{1,0:T(8,128)(2,1)} %all-gather.4.cloned.1.call-done, bf16[128,4096]{1,0:T(8,128)(2,1)} %all-gather.6.cloned.1.call-done, bf16[128,1024]{0,1:T(8,128)(2,1)S(1)} %copy.31), kind=kOutput, calls=%fused_computation.27 | convolution fusion | flops 1074265984 | bytes 10224128 | tf_op jit(solution)/shard_map/dot_general | solution.py:30
  185.5 0.0 copy-done
  185.5 0.4 fusion.21
  185.9 9.9 %all-reduce.1 = (f32[128]{0:T(128)S(1)}, f32[128,4]{0,1:T(4,128)S(1)}) all-reduce(f32[128]{0:T(128)S(1)} %get-tuple-element.6, f32[128,4]{0,1:T(4,128)S(1)} %fusion.21), channel_id=1, replica_groups=mesh['expert'=4,'fsdp'=8] {'expert'}, use_global_device_ids=true, to_apply=%region_3.0 | all-reduce | flops 640 | bytes 5120 | tf_op jit(solution)/shard_map/psum | solution.py:38
  195.8 0.0 copy-start.8
  195.8 0.5 convolution_convert_fusion
  196.2 12.4 %all_to_all.15 = bf16[4,96,1024]{2,1,0:T(8,128)(2,1)S(1)} all-to-all(bf16[4,96,1024]{2,1,0:T(8,128)(2,1)S(1)} %bitcast.45), channel_id=1, replica_groups=mesh['expert'=4,'fsdp'=8] {'expert'}, dimensions={0} | all-to-all | bytes 1572864 | tf_op jit(solution)/shard_map/all_to_all | solution.py:56
  208.7 0.6 copy.32
  209.3 1.1 copy.33
  210.4 0.0 all-gather.8.cloned.1.call-update
  210.5 0.0 copy-done.8
  210.5 0.6 dynamic-slice
  211.8 0.2 select_reduce_fusion
  212.0 0.2 dynamic-update-slice
  212.2 14.3 %all-reduce = bf16[768]{0:T(1024)(128)(2,1)S(1)} all-reduce(bf16[768]{0:T(1024)(128)(2,1)S(1)} %dynamic-update-slice), channel_id=1, replica_groups=mesh['expert'=4,'fsdp'=8] {'fsdp'}, use_global_device_ids=true, to_apply=%add | all-reduce | flops 768 | bytes 3072
  226.6 46.0 %all-gather.8.cloned.1.call-done = bf16[768,4096]{1,0:T(8,128)(2,1)} async-done(((bf16[96,4096]{1,0:T(8,128)(2,1)}), bf16[768,4096]{1,0:T(8,128)(2,1)}) %all-gather.8.cloned.1.call-update) | async-done | bytes 6291472 | tf_op jit(solution)/shard_map/all_gather | solution.py:61
  272.5 0.0 copy-start.6
  272.5 11.9 %fusion.2 = f32[768,1024]{1,0:T(8,128)S(1)} fusion(bf16[768,4096]{1,0:T(8,128)(2,1)} %all-gather.8.cloned.1.call-done, bf16[1,4096,1024]{2,1,0:T(8,128)(2,1)} %param.15), kind=kOutput, calls=%fused_computation.2 | convolution fusion | flops 6442450944 | bytes 17825792 | tf_op jit(solution)/shard_map/dot_general | solution.py:64
  284.5 0.0 copy-done.6
  284.5 9.0 %fusion = f32[768,1024]{1,0:T(8,128)S(1)} fusion(bf16[768,4096]{1,0:T(8,128)(2,1)S(1)} %copy-done.6, bf16[1,4096,1024]{2,1,0:T(8,128)(2,1)} %param.16), kind=kOutput, calls=%fused_computation | convolution fusion | flops 6442450944 | bytes 17825792 | tf_op jit(solution)/shard_map/dot_general | solution.py:65
  293.5 0.0 copy-start.7
  293.5 2.0 fusion.11
  295.5 0.0 copy-done.7
  295.6 10.1 %convert_bitcast_fusion.1 = bf16[1,4096,1024]{2,1,0:T(8,128)(2,1)} fusion(bf16[768,4096]{1,0:T(8,128)(2,1)S(1)} %copy-done.6, f32[768,1024]{1,0:T(8,128)S(1)} %fusion, f32[768,1024]{1,0:T(8,128)S(1)} %fusion.2, bf16[1,768,1024]{2,1,0:T(8,128)(2,1)S(1)} %copy-done.7, f32[768]{0:T(1024)S(1)} %convert_element_type.55), kind=kOutput, calls=%fused_computation.5 | convolution fusion | flops 6456082432 | bytes 22547456 | tf_op jit(solution)/shard_map/dot_general | solution.py:74
  305.6 0.0 copy-start.1
  305.6 9.7 %convert_bitcast_fusion = bf16[1,4096,1024]{2,1,0:T(8,128)(2,1)} fusion(bf16[768,4096]{1,0:T(8,128)(2,1)S(1)} %copy-done.6, bf16[1,768,1024]{2,1,0:T(8,128)(2,1)S(1)} %copy-done.7, f32[768]{0:T(1024)S(1)} %convert_element_type.55, f32[768,1024]{1,0:T(8,128)S(1)} %fusion.2), kind=kOutput, calls=%fused_computation.4 | convolution fusion | flops 6452936704 | bytes 19401728 | tf_op jit(solution)/shard_map/dot_general | solution.py:75
  315.3 0.0 copy-done.1
  (11 shorter events, 0.1 us)
Async XLA Ops:
  7.2 178.3 %copy-start = (bf16[1024,4]{0,1:T(4,128)(2,1)S(1)}, bf16[1024,4]{0,1:T(4,128)(2,1)}, u32[]{:S(2)}) copy-start(bf16[1024,4]{0,1:T(4,128)(2,1)} %param.14) | copy-start | bytes 24580
  7.2 59.2 %reduce-scatter.2.cloned.1.call-start = ((), (), s32[]{:S(2)}) async-start(), calls=%async_computation.2 | async-start | bytes 5242880 | tf_op jit(solution)/shard_map/reduce_scatter | solution.py:25
  7.2 61.6 %copy-start.4 = (bf16[1024]{0:T(1024)(128)(2,1)S(1)}, bf16[1024]{0:T(1024)(128)(2,1)}, u32[]{:S(2)}) copy-start(bf16[1024]{0:T(1024)(128)(2,1)} %param.13) | copy-start | bytes 6148
  7.2 61.6 %copy-start.2 = (bf16[128,1024]{1,0:T(8,128)(2,1)S(1)}, bf16[128,1024]{1,0:T(8,128)(2,1)}, u32[]{:S(2)}) copy-start(bf16[128,1024]{1,0:T(8,128)(2,1)} %param.12) | copy-start | bytes 786436
  7.3 61.8 %copy-start.3 = (s32[128,2]{0,1:T(2,128)S(1)}, s32[128,2]{0,1:T(2,128)}, u32[]{:S(2)}) copy-start(s32[128,2]{0,1:T(2,128)} %param.17) | copy-start | bytes 3076
  7.3 61.8 %copy-start.5 = (s32[128,2]{0,1:T(2,128)S(1)}, s32[128,2]{0,1:T(2,128)}, u32[]{:S(2)}) copy-start(s32[128,2]{0,1:T(2,128)} %param.18) | copy-start | bytes 3076
  7.9 87.1 %all-gather.6.cloned.1.call-start = ((), (), s32[]{:S(2)}) async-start(), calls=%async_computation.4 | async-start | bytes 1310720 | tf_op jit(solution)/shard_map/all_gather | solution.py:29
  8.7 170.7 %all-gather.4.cloned.1.call-start = ((), (), s32[]{:S(2)}) async-start(), calls=%async_computation.3 | async-start | bytes 9437184 | tf_op jit(solution)/shard_map/all_gather | solution.py:32
  68.8 203.7 %all-gather.8.cloned.1.call-start = ((), (), s32[]{:S(2)}) async-start(), calls=%async_computation.5 | async-start | bytes 7077888 | tf_op jit(solution)/shard_map/all_gather | solution.py:61
  195.8 14.7 %copy-start.8 = (u32[32]{0:T(128)S(1)}, u32[32]{0:T(128)}, u32[]{:S(2)}) copy-start(u32[32]{0:T(128)} %constant.30) | copy-start | bytes 388
  272.5 12.0 %copy-start.6 = (bf16[768,4096]{1,0:T(8,128)(2,1)S(1)}, bf16[768,4096]{1,0:T(8,128)(2,1)}, u32[]{:S(2)}) copy-start(bf16[768,4096]{1,0:T(8,128)(2,1)} %all-gather.8.cloned.1.call-done) | copy-start | bytes 18874372
  293.5 2.0 copy-start.7
  305.6 9.7 %copy-start.1 = (bf16[1024,4]{0,1:T(4,128)(2,1)S(1)}, bf16[1024,4]{0,1:T(4,128)(2,1)}, u32[]{:S(2)}) copy-start(bf16[1024,4]{0,1:T(4,128)(2,1)} %param.14) | copy-start | bytes 24580
Sparse Core Ops, SparseCore 0:
  11.0 55.3 reduce-scatter.1
  68.4 26.5 all-gather.5
  97.3 82.0 all-gather.3
  210.6 61.9 all-gather.7
where the time goes:
time: 322 us
  waiting for transfers between devices  215 us (67%)
  matrix products  47.7 us (15%)
  blocking collectives  36.6 us (11%)
  between operations  14.6 us (5%)
  other arithmetic  4.71 us (1%)
    all_gather x1, waiting for transfers between devices, per_device(): lax.all_gather(merged, 'fsdp', axis=0, tiled=True)  84.4 us
    reduce_scatter x1, waiting for transfers between devices, per_device(): lax.psum_scatter(local_branch.astype(jnp.bfloat16), 'expert', scatter_dim...  57.7 us
    all_gather x1, waiting for transfers between devices, per_device(): lax.all_gather(rows_local, 'fsdp', axis=0, tiled=True)  46 us
    all_gather x1, waiting for transfers between devices, per_device(): full_context = lax.all_gather(context, 'expert', axis=1, tiled=True)  25.9 us
    unnamed x1, blocking collectives  14.3 us
    all_to_all x1, blocking collectives, per_device(): lax.all_to_all(sent, 'expert', split_axis=0, concat_axis=2, tiled=True)  12.4 us
    dot_general x1, matrix products, per_device(): jnp.dot(all_rows, gate_weight, preferred_element_type=jnp.float32)  11.9 us
    dot_general x1, matrix products, per_device(): lax.dot_general(all_rows, d_gate, contract, preferred_element_type=jnp.fl...  10.1 us
  transfers between devices with their start and end apart: 4, of which 4 were waited for; matrix products, arithmetic and copies ran while one was open for 1% of the time, Pallas kernels for 0%

commit v1 on v0

v1 whole, which is shorter than its diff:
```python
import jax
import jax.numpy as jnp
from jax import lax
from jax.sharding import PartitionSpec as P

CHUNKS = 2


def exchange(value, axis, offset):
    size = lax.axis_size(axis)
    return lax.ppermute(value, axis, [(i, i ^ offset) for i in range(size)])


def pick(value, index, axis):
    return lax.dynamic_index_in_dim(value, index, axis, keepdims=False)


def pad_rows(value, multiple):
    return jnp.pad(value, ((0, -value.shape[0] % multiple), (0, 0)))


def branch_sum(branch, expert, experts, columns, start, count):
    half = branch.shape[0] // 2
    bits = [1 << i for i in range(experts.bit_length() - 1)]
    halves = []
    for rows, order in ((branch[:half], bits), (branch[half:], bits[::-1])):
        held = {
            k: lax.dynamic_slice_in_dim(rows, (expert ^ k) * columns + start, count, 1)
            for k in range(experts)
        }
        for bit in order:
            away = [k for k in held if k & bit]
            sent = jnp.stack([held[k].astype(jnp.bfloat16) for k in away])
            got = exchange(sent, "expert", bit)
            held = {
                k ^ bit: held[k ^ bit].astype(jnp.float32) + got[i].astype(jnp.float32)
                for i, k in enumerate(away)
            }
        halves.append(held[0])
    return jnp.concatenate(halves)


def per_device(
    branch_wo,
    context,
    residual,
    norm_gain,
    router_w,
    gate_w,
    up_w,
    expert_ids,
    slot_ids,
    cot_hidden,
):
    experts = lax.axis_size("expert")
    blocks = lax.axis_size("fsdp")
    planes = blocks // 2
    expert = lax.axis_index("expert")
    block = lax.axis_index("fsdp")
    plane, core = block // 2, block % 2
    tokens, columns = context.shape
    width = columns * experts
    features = width // blocks
    capacity = cot_hidden.shape[1] // blocks
    hidden_units = cot_hidden.shape[2]
    part = columns // CHUNKS

    extra = jnp.concatenate([norm_gain[None], router_w.T])
    packed = pad_rows(jnp.concatenate([context, extra]), 16)
    full = jnp.zeros((packed.shape[0], width), jnp.bfloat16)
    for k in range(experts):
        piece = exchange(packed, "expert", k) if k else packed
        full = lax.dynamic_update_slice_in_dim(full, piece, (expert ^ k) * columns, 1)
    gain_all = full[tokens].astype(jnp.float32)
    router_all = full[tokens + 1 : tokens + 1 + experts]

    ids = jnp.concatenate([expert_ids, slot_ids], axis=1).astype(jnp.bfloat16)
    id_rows = ids.size // features
    to_blocks = jnp.concatenate(
        [
            full[:tokens].reshape(tokens, blocks, features).transpose(1, 0, 2),
            jnp.broadcast_to(ids.reshape(1, id_rows, features), (blocks, id_rows, features)),
        ],
        axis=1,
    )
    to_blocks = jnp.pad(to_blocks, ((0, 0), (0, -to_blocks.shape[1] % 16), (0, 0)))
    from_blocks = lax.all_to_all(to_blocks, "fsdp", split_axis=0, concat_axis=0, tiled=True)
    context_rows = from_blocks[:, :tokens].reshape(planes, 2, tokens, features)
    ids_all = from_blocks[:, tokens : tokens + id_rows].reshape(planes, 2, tokens, 2, 2)
    ids_all = jnp.stack([pick(ids_all, plane ^ k, 0) for k in range(planes)])
    ids_all = ids_all.astype(jnp.int32)
    expert_of, slot_of = ids_all[:, :, :, 0], ids_all[:, :, :, 1]
    context_sides = [
        pick(context_rows, side, 1).reshape(planes * tokens, features) for side in (core, 1 - core)
    ]
    codes = pick(expert_of * capacity + slot_of, core, 1)

    def slot_choice(which):
        targets = which * capacity + jnp.arange(capacity, dtype=jnp.int32)
        one_hot = jnp.any(codes[:, None] == targets[None, :, None, None], axis=3)
        return one_hot.astype(jnp.bfloat16)

    choices = [slot_choice(expert ^ k) for k in range(experts)]

    own_slots = jnp.arange(capacity, dtype=jnp.int32)
    hits = (slot_of[:, :, None] == own_slots[:, None, None]) & (expert_of[:, :, None] == expert)
    expert_range = jnp.arange(experts, dtype=jnp.int32)
    chosen = (expert_of[..., None] == expert_range).astype(jnp.float32)
    signs = chosen - chosen[:, :, :, ::-1]
    signs = jnp.einsum("pcstk,pctke->pcse", hits.astype(jnp.float32), signs).reshape(-1, experts)
    filled = jnp.any(hits, axis=(3, 4)).reshape(-1, 1)

    merged_parts = []
    row_parts = []
    for c in range(CHUNKS):
        span = slice(c * part, (c + 1) * part)
        summed = branch_sum(branch_wo[0], expert, experts, columns, c * part, part)
        merged = (summed / experts).astype(jnp.bfloat16)
        merged_parts.append(merged)

        def attend(rows):
            out = jnp.dot(rows, merged, preferred_element_type=jnp.float32)
            return out.reshape(planes, tokens, part)

        swapped = exchange(attend(context_sides[1]).astype(jnp.bfloat16), "fsdp", 1)
        pair = attend(context_sides[0]) + swapped.astype(jnp.float32)
        pair_sent = pair.astype(jnp.bfloat16)
        hstate = residual[:, span].astype(jnp.float32) + pick(pair, plane, 0)
        for k in range(1, planes):
            arrived = exchange(pick(pair_sent, plane ^ k, 0), "fsdp", 2 * k)
            hstate = hstate + arrived.astype(jnp.float32)
        scaled = (hstate * norm_gain[span].astype(jnp.float32)).astype(jnp.bfloat16)
        own_tokens = jnp.stack(
            [exchange(scaled, "fsdp", 2 * k) if k else scaled for k in range(planes)]
        )

        rows_half = jnp.zeros((planes, capacity, experts * part), jnp.bfloat16)
        for k in range(experts):
            piece = lax.dot_general(
                choices[k],
                own_tokens,
                (((2,), (1,)), ((0,), (0,))),
                preferred_element_type=jnp.float32,
            ).astype(jnp.bfloat16)
            if k > 0:
                piece = exchange(piece, "expert", k)
            rows_half = lax.dynamic_update_slice_in_dim(rows_half, piece, (expert ^ k) * part, 2)
        rows_other = exchange(rows_half, "fsdp", 1)
        first = jnp.where(core == 0, rows_half, rows_other)
        second = jnp.where(core == 0, rows_other, rows_half)
        row_parts.append(jnp.stack([first, second], axis=1).reshape(-1, experts, part))

    by_part = lambda value: value.reshape(value.shape[:-1] + (experts, CHUNKS, part))
    gains = by_part(gain_all)
    routers = by_part(router_all)
    gate_by_part = gate_w[0].reshape(experts, CHUNKS, part, hidden_units)
    up_by_part = up_w[0].reshape(experts, CHUNKS, part, hidden_units)
    squares = logits = gate_pre = up_pre = 0.0
    for c in range(CHUNKS):
        rows = row_parts[c]
        squares += jnp.sum((rows.astype(jnp.float32) / gains[:, c]) ** 2, axis=(1, 2))
        logits += jnp.einsum(
            "rep,kep->rk", rows, routers[:, :, c], preferred_element_type=jnp.float32
        )
        for k in range(experts):
            gate_pre += jnp.dot(rows[:, k], gate_by_part[k, c], preferred_element_type=jnp.float32)
            up_pre += jnp.dot(rows[:, k], up_by_part[k, c], preferred_element_type=jnp.float32)
    inverse_col = lax.rsqrt(squares[:, None] / width + 1e-05)
    margin = jnp.sum(logits * signs, axis=1, keepdims=True) * inverse_col
    weight_col = jnp.where(filled, jax.nn.sigmoid(margin), 0.0)
    weight_col = weight_col.astype(jnp.bfloat16).astype(jnp.float32)

    def reorder(value):
        value = value.reshape(planes, -1, hidden_units)
        return jnp.stack([pick(value, plane ^ k, 0) for k in range(planes)]).reshape(-1, hidden_units)

    gate_pre = inverse_col * gate_pre
    up_pre = inverse_col * up_pre
    sig_gate = jax.nn.sigmoid(gate_pre)
    act_gate = gate_pre * sig_gate
    hidden = reorder((weight_col * act_gate * up_pre).astype(jnp.bfloat16))
    d_pre = reorder(cot_hidden[0]).astype(jnp.float32) * (weight_col * inverse_col)
    d_gate = (d_pre * up_pre * sig_gate * (1.0 + gate_pre * (1.0 - sig_gate))).astype(jnp.bfloat16)
    d_up = (d_pre * act_gate).astype(jnp.bfloat16)
    all_rows = jnp.stack(row_parts, axis=2).reshape(-1, width)
    contract = (((0,), (0,)), ((), ()))
    grad_gate = lax.dot_general(all_rows, d_gate, contract, preferred_element_type=jnp.float32)
    grad_up = lax.dot_general(all_rows, d_up, contract, preferred_element_type=jnp.float32)
    return (
        jnp.concatenate(merged_parts, axis=1),
        hidden[None],
        grad_gate.astype(jnp.bfloat16)[None],
        grad_up.astype(jnp.bfloat16)[None],
    )


def solution(mesh):
    placed = (
        P("expert", "fsdp", None),
        P("fsdp", "expert"),
        P("fsdp", "expert"),
        P("expert"),
        P("expert", None),
        P("expert", None, "fsdp"),
        P("expert", None, "fsdp"),
        P("fsdp", None),
        P("fsdp", None),
        P("expert", None, "fsdp"),
    )
    return jax.shard_map(
        per_device,
        mesh=mesh,
        in_specs=placed,
        out_specs=(
            P("fsdp", "expert"),
            P("expert", None, "fsdp"),
            P("expert", None, "fsdp"),
            P("expert", None, "fsdp"),
        ),
        check_vma=False,
    )
```

time: 322 us -> 365 us (1.13); the launches traced: 322 us -> 359 us
  waiting for transfers between devices: 215 us -> 79.9 us
  local copies, waits for them, and re-layouts: 2.82 us -> 86.6 us
  matrix products: 47.7 us -> 110 us
  starting transfers between devices: 0.16 us -> 45.7 us
  blocking collectives: 36.6 us -> 0 us
  other arithmetic: 4.71 us -> 36 us
  between operations: 14.6 us -> 1.69 us
    all_gather x3 -> x0, waiting for transfers between devices: 156 us -> none  [the longest x1 84.4 us: per_device(): lax.all_gather(merged, 'fsdp', axis=0, tiled=True)]
    ppermute x0 -> x33, waiting for transfers between devices: none -> 77.8 us  [exchange(): return lax.ppermute(value, axis, [(i, i ^ offset) for i in range(size)])]
    dot_general x5 -> x31, matrix products: 27.9 us -> 87.4 us  [the longest x8 37.8 us: per_device(): jnp.dot(rows[:, k], gate_by_part[k, c], preferred_element_type=jnp.float32)]
    reduce_scatter x1 -> x0, waiting for transfers between devices: 57.7 us -> none  [per_device(): lax.psum_scatter(local_branch.astype(jnp.bfloat16), 'expert', scatter_dim...]
    ppermute x0 -> x33, starting transfers between devices: none -> 40.5 us  [exchange(): return lax.ppermute(value, axis, [(i, i ^ offset) for i in range(size)])]
    another operation x0 -> x8, local copies, waits for them, and re-layouts: none -> 26.7 us  [the longest x3 23.1 us: per_device(): all_rows = jnp.stack(row_parts, axis=2).reshape(-1, width)]
    slice x0 -> x8, local copies, waits for them, and re-layouts: none -> 22.6 us  [the longest x2 16.4 us: per_device(): rows[:, k]]
    another operation x0 -> x13, other arithmetic: none -> 19.9 us  [the longest x1 9.3 us: per_device(): all_rows = jnp.stack(row_parts, axis=2).reshape(-1, width)]
  transfers between devices with their start and end apart: 4 -> 34, of which waited for: 4 -> 19; matrix products, arithmetic and copies ran while one was open for 1% -> 22% of each run, Pallas kernels for 0% -> 0%
where the time goes in v1:
time: 365 us; the launch traced here: 359 us
  matrix products  110 us (30%)
  local copies, waits for them, and re-layouts  86.6 us (24%)
  waiting for transfers between devices  79.9 us (22%)
  starting transfers between devices  45.7 us (13%)
  other arithmetic  36 us (10%)
    ppermute x33, waiting for transfers between devices, exchange(): return lax.ppermute(value, axis, [(i, i ^ offset) for i in range(size)])  77.8 us
    ppermute x33, starting transfers between devices, exchange(): return lax.ppermute(value, axis, [(i, i ^ offset) for i in range(size)])  40.5 us
    dot_general x8, matrix products, per_device(): jnp.dot(rows[:, k], gate_by_part[k, c], preferred_element_type=jnp.float32)  37.8 us
    dot_general x8, matrix products, per_device(): jnp.dot(rows[:, k], up_by_part[k, c], preferred_element_type=jnp.float32)  34.9 us
    another operation x3, local copies, waits for them, and re-layouts, per_device(): all_rows = jnp.stack(row_parts, axis=2).reshape(-1, width)  23.1 us
    slice x2, local copies, waits for them, and re-layouts, per_device(): rows[:, k]  16.4 us
    dot_general x1, matrix products, per_device(): lax.dot_general(all_rows, d_up, contract, preferred_element_type=jnp.floa...  12.6 us
    unnamed x55, local copies, waits for them, and re-layouts  12.6 us
  transfers between devices with their start and end apart: 34, of which 19 were waited for; matrix products, arithmetic and copies ran while one was open for 22% of the time, Pallas kernels for 0%

profile of v1, /device:TPU:0, one launch (start us, length us, event | category | flops | bytes accessed | tf_op | source)
XLA Modules:
  0.0 359.5 jit_solution(281013619065167835)
XLA Ops:
  4.7 2.9 collective-permute-start.8
  9.2 4.7 %fusion.137 = (bf16[1,256,4096]{2,1,0:T(8,128)(2,1)}, bf16[1,256,4096]{2,1,0:T(8,128)(2,1)}) fusion(bf16[1,512,4096]{2,1,0:T(8,128)(2,1)} %param.10), kind=kLoop, calls=%fused_computation.247 | loop fusion | bytes 8388608 | tf_op jit(solution)/shard_map/slice | solution.py:26
  16.1 2.0 collective-permute-start.2
  25.2 2.0 collective-permute-start
  28.3 5.7 %collective-permute-done.9 = bf16[144,1024]{0,1:T(8,128)(2,1)S(1)} collective-permute-done((bf16[144,1024]{0,1:T(8,128)(2,1)}, bf16[144,1024]{0,1:T(8,128)(2,1)S(1)}, u32[]{:S(2)}, u32[]{:S(2)}) %collective-permute-start.9) | collective-permute-done | bytes 294944 | tf_op jit(solution)/shard_map/ppermute | solution.py:11
  34.7 1.8 pad_maximum_fusion.3
  36.5 2.8 copy.187
  40.5 5.2 %all-to-all-start = ((bf16[8,144,512]{2,1,0:T(8,128)(2,1)}), bf16[8,144,512]{2,1,0:T(8,128)(2,1)S(1)}, u32[]{:S(2)}, u32[]{:S(2)}) async-start(bf16[8,144,512]{2,1,0:T(8,128)(2,1)} %pad.9.clone), calls=%async_computation | async-start | bytes 2359296 | tf_op jit(solution)/shard_map/all_to_all | solution.py:87
  46.8 2.0 collective-permute-start.3
  52.9 3.7 %collective-permute-done.6 = bf16[2,256,512]{2,1,0:T(8,128)(2,1)} collective-permute-done((bf16[2,256,512]{2,1,0:T(8,128)(2,1)}, bf16[2,256,512]{2,1,0:T(8,128)(2,1)}, u32[]{:S(2)}, u32[]{:S(2)}) %collective-permute-start.6) | collective-permute-done | bytes 524320 | tf_op jit(solution)/shard_map/ppermute | solution.py:11
  56.5 2.6 collective-permute-done.3
  60.5 1.8 collective-permute-start.7
  65.4 2.7 collective-permute-done.7
  73.0 2.1 all-to-all-done
  84.0 2.8 collective-permute-start.12
  90.8 2.1 collective-permute-start.23
  92.9 3.6 collective-permute-done.13
  96.4 2.8 collective-permute-done.25
  99.2 7.5 %collective-permute-done.24 = bf16[128,512]{1,0:T(8,128)(2,1)S(1)} collective-permute-done((bf16[128,512]{1,0:T(8,128)(2,1)S(1)}, bf16[128,512]{1,0:T(8,128)(2,1)S(1)}, u32[]{:S(2)}, u32[]{:S(2)}) %collective-permute-start.24) | collective-permute-done | bytes 131104 | tf_op jit(solution)/shard_map/ppermute | solution.py:11
  107.0 2.5 collective-permute-start.28
  109.4 2.0 collective-permute-start.26
  111.6 3.7 %collective-permute-done.28 = bf16[128,512]{1,0:T(8,128)(2,1)S(1)} collective-permute-done((bf16[128,512]{1,0:T(8,128)(2,1)S(1)}, bf16[128,512]{1,0:T(8,128)(2,1)S(1)}, u32[]{:S(2)}, u32[]{:S(2)}) %collective-permute-start.28) | collective-permute-done | bytes 131104 | tf_op jit(solution)/shard_map/ppermute | solution.py:11
  115.3 4.6 %collective-permute-done.27 = bf16[128,512]{1,0:T(8,128)(2,1)S(1)} collective-permute-done((bf16[128,512]{1,0:T(8,128)(2,1)S(1)}, bf16[128,512]{1,0:T(8,128)(2,1)S(1)}, u32[]{:S(2)}, u32[]{:S(2)}) %collective-permute-start.27) | collective-permute-done | bytes 131104 | tf_op jit(solution)/shard_map/ppermute | solution.py:11
  120.2 2.0 collective-permute-start.29
  124.8 7.3 %collective-permute-done.29 = bf16[4,96,512]{2,1,0:T(8,128)(2,1)S(1)} collective-permute-done((bf16[4,96,512]{2,1,0:T(8,128)(2,1)S(1)}, bf16[4,96,512]{2,1,0:T(8,128)(2,1)S(1)}, u32[]{:S(2)}, u32[]{:S(2)}) %collective-permute-start.29) | collective-permute-done | bytes 393248 | tf_op jit(solution)/shard_map/ppermute | solution.py:11
  132.2 9.4 %collective-permute-done.30 = bf16[4,96,512]{2,1,0:T(8,128)(2,1)S(1)} collective-permute-done((bf16[4,96,512]{2,1,0:T(8,128)(2,1)S(1)}, bf16[4,96,512]{2,1,0:T(8,128)(2,1)S(1)}, u32[]{:S(2)}, u32[]{:S(2)}) %collective-permute-start.30) | collective-permute-done | bytes 393248 | tf_op jit(solution)/shard_map/ppermute | solution.py:11
  143.4 2.9 collective-permute-start.15
  147.1 3.2 collective-permute-done.17
  150.3 5.1 %collective-permute-done.16 = bf16[128,512]{1,0:T(8,128)(2,1)} collective-permute-done((bf16[128,512]{1,0:T(8,128)(2,1)S(1)}, bf16[128,512]{1,0:T(8,128)(2,1)}, u32[]{:S(2)}, u32[]{:S(2)}) %collective-permute-start.16) | collective-permute-done | bytes 131104 | tf_op jit(solution)/shard_map/ppermute | solution.py:11
  164.3 2.0 fusion.17
  166.3 2.4 collective-permute-done.18
  169.5 8.7 %collective-permute-done.19 = bf16[4,96,512]{2,1,0:T(8,128)(2,1)S(1)} collective-permute-done((bf16[4,96,512]{2,1,0:T(8,128)(2,1)S(1)}, bf16[4,96,512]{2,1,0:T(8,128)(2,1)S(1)}, u32[]{:S(2)}, u32[]{:S(2)}) %collective-permute-start.19) | collective-permute-done | bytes 393248 | tf_op jit(solution)/shard_map/ppermute | solution.py:11
  181.6 1.9 pad_maximum_fusion.2
  183.6 4.8 %reshape.226 = bf16[768,4,512]{2,1,0:T(4,128)(2,1)S(1)} reshape(bf16[4,2,96,2048]{3,2,1,0:T(8,128)(2,1)} %pad_maximum_fusion.2) | data formatting | bytes 6291456 | tf_op jit(solution)/shard_map/reshape | solution.py:151
  188.4 5.6 %fusion.138 = (bf16[768,1,512]{2,1,0:T(2,128)(2,1)}, bf16[768,1,512]{2,1,0:T(2,128)(2,1)S(1)}, bf16[768,1,512]{2,1,0:T(2,128)(2,1)S(1)}, bf16[768,1,512]{2,1,0:T(2,128)(2,1)S(1)}) fusion(bf16[768,4,512]{2,1,0:T(4,128)(2,1)S(1)} %reshape.226), kind=kLoop, calls=%fused_computation.248 | loop fusion | bytes 6291456 | tf_op jit(solution)/shard_map/slice | solution.py:166
  194.0 3.9 %fusion.40 = f32[768,1024]{1,0:T(8,128)} fusion(bf16[4,2,512,1024]{3,2,1,0:T(8,128)(2,1)} %bitcast.262, bf16[768,1,512]{2,1,0:T(2,128)(2,1)S(1)} %get-tuple-element.15), kind=kOutput, calls=%fused_computation.69 | convolution fusion | flops 805306368 | bytes 4980736 | tf_op jit(solution)/shard_map/dot_general | solution.py:166
  197.9 3.9 %fusion.41 = f32[768,1024]{1,0:T(8,128)} fusion(bf16[4,2,512,1024]{3,2,1,0:T(8,128)(2,1)} %bitcast.263, bf16[768,1,512]{2,1,0:T(2,128)(2,1)S(1)} %get-tuple-element.16), kind=kOutput, calls=%fused_computation.71 | convolution fusion | flops 805306368 | bytes 4980736 | tf_op jit(solution)/shard_map/dot_general | solution.py:166
  201.8 3.8 %fusion.33 = f32[768,1024]{1,0:T(8,128)} fusion(bf16[4,2,512,1024]{3,2,1,0:T(8,128)(2,1)} %bitcast.270, bf16[768,1,512]{2,1,0:T(2,128)(2,1)S(1)} %get-tuple-element.15), kind=kOutput, calls=%fused_computation.54 | convolution fusion | flops 805306368 | bytes 4980736 | tf_op jit(solution)/shard_map/dot_general | solution.py:167
  205.6 3.9 %fusion.34 = f32[768,1024]{1,0:T(8,128)} fusion(bf16[4,2,512,1024]{3,2,1,0:T(8,128)(2,1)} %bitcast.271, bf16[768,1,512]{2,1,0:T(2,128)(2,1)S(1)} %get-tuple-element.16), kind=kOutput, calls=%fused_computation.56 | convolution fusion | flops 805306368 | bytes 4980736 | tf_op jit(solution)/shard_map/dot_general | solution.py:167
  209.5 3.9 %fusion.42 = f32[768,1024]{1,0:T(8,128)} fusion(bf16[4,2,512,1024]{3,2,1,0:T(8,128)(2,1)} %bitcast.264, bf16[768,1,512]{2,1,0:T(2,128)(2,1)S(1)} %get-tuple-element.17), kind=kOutput, calls=%fused_computation.73 | convolution fusion | flops 805306368 | bytes 4980736 | tf_op jit(solution)/shard_map/dot_general | solution.py:166
  213.4 3.9 %fusion.35 = f32[768,1024]{1,0:T(8,128)} fusion(bf16[4,2,512,1024]{3,2,1,0:T(8,128)(2,1)} %bitcast.272, bf16[768,1,512]{2,1,0:T(2,128)(2,1)S(1)} %get-tuple-element.17), kind=kOutput, calls=%fused_computation.58 | convolution fusion | flops 805306368 | bytes 4980736 | tf_op jit(solution)/shard_map/dot_general | solution.py:167
  217.3 2.1 select_bitcast_fusion.3
  221.0 2.1 copy.159
  223.1 6.2 %reshape.224 = bf16[768,4,512]{2,1,0:T(4,128)(2,1)} reshape(bf16[4,2,96,2048]{3,2,1,0:T(8,128)(2,1)} %copy.159) | data formatting | bytes 6291456 | tf_op jit(solution)/shard_map/reshape | solution.py:151
  229.3 10.8 %fusion.139 = (bf16[768,1,512]{2,1,0:T(2,128)(2,1)S(1)}, bf16[768,1,512]{2,1,0:T(2,128)(2,1)S(1)}, bf16[768,1,512]{2,1,0:T(2,128)(2,1)S(1)}, bf16[768,1,512]{2,1,0:T(2,128)(2,1)S(1)}) fusion(bf16[768,4,512]{2,1,0:T(4,128)(2,1)} %reshape.224), kind=kLoop, calls=%fused_computation.249 | loop fusion | bytes 6291456 | tf_op jit(solution)/shard_map/slice | solution.py:166
  240.1 3.8 %fusion.43 = f32[768,1024]{1,0:T(8,128)} fusion(bf16[4,2,512,1024]{3,2,1,0:T(8,128)(2,1)} %bitcast.265, bf16[768,1,512]{2,1,0:T(2,128)(2,1)S(1)} %get-tuple-element.19), kind=kOutput, calls=%fused_computation.75 | convolution fusion | flops 805306368 | bytes 4980736 | tf_op jit(solution)/shard_map/dot_general | solution.py:166
  243.9 3.9 %fusion.36 = f32[768,1024]{1,0:T(8,128)} fusion(bf16[4,2,512,1024]{3,2,1,0:T(8,128)(2,1)} %bitcast.273, bf16[768,1,512]{2,1,0:T(2,128)(2,1)S(1)} %get-tuple-element.19), kind=kOutput, calls=%fused_computation.60 | convolution fusion | flops 805306368 | bytes 4980736 | tf_op jit(solution)/shard_map/dot_general | solution.py:167
  247.8 3.9 %fusion.44 = f32[768,1024]{1,0:T(8,128)} fusion(bf16[4,2,512,1024]{3,2,1,0:T(8,128)(2,1)} %bitcast.266, bf16[768,1,512]{2,1,0:T(2,128)(2,1)S(1)} %get-tuple-element.20), kind=kOutput, calls=%fused_computation.77 | convolution fusion | flops 805306368 | bytes 4980736 | tf_op jit(solution)/shard_map/dot_general | solution.py:166
  251.7 3.8 %fusion.37 = f32[768,1024]{1,0:T(8,128)} fusion(bf16[4,2,512,1024]{3,2,1,0:T(8,128)(2,1)} %bitcast.274, bf16[768,1,512]{2,1,0:T(2,128)(2,1)S(1)} %get-tuple-element.20), kind=kOutput, calls=%fused_computation.62 | convolution fusion | flops 805306368 | bytes 4980736 | tf_op jit(solution)/shard_map/dot_general | solution.py:167
  255.5 4.0 %fusion.46 = f32[768,1024]{1,0:T(8,128)} fusion(bf16[4,2,512,1024]{3,2,1,0:T(8,128)(2,1)} %bitcast.267, bf16[768,1,512]{2,1,0:T(2,128)(2,1)S(1)} %get-tuple-element.21), kind=kOutput, calls=%fused_computation.81 | convolution fusion | flops 805306368 | bytes 4980736 | tf_op jit(solution)/shard_map/dot_general | solution.py:166
  259.5 3.8 %fusion.39 = f32[768,1024]{1,0:T(8,128)} fusion(bf16[4,2,512,1024]{3,2,1,0:T(8,128)(2,1)} %bitcast.275, bf16[768,1,512]{2,1,0:T(2,128)(2,1)S(1)} %get-tuple-element.21), kind=kOutput, calls=%fused_computation.66 | convolution fusion | flops 805306368 | bytes 4980736 | tf_op jit(solution)/shard_map/dot_general | solution.py:167
  263.3 3.9 %fusion.45 = f32[768,1024]{1,0:T(8,128)} fusion(bf16[4,2,512,1024]{3,2,1,0:T(8,128)(2,1)} %bitcast.268, bf16[768,1,512]{2,1,0:T(2,128)(2,1)S(1)} %get-tuple-element.18), kind=kOutput, calls=%fused_computation.79 | convolution fusion | flops 805306368 | bytes 4980736 | tf_op jit(solution)/shard_map/dot_general | solution.py:166
  267.1 3.9 %fusion.38 = f32[768,1024]{1,0:T(8,128)} fusion(bf16[4,2,512,1024]{3,2,1,0:T(8,128)(2,1)} %bitcast.276, bf16[768,1,512]{2,1,0:T(2,128)(2,1)S(1)} %get-tuple-element.18), kind=kOutput, calls=%fused_computation.64 | convolution fusion | flops 805306368 | bytes 4980736 | tf_op jit(solution)/shard_map/dot_general | solution.py:167
  271.1 6.2 %stack_reshape.7 = bf16[768,4,1,512]{3,1,0,2:T(4,128)(2,1)} reshape(bf16[4,2,96,2048]{3,2,1,0:T(8,128)(2,1)} %pad_maximum_fusion.2) | data formatting | bytes 6291456 | tf_op jit(solution)/shard_map/stack;reshape | solution.py:185
  277.3 6.1 %stack_reshape.6 = bf16[768,4,1,512]{3,1,0,2:T(4,128)(2,1)} reshape(bf16[4,2,96,2048]{3,2,1,0:T(8,128)(2,1)} %copy.159) | data formatting | bytes 6291456 | tf_op jit(solution)/shard_map/stack;reshape | solution.py:185
  283.4 2.5 multiply_reduce_fusion.1
  287.5 2.2 fusion.21
  289.7 2.0 fusion.30
  291.8 10.6 %add_multiply_fusion.1 = f32[768,1024]{1,0:T(8,128)} fusion(f32[768,1024]{1,0:T(8,128)S(1)} %copy-done.15, f32[768,1024]{1,0:T(8,128)} %fusion.41, f32[768,1024]{1,0:T(8,128)} %fusion.42, f32[768,1024]{1,0:T(8,128)} %fusion.43, f32[768,1024]{1,0:T(8,128)} %fusion.44, f32[768,1024]{1,0:T(8,128)} %fusion.46, f32[768,1024]{1,0:T(8,128)} %fusion.45, ...), kind=kOutput, calls=%fused_computation.22 | convolution fusion | flops 811597824 | bytes 27790336 | tf_op jit(solution)/shard_map/dot_general | solution.py:166
  305.5 7.8 %multiply_convert_fusion = (bf16[768,1024]{1,0:T(8,128)(2,1)S(1)}, f32[768,1024]{1,0:T(8,128)}) fusion(f32[768]{0:T(1024)S(1)} %get-tuple-element.9, f32[768,1024]{1,0:T(8,128)} %add_multiply_fusion.1, bf16[4,2,512,1024]{3,2,1,0:T(8,128)(2,1)} %bitcast.277, bf16[768,1,512]{2,1,0:T(2,128)(2,1)} %get-tuple-element.14, f32[768,1024]{1,0:T(8,128)S(1)} %copy-done.7, ...), kind=kOutput, calls=%fused_computation.18 | convolution fusion | flops 817102848 | bytes 32512000 | tf_op jit(solution)/shard_map/dot_general | solution.py:167
  315.6 9.3 %pad_maximum_fusion = bf16[768,4,2,512]{3,1,0,2:T(4,128)(2,1)} fusion(bf16[768,4,1,512]{3,1,0,2:T(4,128)(2,1)S(1)} %copy-done.13, bf16[768,4,1,512]{3,1,0,2:T(4,128)(2,1)} %stack_reshape.6), kind=kLoop, calls=%fused_computation.2 | loop fusion | flops 3145728 | bytes 12582912 | tf_op jit(solution)/shard_map/stack | solution.py:185
  324.9 10.7 %copy.171 = bf16[768,4,2,512]{0,3,2,1:T(8,128)(2,1)} copy(bf16[768,4,2,512]{3,1,0,2:T(4,128)(2,1)} %pad_maximum_fusion) | data formatting | bytes 12582912 | tf_op jit(solution)/shard_map/stack | solution.py:185
  335.7 12.6 %convert_bitcast_fusion = bf16[1,4096,1024]{2,1,0:T(8,128)(2,1)} fusion(bf16[768,4096]{0,1:T(8,128)(2,1)} %bitcast.279, bf16[768,1024]{1,0:T(8,128)(2,1)} %bitcast.284, f32[768]{0:T(1024)S(1)} %get-tuple-element.8, f32[768,1024]{1,0:T(8,128)S(1)} %copy-done.14), kind=kOutput, calls=%fused_computation | convolution fusion | flops 6452936704 | bytes 19401728 | tf_op jit(solution)/shard_map/dot_general | solution.py:188
  348.3 9.5 %convert_bitcast_fusion.1 = bf16[1,4096,1024]{2,1,0:T(8,128)(2,1)} fusion(bf16[768,4096]{0,1:T(8,128)(2,1)S(1)} %bitcast.280, f32[768,1024]{1,0:T(8,128)S(1)} %copy-done.17, bf16[768,1024]{1,0:T(8,128)(2,1)S(1)} %bitcast.285, f32[768,1024]{1,0:T(8,128)S(1)} %copy-done.14, f32[768]{0:T(1024)S(1)} %get-tuple-element.8), kind=kOutput, calls=%fused_computation.1 | convolution fusion | flops 6456082432 | bytes 22547456 | tf_op jit(solution)/shard_map/dot_general | solution.py:187
  (188 shorter events, 73.7 us)
Async XLA Ops:
  4.7 20.5 %collective-permute-start.8 = (bf16[144,1024]{0,1:T(8,128)(2,1)}, bf16[144,1024]{0,1:T(8,128)(2,1)}, u32[]{:S(2)}, u32[]{:S(2)}) collective-permute-start(bf16[144,1024]{0,1:T(8,128)(2,1)} %get-tuple-element.11), channel_id=1, source_target_pairs={{0,8},{8,0},{16,24},{24,16},{1,9},{9,1},{17,25},{25,17},{2,10},{10... | collective-permute-start | bytes 884744 | tf_op jit(solution)/shard_map/ppermute | solution.py:11
  7.7 26.3 %collective-permute-start.9 = (bf16[144,1024]{0,1:T(8,128)(2,1)}, bf16[144,1024]{0,1:T(8,128)(2,1)S(1)}, u32[]{:S(2)}, u32[]{:S(2)}) collective-permute-start(bf16[144,1024]{0,1:T(8,128)(2,1)} %get-tuple-element.11), channel_id=1, source_target_pairs={{0,16},{8,24},{16,0},{24,8},{1,17},{9,25},{17,1},{25,9},{2,18},{10... | collective-permute-start | bytes 884744 | tf_op jit(solution)/shard_map/ppermute | solution.py:11
  9.2 24.8 %collective-permute-start.10 = (bf16[144,1024]{0,1:T(8,128)(2,1)}, bf16[144,1024]{0,1:T(8,128)(2,1)S(1)}, u32[]{:S(2)}, u32[]{:S(2)}) collective-permute-start(bf16[144,1024]{0,1:T(8,128)(2,1)} %get-tuple-element.11), channel_id=1, source_target_pairs={{0,24},{8,16},{16,8},{24,0},{1,25},{9,17},{17,9},{25,1},{2,26},{10... | collective-permute-start | bytes 884744 | tf_op jit(solution)/shard_map/ppermute | solution.py:11
  13.9 5.0 %copy-start.23 = (bf16[1024]{0:T(1024)(128)(2,1)S(1)}, bf16[1024]{0:T(1024)(128)(2,1)}, u32[]{:S(2)}) copy-start(bf16[1024]{0:T(1024)(128)(2,1)} %param.13) | copy-start | bytes 6148
  13.9 5.0 %copy-start.24 = (s32[128,2]{0,1:T(2,128)S(1)}, s32[128,2]{0,1:T(2,128)}, u32[]{:S(2)}) copy-start(s32[128,2]{0,1:T(2,128)} %param.18) | copy-start | bytes 3076
  13.9 5.1 %copy-start.25 = (s32[128,2]{0,1:T(2,128)S(1)}, s32[128,2]{0,1:T(2,128)}, u32[]{:S(2)}) copy-start(s32[128,2]{0,1:T(2,128)} %param.17) | copy-start | bytes 3076
  16.1 29.7 %collective-permute-start.2 = (bf16[2,256,512]{2,1,0:T(8,128)(2,1)}, bf16[2,256,512]{2,1,0:T(8,128)(2,1)}, u32[]{:S(2)}, u32[]{:S(2)}) collective-permute-start(bf16[2,256,512]{2,1,0:T(8,128)(2,1)} %pad_maximum_fusion.8), channel_id=1, source_target_pairs={{0,16},{8,24},{16,0},{24,8},{1,17},{9,25},{17,1},{25,9},{2,18},{10... | collective-permute-start | bytes 1572872 | tf_op jit(solution)/shard_map/ppermute | solution.py:11
  18.9 37.6 %collective-permute-start.6 = (bf16[2,256,512]{2,1,0:T(8,128)(2,1)}, bf16[2,256,512]{2,1,0:T(8,128)(2,1)}, u32[]{:S(2)}, u32[]{:S(2)}) collective-permute-start(bf16[2,256,512]{2,1,0:T(8,128)(2,1)} %pad_maximum_fusion.10), channel_id=1, source_target_pairs={{0,16},{8,24},{16,0},{24,8},{1,17},{9,25},{17,1},{25,9},{2,18},{10... | collective-permute-start | bytes 1572872 | tf_op jit(solution)/shard_map/ppermute | solution.py:11
  25.2 23.6 %collective-permute-start = (bf16[2,256,512]{2,1,0:T(8,128)(2,1)}, bf16[2,256,512]{2,1,0:T(8,128)(2,1)}, u32[]{:S(2)}, u32[]{:S(2)}) collective-permute-start(bf16[2,256,512]{2,1,0:T(8,128)(2,1)} %pad_maximum_fusion.7), channel_id=1, source_target_pairs={{0,8},{8,0},{16,24},{24,16},{1,9},{9,1},{17,25},{25,17},{2,10},{10... | collective-permute-start | bytes 1572872 | tf_op jit(solution)/shard_map/ppermute | solution.py:11
  34.0 28.4 %collective-permute-start.4 = (bf16[2,256,512]{2,1,0:T(8,128)(2,1)}, bf16[2,256,512]{2,1,0:T(8,128)(2,1)}, u32[]{:S(2)}, u32[]{:S(2)}) collective-permute-start(bf16[2,256,512]{2,1,0:T(8,128)(2,1)} %pad_maximum_fusion.9), channel_id=1, source_target_pairs={{0,8},{8,0},{16,24},{24,16},{1,9},{9,1},{17,25},{25,17},{2,10},{10... | collective-permute-start | bytes 1572872 | tf_op jit(solution)/shard_map/ppermute | solution.py:11
  40.5 34.6 %all-to-all-start = ((bf16[8,144,512]{2,1,0:T(8,128)(2,1)}), bf16[8,144,512]{2,1,0:T(8,128)(2,1)S(1)}, u32[]{:S(2)}, u32[]{:S(2)}) async-start(bf16[8,144,512]{2,1,0:T(8,128)(2,1)} %pad.9.clone), calls=%async_computation | async-start | bytes 2359296 | tf_op jit(solution)/shard_map/all_to_all | solution.py:87
  46.8 12.3 %collective-permute-start.3 = (bf16[1,256,512]{2,1,0:T(8,128)(2,1)S(1)}, bf16[1,256,512]{2,1,0:T(8,128)(2,1)S(1)}, u32[]{:S(2)}, u32[]{:S(2)}) collective-permute-start(bf16[1,256,512]{2,1,0:T(8,128)(2,1)S(1)} %add_convert_fusion.2), channel_id=1, source_target_pairs={{0,8},{8,0},{16,24},{24,16},{1,9},{9,1},{17,25},{25,17},{2,10},{10... | collective-permute-start | bytes 786440 | tf_op jit(solution)/shard_map/ppermute | solution.py:11
  49.9 12.4 %collective-permute-start.1 = (bf16[1,256,512]{2,1,0:T(8,128)(2,1)S(1)}, bf16[1,256,512]{2,1,0:T(8,128)(2,1)S(1)}, u32[]{:S(2)}, u32[]{:S(2)}) collective-permute-start(bf16[1,256,512]{2,1,0:T(8,128)(2,1)S(1)} %add_convert_fusion.3), channel_id=1, source_target_pairs={{0,16},{8,24},{16,0},{24,8},{1,17},{9,25},{17,1},{25,9},{2,18},{10... | collective-permute-start | bytes 786440 | tf_op jit(solution)/shard_map/ppermute | solution.py:11
  60.5 7.6 %collective-permute-start.7 = (bf16[1,256,512]{2,1,0:T(8,128)(2,1)S(1)}, bf16[1,256,512]{2,1,0:T(8,128)(2,1)S(1)}, u32[]{:S(2)}, u32[]{:S(2)}) collective-permute-start(bf16[1,256,512]{2,1,0:T(8,128)(2,1)S(1)} %get-tuple-element.33), channel_id=1, source_target_pairs={{0,8},{8,0},{16,24},{24,16},{1,9},{9,1},{17,25},{25,17},{2,10},{10... | collective-permute-start | bytes 786440 | tf_op jit(solution)/shard_map/ppermute | solution.py:11
  63.7 7.0 %collective-permute-start.5 = (bf16[1,256,512]{2,1,0:T(8,128)(2,1)S(1)}, bf16[1,256,512]{2,1,0:T(8,128)(2,1)S(1)}, u32[]{:S(2)}, u32[]{:S(2)}) collective-permute-start(bf16[1,256,512]{2,1,0:T(8,128)(2,1)S(1)} %get-tuple-element.27), channel_id=1, source_target_pairs={{0,16},{8,24},{16,0},{24,8},{1,17},{9,25},{17,1},{25,9},{2,18},{10... | collective-permute-start | bytes 786440 | tf_op jit(solution)/shard_map/ppermute | solution.py:11
  79.7 2.2 collective-permute-start.11
  79.8 7.1 %collective-permute-start.22 = (bf16[4,128,512]{2,1,0:T(8,128)(2,1)}, bf16[4,128,512]{2,1,0:T(8,128)(2,1)S(1)}, u32[]{:S(2)}, u32[]{:S(2)}) collective-permute-start(bf16[4,128,512]{2,1,0:T(8,128)(2,1)} %convolution_convert_fusion), channel_id=1, source_target_pairs={{0,1},{1,0},{2,3},{3,2},{4,5},{5,4},{6,7},{7,6},{8,9},{9,8},{10,11... | collective-permute-start | bytes 1572872 | tf_op jit(solution)/shard_map/ppermute | solution.py:11
  82.4 24.4 %copy-start.22 = (bf16[128,1024]{1,0:T(8,128)(2,1)S(1)}, bf16[128,1024]{1,0:T(8,128)(2,1)}, u32[]{:S(2)}) copy-start(bf16[128,1024]{1,0:T(8,128)(2,1)} %param.12) | copy-start | bytes 786436
  82.4 8.3 %collective-permute-start.14 = (bf16[128,512]{1,0:T(8,128)(2,1)S(1)}, bf16[128,512]{1,0:T(8,128)(2,1)S(1)}, u32[]{:S(2)}, u32[]{:S(2)}) collective-permute-start(bf16[128,512]{1,0:T(8,128)(2,1)S(1)} %get-tuple-element.47), channel_id=1, source_target_pairs={{0,6},{1,7},{2,4},{3,5},{4,2},{5,3},{6,0},{7,1},{8,14},{9,15},{10,... | collective-permute-start | bytes 393224 | tf_op jit(solution)/shard_map/ppermute | solution.py:11
  84.0 12.4 %collective-permute-start.13 = (bf16[128,512]{1,0:T(8,128)(2,1)S(1)}, bf16[128,512]{1,0:T(8,128)(2,1)S(1)}, u32[]{:S(2)}, u32[]{:S(2)}) collective-permute-start(bf16[128,512]{1,0:T(8,128)(2,1)S(1)} %get-tuple-element.48), channel_id=1, source_target_pairs={{0,4},{1,5},{2,6},{3,7},{4,0},{5,1},{6,2},{7,3},{8,12},{9,13},{10,... | collective-permute-start | bytes 393224 | tf_op jit(solution)/shard_map/ppermute | solution.py:11
  84.0 12.4 %collective-permute-start.12 = (bf16[128,512]{1,0:T(8,128)(2,1)S(1)}, bf16[128,512]{1,0:T(8,128)(2,1)S(1)}, u32[]{:S(2)}, u32[]{:S(2)}) collective-permute-start(bf16[128,512]{1,0:T(8,128)(2,1)S(1)} %get-tuple-element.46), channel_id=1, source_target_pairs={{0,2},{1,3},{2,0},{3,1},{4,6},{5,7},{6,4},{7,5},{8,10},{9,11},{10,... | collective-permute-start | bytes 393224 | tf_op jit(solution)/shard_map/ppermute | solution.py:11
  87.4 11.9 %collective-permute-start.25 = (bf16[128,512]{1,0:T(8,128)(2,1)S(1)}, bf16[128,512]{1,0:T(8,128)(2,1)S(1)}, u32[]{:S(2)}, u32[]{:S(2)}) collective-permute-start(bf16[128,512]{1,0:T(8,128)(2,1)S(1)} %get-tuple-element.50), channel_id=1, source_target_pairs={{0,6},{1,7},{2,4},{3,5},{4,2},{5,3},{6,0},{7,1},{8,14},{9,15},{10,... | collective-permute-start | bytes 393224 | tf_op jit(solution)/shard_map/ppermute | solution.py:11
  89.0 17.8 %collective-permute-start.24 = (bf16[128,512]{1,0:T(8,128)(2,1)S(1)}, bf16[128,512]{1,0:T(8,128)(2,1)S(1)}, u32[]{:S(2)}, u32[]{:S(2)}) collective-permute-start(bf16[128,512]{1,0:T(8,128)(2,1)S(1)} %get-tuple-element.51), channel_id=1, source_target_pairs={{0,4},{1,5},{2,6},{3,7},{4,0},{5,1},{6,2},{7,3},{8,12},{9,13},{10,... | collective-permute-start | bytes 393224 | tf_op jit(solution)/shard_map/ppermute | solution.py:11
  90.8 16.0 %collective-permute-start.23 = (bf16[128,512]{1,0:T(8,128)(2,1)S(1)}, bf16[128,512]{1,0:T(8,128)(2,1)S(1)}, u32[]{:S(2)}, u32[]{:S(2)}) collective-permute-start(bf16[128,512]{1,0:T(8,128)(2,1)S(1)} %get-tuple-element.49), channel_id=1, source_target_pairs={{0,2},{1,3},{2,0},{3,1},{4,6},{5,7},{6,4},{7,5},{8,10},{9,11},{10,... | collective-permute-start | bytes 393224 | tf_op jit(solution)/shard_map/ppermute | solution.py:11
  107.0 8.3 %collective-permute-start.28 = (bf16[128,512]{1,0:T(8,128)(2,1)S(1)}, bf16[128,512]{1,0:T(8,128)(2,1)S(1)}, u32[]{:S(2)}, u32[]{:S(2)}) collective-permute-start(bf16[128,512]{1,0:T(8,128)(2,1)S(1)} %get-tuple-element.57), channel_id=1, source_target_pairs={{0,6},{1,7},{2,4},{3,5},{4,2},{5,3},{6,0},{7,1},{8,14},{9,15},{10,... | collective-permute-start | bytes 393224 | tf_op jit(solution)/shard_map/ppermute | solution.py:11
  109.4 10.5 %collective-permute-start.27 = (bf16[128,512]{1,0:T(8,128)(2,1)S(1)}, bf16[128,512]{1,0:T(8,128)(2,1)S(1)}, u32[]{:S(2)}, u32[]{:S(2)}) collective-permute-start(bf16[128,512]{1,0:T(8,128)(2,1)S(1)} %get-tuple-element.57), channel_id=1, source_target_pairs={{0,4},{1,5},{2,6},{3,7},{4,0},{5,1},{6,2},{7,3},{8,12},{9,13},{10,... | collective-permute-start | bytes 393224 | tf_op jit(solution)/shard_map/ppermute | solution.py:11
  109.4 10.5 %collective-permute-start.26 = (bf16[128,512]{1,0:T(8,128)(2,1)S(1)}, bf16[128,512]{1,0:T(8,128)(2,1)S(1)}, u32[]{:S(2)}, u32[]{:S(2)}) collective-permute-start(bf16[128,512]{1,0:T(8,128)(2,1)S(1)} %get-tuple-element.57), channel_id=1, source_target_pairs={{0,2},{1,3},{2,0},{3,1},{4,6},{5,7},{6,4},{7,5},{8,10},{9,11},{10,... | collective-permute-start | bytes 393224 | tf_op jit(solution)/shard_map/ppermute | solution.py:11
  120.2 12.0 %collective-permute-start.29 = (bf16[4,96,512]{2,1,0:T(8,128)(2,1)S(1)}, bf16[4,96,512]{2,1,0:T(8,128)(2,1)S(1)}, u32[]{:S(2)}, u32[]{:S(2)}) collective-permute-start(bf16[4,96,512]{2,1,0:T(8,128)(2,1)S(1)} %convolution_convert_fusion.4), channel_id=1, source_target_pairs={{0,8},{8,0},{16,24},{24,16},{1,9},{9,1},{17,25},{25,17},{2,10},{10... | collective-permute-start | bytes 1179656 | tf_op jit(solution)/shard_map/ppermute | solution.py:11
  122.4 19.2 %collective-permute-start.30 = (bf16[4,96,512]{2,1,0:T(8,128)(2,1)S(1)}, bf16[4,96,512]{2,1,0:T(8,128)(2,1)S(1)}, u32[]{:S(2)}, u32[]{:S(2)}) collective-permute-start(bf16[4,96,512]{2,1,0:T(8,128)(2,1)S(1)} %convolution_convert_fusion.3), channel_id=1, source_target_pairs={{0,16},{8,24},{16,0},{24,8},{1,17},{9,25},{17,1},{25,9},{2,18},{10... | collective-permute-start | bytes 1179656 | tf_op jit(solution)/shard_map/ppermute | solution.py:11
  124.3 17.4 %collective-permute-start.31 = (bf16[4,96,512]{2,1,0:T(8,128)(2,1)S(1)}, bf16[4,96,512]{2,1,0:T(8,128)(2,1)S(1)}, u32[]{:S(2)}, u32[]{:S(2)}) collective-permute-start(bf16[4,96,512]{2,1,0:T(8,128)(2,1)S(1)} %convolution_convert_fusion.2), channel_id=1, source_target_pairs={{0,24},{8,16},{16,8},{24,0},{1,25},{9,17},{17,9},{25,1},{2,26},{10... | collective-permute-start | bytes 1179656 | tf_op jit(solution)/shard_map/ppermute | solution.py:11
  141.8 38.0 %collective-permute-start.32 = (bf16[4,96,2048]{2,1,0:T(8,128)(2,1)S(1)}, bf16[4,96,2048]{2,1,0:T(8,128)(2,1)S(1)}, u32[]{:S(2)}, u32[]{:S(2)}) collective-permute-start(bf16[4,96,2048]{2,1,0:T(8,128)(2,1)S(1)} %constant_dynamic-update-slice_fusion), channel_id=1, source_target_pairs={{0,1},{1,0},{2,3},{3,2},{4,5},{5,4},{6,7},{7,6},{8,9},{9,8},{10,11... | collective-permute-start | bytes 4718600 | tf_op jit(solution)/shard_map/ppermute | solution.py:11
  141.9 8.4 %collective-permute-start.17 = (bf16[128,512]{1,0:T(8,128)(2,1)S(1)}, bf16[128,512]{1,0:T(8,128)(2,1)}, u32[]{:S(2)}, u32[]{:S(2)}) collective-permute-start(bf16[128,512]{1,0:T(8,128)(2,1)S(1)} %get-tuple-element.56), channel_id=1, source_target_pairs={{0,6},{1,7},{2,4},{3,5},{4,2},{5,3},{6,0},{7,1},{8,14},{9,15},{10,... | collective-permute-start | bytes 393224 | tf_op jit(solution)/shard_map/ppermute | solution.py:11
  143.4 12.0 %collective-permute-start.16 = (bf16[128,512]{1,0:T(8,128)(2,1)S(1)}, bf16[128,512]{1,0:T(8,128)(2,1)}, u32[]{:S(2)}, u32[]{:S(2)}) collective-permute-start(bf16[128,512]{1,0:T(8,128)(2,1)S(1)} %get-tuple-element.56), channel_id=1, source_target_pairs={{0,4},{1,5},{2,6},{3,7},{4,0},{5,1},{6,2},{7,3},{8,12},{9,13},{10,... | collective-permute-start | bytes 393224 | tf_op jit(solution)/shard_map/ppermute | solution.py:11
  143.4 12.0 %collective-permute-start.15 = (bf16[128,512]{1,0:T(8,128)(2,1)S(1)}, bf16[128,512]{1,0:T(8,128)(2,1)}, u32[]{:S(2)}, u32[]{:S(2)}) collective-permute-start(bf16[128,512]{1,0:T(8,128)(2,1)S(1)} %get-tuple-element.56), channel_id=1, source_target_pairs={{0,2},{1,3},{2,0},{3,1},{4,6},{5,7},{6,4},{7,5},{8,10},{9,11},{10,... | collective-permute-start | bytes 393224 | tf_op jit(solution)/shard_map/ppermute | solution.py:11
  156.7 12.0 %collective-permute-start.18 = (bf16[4,96,512]{2,1,0:T(8,128)(2,1)S(1)}, bf16[4,96,512]{2,1,0:T(8,128)(2,1)S(1)}, u32[]{:S(2)}, u32[]{:S(2)}) collective-permute-start(bf16[4,96,512]{2,1,0:T(8,128)(2,1)S(1)} %convolution_convert_fusion.8), channel_id=1, source_target_pairs={{0,8},{8,0},{16,24},{24,16},{1,9},{9,1},{17,25},{25,17},{2,10},{10... | collective-permute-start | bytes 1179656 | tf_op jit(solution)/shard_map/ppermute | solution.py:11
  158.9 19.3 %collective-permute-start.19 = (bf16[4,96,512]{2,1,0:T(8,128)(2,1)S(1)}, bf16[4,96,512]{2,1,0:T(8,128)(2,1)S(1)}, u32[]{:S(2)}, u32[]{:S(2)}) collective-permute-start(bf16[4,96,512]{2,1,0:T(8,128)(2,1)S(1)} %convolution_convert_fusion.7), channel_id=1, source_target_pairs={{0,16},{8,24},{16,0},{24,8},{1,17},{9,25},{17,1},{25,9},{2,18},{10... | collective-permute-start | bytes 1179656 | tf_op jit(solution)/shard_map/ppermute | solution.py:11
  161.5 17.5 %collective-permute-start.20 = (bf16[4,96,512]{2,1,0:T(8,128)(2,1)S(1)}, bf16[4,96,512]{2,1,0:T(8,128)(2,1)S(1)}, u32[]{:S(2)}, u32[]{:S(2)}) collective-permute-start(bf16[4,96,512]{2,1,0:T(8,128)(2,1)S(1)} %convolution_convert_fusion.6), channel_id=1, source_target_pairs={{0,24},{8,16},{16,8},{24,0},{1,25},{9,17},{17,9},{25,1},{2,26},{10... | collective-permute-start | bytes 1179656 | tf_op jit(solution)/shard_map/ppermute | solution.py:11
  179.7 37.5 %collective-permute-start.21 = (bf16[4,96,2048]{2,1,0:T(8,128)(2,1)}, bf16[4,96,2048]{2,1,0:T(8,128)(2,1)}, u32[]{:S(2)}, u32[]{:S(2)}) collective-permute-start(bf16[4,96,2048]{2,1,0:T(8,128)(2,1)} %constant_dynamic-update-slice_fusion.3), channel_id=1, source_target_pairs={{0,1},{1,0},{2,3},{3,2},{4,5},{5,4},{6,7},{7,6},{8,9},{9,8},{10,11... | collective-permute-start | bytes 4718600 | tf_op jit(solution)/shard_map/ppermute | solution.py:11
  180.0 1.2 copy-start.1
  180.0 1.7 copy-start.3
  219.4 1.1 copy-start.5
  219.4 1.7 copy-start.6
  283.4 2.5 copy-start.2
  283.4 2.8 copy-start.4
  287.5 2.2 copy-start
  287.5 4.2 %copy-start.15 = (f32[768,1024]{1,0:T(8,128)S(1)}, f32[768,1024]{1,0:T(8,128)}, u32[]{:S(2)}) copy-start(f32[768,1024]{1,0:T(8,128)} %fusion.40) | copy-start | bytes 9437188
  291.7 10.6 %copy-start.7 = (f32[768,1024]{1,0:T(8,128)S(1)}, f32[768,1024]{1,0:T(8,128)}, u32[]{:S(2)}) copy-start(f32[768,1024]{1,0:T(8,128)} %fusion.33) | copy-start | bytes 9437188
  291.8 10.6 %copy-start.8 = (f32[768,1024]{1,0:T(8,128)S(1)}, f32[768,1024]{1,0:T(8,128)}, u32[]{:S(2)}) copy-start(f32[768,1024]{1,0:T(8,128)} %fusion.34) | copy-start | bytes 9437188
  291.8 10.6 %copy-start.9 = (f32[768,1024]{1,0:T(8,128)S(1)}, f32[768,1024]{1,0:T(8,128)}, u32[]{:S(2)}) copy-start(f32[768,1024]{1,0:T(8,128)} %fusion.35) | copy-start | bytes 9437188
  291.8 11.9 %copy-start.10 = (f32[768,1024]{1,0:T(8,128)S(1)}, f32[768,1024]{1,0:T(8,128)}, u32[]{:S(2)}) copy-start(f32[768,1024]{1,0:T(8,128)} %fusion.36) | copy-start | bytes 9437188
  291.8 12.8 %copy-start.11 = (f32[768,1024]{1,0:T(8,128)S(1)}, f32[768,1024]{1,0:T(8,128)}, u32[]{:S(2)}) copy-start(f32[768,1024]{1,0:T(8,128)} %fusion.37) | copy-start | bytes 9437188
  291.8 13.7 %copy-start.12 = (f32[768,1024]{1,0:T(8,128)S(1)}, f32[768,1024]{1,0:T(8,128)}, u32[]{:S(2)}) copy-start(f32[768,1024]{1,0:T(8,128)} %fusion.39) | copy-start | bytes 9437188
  313.3 2.3 copy-start.13
  324.9 10.7 %copy-start.14 = (f32[768,1024]{1,0:T(8,128)S(1)}, f32[768,1024]{1,0:T(8,128)}, u32[]{:S(2)}) copy-start(f32[768,1024]{1,0:T(8,128)} %add_multiply_fusion.1) | copy-start | bytes 9437188
  335.6 12.7 %copy-start.16 = (bf16[768,4,2,512]{0,3,2,1:T(8,128)(2,1)S(1)}, bf16[768,4,2,512]{0,3,2,1:T(8,128)(2,1)}, u32[]{:S(2)}) copy-start(bf16[768,4,2,512]{0,3,2,1:T(8,128)(2,1)} %copy.171) | copy-start | bytes 18874372
  335.6 12.7 %copy-start.17 = (f32[768,1024]{1,0:T(8,128)S(1)}, f32[768,1024]{1,0:T(8,128)}, u32[]{:S(2)}) copy-start(f32[768,1024]{1,0:T(8,128)} %get-tuple-element.69) | copy-start | bytes 9437188
  335.6 12.7 %copy-start.18 = (bf16[4,192,1024]{2,1,0:T(8,128)(2,1)S(1)}, bf16[4,192,1024]{2,1,0:T(8,128)(2,1)}, u32[]{:S(2)}) copy-start(bf16[4,192,1024]{2,1,0:T(8,128)(2,1)} %pad_maximum_fusion.5) | copy-start | bytes 4718596
  348.3 9.6 %copy-start.19 = (bf16[1,192,1024]{2,1,0:T(8,128)(2,1)S(1)}, bf16[1,192,1024]{2,1,0:T(8,128)(2,1)}, u32[]{:S(2)}) copy-start(bf16[1,192,1024]{2,1,0:T(8,128)(2,1)} %get-tuple-element.43) | copy-start | bytes 1179652
  348.3 9.6 %copy-start.20 = (bf16[1,192,1024]{2,1,0:T(8,128)(2,1)S(1)}, bf16[1,192,1024]{2,1,0:T(8,128)(2,1)}, u32[]{:S(2)}) copy-start(bf16[1,192,1024]{2,1,0:T(8,128)(2,1)} %get-tuple-element.44) | copy-start | bytes 1179652
  348.3 9.6 %copy-start.21 = (bf16[1,192,1024]{2,1,0:T(8,128)(2,1)S(1)}, bf16[1,192,1024]{2,1,0:T(8,128)(2,1)}, u32[]{:S(2)}) copy-start(bf16[1,192,1024]{2,1,0:T(8,128)(2,1)} %get-tuple-element.45) | copy-start | bytes 1179652

commit v2 on v0

v2 whole, which is shorter than its diff:
```python
import functools

import jax
import jax.numpy as jnp
from jax import lax
from jax.experimental import pallas as pl
from jax.experimental.pallas import tpu as pltpu
from jax.sharding import PartitionSpec as P

CHUNKS = 2
VMEM_LIMIT = 50 * 1024 * 1024


def exchange(value, axis, offset):
    size = lax.axis_size(axis)
    return lax.ppermute(value, axis, [(i, i ^ offset) for i in range(size)])


def pick(value, index, axis):
    return lax.dynamic_index_in_dim(value, index, axis, keepdims=False)


def bits_of(size):
    return size.bit_length() - 1


def whole(shape):
    return pl.BlockSpec(shape, lambda *_: (0,) * len(shape))


def smem():
    return pl.BlockSpec(memory_space=pltpu.SMEM)


def params():
    return pltpu.CompilerParams(vmem_limit_bytes=VMEM_LIMIT)


def signs_kernel(experts, position_ref, ids_ref, out_ref):
    blocks, capacity, lanes = out_ref.shape
    tokens = ids_ref.shape[2]
    expert = position_ref[0]
    slots = lax.broadcasted_iota(jnp.int32, (capacity, tokens), 0)
    rows = lax.broadcasted_iota(jnp.int32, (lanes, tokens), 0)
    last = lax.broadcasted_iota(jnp.int32, (capacity, lanes), 1) == lanes - 1
    for b in range(blocks):
        ids = ids_ref[b]
        e0, e1, s0, s1 = ids[0:1], ids[1:2], ids[2:3], ids[3:4]
        hit0 = jnp.where((e0 == expert) & (s0 == slots), 1.0, 0.0)
        hit1 = jnp.where((e1 == expert) & (s1 == slots), 1.0, 0.0)
        table = jnp.where(e0 == rows - 1, 1.0, 0.0) - jnp.where(e1 == rows - 1, 1.0, 0.0)
        signs = lax.dot_general(
            (hit0 - hit1).astype(jnp.bfloat16),
            table.astype(jnp.bfloat16),
            (((1,), (1,)), ((), ())),
            preferred_element_type=jnp.float32,
        )
        filled = jnp.sum(hit0 + hit1, axis=1, keepdims=True)
        out_ref[b] = jnp.where(last, filled, signs)


def dispatch_kernel(position_ref, ids_ref, *refs):
    *token_refs, out_ref = refs
    experts, planes, capacity, part = out_ref.shape
    tokens = ids_ref.shape[2]
    plane, core = position_ref[1], position_ref[2]
    slots = lax.broadcasted_iota(jnp.int32, (experts * capacity, tokens), 0)
    for k in range(planes):
        source = plane ^ k
        ids = ids_ref[source * 2 + core]
        code0 = ids[0:1] * capacity + ids[2:3]
        code1 = ids[1:2] * capacity + ids[3:4]
        one_hot = jnp.where((code0 == slots) | (code1 == slots), 1.0, 0.0).astype(jnp.bfloat16)
        picked = jnp.dot(one_hot, token_refs[k][...], preferred_element_type=jnp.float32)
        out_ref[:, source] = picked.reshape(experts, capacity, part).astype(jnp.bfloat16)


def row_stats(rows, aux):
    experts, count, part = rows.shape
    squares = jnp.zeros((count, part), jnp.float32)
    logits = jnp.zeros((count, aux.shape[1]), jnp.float32)
    for e in range(experts):
        ratio = rows[e].astype(jnp.float32) / aux[e, 0:1].astype(jnp.float32)
        squares = squares + ratio * ratio
        logits = logits + lax.dot_general(
            rows[e], aux[e], (((1,), (1,)), ((), ())), preferred_element_type=jnp.float32
        )
    total = jnp.sum(squares, axis=1, keepdims=True)
    return jnp.where(lax.broadcasted_iota(jnp.int32, logits.shape, 1) == 0, total, logits)


def products(rows_ref, weight_ref):
    total = None
    for e in range(rows_ref.shape[0]):
        term = jnp.dot(rows_ref[e], weight_ref[e, 0], preferred_element_type=jnp.float32)
        total = term if total is None else total + term
    return total


def early_kernel(own_ref, other_ref, aux_ref, gate_ref, up_ref, gate_out, up_out, stats_out):
    for side, rows_ref in enumerate((own_ref, other_ref)):
        gate_out[side] = products(rows_ref, gate_ref)
        up_out[side] = products(rows_ref, up_ref)

    @pl.when(pl.program_id(0) == 0)
    def _():
        for side, rows_ref in enumerate((own_ref, other_ref)):
            stats_out[side] = row_stats(rows_ref[...], aux_ref[...])


def late_kernel(
    width,
    tiles,
    position_ref,
    own0_ref,
    other0_ref,
    own1_ref,
    other1_ref,
    aux_ref,
    gate_ref,
    up_ref,
    gate_acc,
    up_acc,
    stats_ref,
    signs_ref,
    cot_ref,
    hidden_out,
    grad_gate_out,
    grad_up_out,
    scale_scratch,
    weight_scratch,
    d_gate_scratch,
    d_up_scratch,
    turned_scratch,
):
    step = pl.program_id(0)
    core = position_ref[2]
    planes, _, capacity, tile = hidden_out.shape
    count = planes * capacity
    experts = own0_ref.shape[0]
    lanes = stats_ref.shape[2]

    @pl.when(step == 0)
    def _():
        for side, rows_ref in enumerate((own1_ref, other1_ref)):
            stats = stats_ref[side] + row_stats(rows_ref[...], aux_ref[...])
            inverse = lax.rsqrt(stats[:, 0:1] / width + 1e-05)
            signs = signs_ref[:, pl.ds(core ^ side, 1)].reshape(count, lanes)
            filled = signs[:, lanes - 1 :]
            column = lax.broadcasted_iota(jnp.int32, stats.shape, 1)
            router = (column >= 1) & (column <= experts)
            margin = jnp.sum(jnp.where(router, stats * signs, 0.0), axis=1, keepdims=True)
            prob = jax.nn.sigmoid(margin * inverse).astype(jnp.bfloat16).astype(jnp.float32)
            scale_scratch[side] = inverse
            weight_scratch[side] = jnp.where(filled > 0.0, prob, 0.0)

    @pl.when(step < tiles)
    def _():
        start = pl.multiple_of(step * tile, tile)
        for side, rows_ref in enumerate((own1_ref, other1_ref)):
            inverse = scale_scratch[side]
            weight = weight_scratch[side]
            gate_pre = inverse * (gate_acc[side] + products(rows_ref, gate_ref))
            up_pre = inverse * (up_acc[side] + products(rows_ref, up_ref))
            sig_gate = jax.nn.sigmoid(gate_pre)
            act_gate = gate_pre * sig_gate
            hidden = (weight * act_gate * up_pre).astype(jnp.bfloat16)
            hidden_out[:, pl.ds(core ^ side, 1)] = hidden.reshape(planes, 1, capacity, tile)
            cot = cot_ref[:, pl.ds(core ^ side, 1)].reshape(count, tile)
            d_pre = cot.astype(jnp.float32) * (weight * inverse)
            d_gate = d_pre * up_pre * sig_gate * (1.0 + gate_pre * (1.0 - sig_gate))
            rows = pl.ds(side * count, count)
            d_gate_scratch[rows, pl.ds(start, tile)] = d_gate.astype(jnp.bfloat16)
            d_up_scratch[rows, pl.ds(start, tile)] = (d_pre * act_gate).astype(jnp.bfloat16)

    @pl.when(step >= tiles)
    def _():
        e = (step - tiles) // 2
        for c, sides in enumerate(((own0_ref, other0_ref), (own1_ref, other1_ref))):

            @pl.when((step - tiles) % 2 == c)
            def _():
                for side, rows_ref in enumerate(sides):
                    turned_scratch[:, side * count : (side + 1) * count] = rows_ref[e].T

        for t in range(tiles):
            span = slice(t * tile, (t + 1) * tile)
            for scratch, out in ((d_gate_scratch, grad_gate_out), (d_up_scratch, grad_up_out)):
                out[0, 0, :, span] = jnp.dot(
                    turned_scratch[...], scratch[:, span], preferred_element_type=jnp.float32
                ).astype(jnp.bfloat16)


def per_device(
    branch_wo,
    context,
    residual,
    norm_gain,
    router_w,
    gate_w,
    up_w,
    expert_ids,
    slot_ids,
    cot_hidden,
):
    experts = lax.axis_size("expert")
    blocks = lax.axis_size("fsdp")
    planes = blocks // 2
    expert = lax.axis_index("expert")
    block = lax.axis_index("fsdp")
    plane, core = block // 2, block % 2
    tokens, columns = context.shape
    width = columns * experts
    features = width // blocks
    capacity = cot_hidden.shape[1] // blocks
    units = cot_hidden.shape[2]
    part = columns // CHUNKS
    quarter = tokens // experts
    count = planes * capacity
    position = jnp.stack([expert, plane, core]).astype(jnp.int32)
    bits = bits_of(experts)

    extra = jnp.concatenate([norm_gain[None], router_w.T])
    lanes = experts + 2 + (-(experts + 2)) % 16
    extra = jnp.pad(extra, ((0, lanes - extra.shape[0]), (0, 0)))
    to_experts = jnp.concatenate(
        [
            context.reshape(experts, quarter, columns),
            jnp.broadcast_to(extra, (experts, lanes, columns)),
        ],
        axis=1,
    )
    shares = lax.all_to_all(to_experts, "expert", split_axis=0, concat_axis=0, tiled=True)
    aux = shares[:, quarter:]
    per_expert = blocks // experts
    spread = shares[:, :quarter].reshape(experts, quarter, per_expert, features)
    spread = spread.transpose(0, 2, 1, 3).reshape(blocks, quarter, features)
    ids = jnp.concatenate([expert_ids, slot_ids], axis=1).T.astype(jnp.bfloat16)
    id_rows = ids.size // features
    ids = jnp.pad(ids.reshape(id_rows, features), ((0, -id_rows % 16), (0, 0)))
    to_blocks = jnp.concatenate(
        [spread, jnp.broadcast_to(ids, (blocks,) + ids.shape)], axis=1
    )
    from_blocks = lax.all_to_all(to_blocks, "fsdp", split_axis=0, concat_axis=0, tiled=True)
    ids_all = from_blocks[:, quarter : quarter + id_rows].astype(jnp.int32)
    ids_all = ids_all.reshape(blocks, 4, tokens)
    share = from_blocks[:, :quarter]
    context_rows = jnp.zeros((blocks, experts, quarter, features), jnp.bfloat16)
    for k in range(experts):
        piece = exchange(share, "expert", k) if k else share
        context_rows = lax.dynamic_update_slice_in_dim(
            context_rows, piece[:, None], expert ^ k, 1
        )
    context_rows = context_rows.reshape(planes, 2, tokens, features)
    sides = [
        pick(context_rows, side, 1).reshape(planes * tokens, features) for side in (core, 1 - core)
    ]

    signs = pl.pallas_call(
        functools.partial(signs_kernel, experts),
        out_shape=jax.ShapeDtypeStruct((blocks, capacity, lanes), jnp.float32),
        in_specs=[smem(), whole(ids_all.shape)],
        out_specs=whole((blocks, capacity, lanes)),
        grid=(1,),
        compiler_params=params(),
        name="signs",
    )(position, ids_all).reshape(planes, 2, capacity, lanes)

    branch = branch_wo[0]
    half = branch.shape[0] // 2
    own_bits = [(expert >> (bits - 1 - i)) & 1 for i in range(bits)]

    def block_view(c, h):
        rows = branch[h * half : (h + 1) * half].reshape((half,) + (2,) * bits + (columns,))
        return rows[..., c * part : (c + 1) * part]

    held = {(c, h): block_view(c, h) for c in range(CHUNKS) for h in range(2)}
    remaining = {h: list(range(bits)) for h in range(2)}
    for phase in range(bits):
        before = None
        for c in range(CHUNKS):
            sends, axes = [], []
            for h in range(2):
                i = bits - 1 - phase if h == 0 else phase
                axis = 1 + sum(1 for j in remaining[h] if j < i)
                axes.append((i, axis))
                sends.append(pick(held[c, h], 1 - own_bits[i], axis).astype(jnp.bfloat16))
            if before is not None:
                sends, before = lax.optimization_barrier((sends, before))
            got = [
                exchange(sends[h], "expert", 1 << (bits - 1 - axes[h][0])) for h in range(2)
            ]
            before = got
            for h in range(2):
                kept = pick(held[c, h], own_bits[axes[h][0]], axes[h][1])
                held[c, h] = kept.astype(jnp.float32) + got[h].astype(jnp.float32)
        for h in range(2):
            remaining[h].remove(bits - 1 - phase if h == 0 else phase)

    gate_view = gate_w.reshape(experts, CHUNKS, part, units)
    up_view = up_w.reshape(experts, CHUNKS, part, units)
    tile = min(256, units)
    tiles = units // tile
    merged_parts = []
    row_parts = []
    partial = None
    for c in range(CHUNKS):
        span = slice(c * part, (c + 1) * part)
        merged = jnp.concatenate([held[c, 0], held[c, 1]]) / experts
        merged = merged.astype(jnp.bfloat16)
        merged_parts.append(merged)

        def attend(rows):
            out = jnp.dot(rows, merged, preferred_element_type=jnp.float32)
            return out.reshape(planes, tokens, part)

        swapped = exchange(attend(sides[1]).astype(jnp.bfloat16), "fsdp", 1)
        pair = attend(sides[0]) + swapped.astype(jnp.float32)
        hstate = residual[:, span].astype(jnp.float32) + pick(pair, plane, 0)
        for k in range(1, planes):
            arrived = exchange(pick(pair, plane ^ k, 0).astype(jnp.bfloat16), "fsdp", 2 * k)
            hstate = hstate + arrived.astype(jnp.float32)
        scaled = (hstate * norm_gain[span].astype(jnp.float32)).astype(jnp.bfloat16)
        own_tokens = [exchange(scaled, "fsdp", 2 * k) if k else scaled for k in range(planes)]

        slots = pl.pallas_call(
            dispatch_kernel,
            out_shape=jax.ShapeDtypeStruct((experts, planes, capacity, part), jnp.bfloat16),
            in_specs=[smem(), whole(ids_all.shape)] + [whole((tokens, part))] * planes,
            out_specs=whole((experts, planes, capacity, part)),
            grid=(1,),
            compiler_params=params(),
            name="dispatch",
        )(position, ids_all, *own_tokens)
        rows = lax.all_to_all(
            slots.reshape(experts, count, part), "expert", split_axis=0, concat_axis=0, tiled=True
        )
        other = exchange(rows, "fsdp", 1)
        row_parts.append((rows, other))

        if c == 0:
            aux_spec = pl.BlockSpec((experts, lanes, part), lambda n: (0, 0, 0))
            weight_spec = pl.BlockSpec((experts, 1, part, tile), lambda n: (0, 0, 0, n))
            sums = jax.ShapeDtypeStruct((2, count, units), jnp.float32)
            sum_spec = pl.BlockSpec((2, count, tile), lambda n: (0, 0, n))
            partial = pl.pallas_call(
                early_kernel,
                out_shape=(sums, sums, jax.ShapeDtypeStruct((2, count, lanes), jnp.float32)),
                in_specs=[whole(rows.shape)] * 2 + [aux_spec, weight_spec, weight_spec],
                out_specs=(sum_spec, sum_spec, whole((2, count, lanes))),
                grid=(tiles,),
                compiler_params=params(),
                cost_estimate=pl.CostEstimate(
                    flops=8 * count * experts * part * units,
                    bytes_accessed=4 * experts * part * units,
                    transcendentals=0,
                ),
                name="early",
            )(rows, other, aux, gate_view, up_view)

    aux_spec = pl.BlockSpec((experts, lanes, part), lambda i: (0, 0, 1))
    tile_of = lambda i: jnp.minimum(i, tiles - 1)
    weight_spec = pl.BlockSpec((experts, 1, part, tile), lambda i: (0, 1, 0, tile_of(i)))
    sum_spec = pl.BlockSpec((2, count, tile), lambda i: (0, 0, tile_of(i)))
    unit_spec = pl.BlockSpec((planes, 2, capacity, tile), lambda i: (0, 0, 0, tile_of(i)))

    def grad_index(i):
        place = jnp.maximum(i - tiles, 0)
        return (place // 2, place % 2, 0, 0)

    grad_spec = pl.BlockSpec((1, 1, part, units), grad_index)
    grad_shape = jax.ShapeDtypeStruct((experts, CHUNKS, part, units), jnp.bfloat16)
    row_spec = whole(row_parts[0][0].shape)
    hidden, grad_gate, grad_up = pl.pallas_call(
        functools.partial(late_kernel, float(width), tiles),
        out_shape=(
            jax.ShapeDtypeStruct((planes, 2, capacity, units), jnp.bfloat16),
            grad_shape,
            grad_shape,
        ),
        in_specs=[smem()]
        + [row_spec] * 4
        + [aux_spec, weight_spec, weight_spec, sum_spec, sum_spec]
        + [whole((2, count, lanes)), whole(signs.shape), unit_spec],
        out_specs=(unit_spec, grad_spec, grad_spec),
        grid=(tiles + experts * CHUNKS,),
        scratch_shapes=[
            pltpu.VMEM((2, count, 1), jnp.float32),
            pltpu.VMEM((2, count, 1), jnp.float32),
            pltpu.VMEM((2 * count, units), jnp.bfloat16),
            pltpu.VMEM((2 * count, units), jnp.bfloat16),
            pltpu.VMEM((part, 2 * count), jnp.bfloat16),
        ],
        compiler_params=params(),
        name="late",
    )(
        position,
        *row_parts[0],
        *row_parts[1],
        aux,
        gate_view,
        up_view,
        *partial,
        signs,
        cot_hidden.reshape(planes, 2, capacity, units),
    )
    return (
        jnp.concatenate(merged_parts, axis=1),
        hidden.reshape(1, -1, units),
        grad_gate.reshape(1, width, units),
        grad_up.reshape(1, width, units),
    )


def solution(mesh):
    placed = (
        P("expert", "fsdp", None),
        P("fsdp", "expert"),
        P("fsdp", "expert"),
        P("expert"),
        P("expert", None),
        P("expert", None, "fsdp"),
        P("expert", None, "fsdp"),
        P("fsdp", None),
        P("fsdp", None),
        P("expert", None, "fsdp"),
    )
    return jax.shard_map(
        per_device,
        mesh=mesh,
        in_specs=placed,
        out_specs=(
            P("fsdp", "expert"),
            P("expert", None, "fsdp"),
            P("expert", None, "fsdp"),
            P("expert", None, "fsdp"),
        ),
        check_vma=False,
    )
```

time: 322 us -> 227 us (0.70)
  waiting for transfers between devices: 215 us -> 73.4 us
  Pallas kernels: 0 us -> 49.7 us
  starting transfers between devices: 0.16 us -> 48.6 us
  matrix products: 47.7 us -> 5.44 us
  blocking collectives: 36.6 us -> 0 us
  local copies, waits for them, and re-layouts: 2.82 us -> 33 us
  between operations: 14.6 us -> 1.25 us
  other arithmetic: 4.71 us -> 14.3 us
    all_gather x3 -> x0, waiting for transfers between devices: 156 us -> none  [the longest x1 84.4 us: per_device(): lax.all_gather(merged, 'fsdp', axis=0, tiled=True)]
    reduce_scatter x1 -> x0, waiting for transfers between devices: 57.7 us -> none  [per_device(): lax.psum_scatter(local_branch.astype(jnp.bfloat16), 'expert', scatter_dim...]
    ppermute x0 -> x27, waiting for transfers between devices: none -> 50.5 us  [exchange(): return lax.ppermute(value, axis, [(i, i ^ offset) for i in range(size)])]
    pallas_call x0 -> x5, Pallas kernels: none -> 49.7 us  [the longest x1 32.4 us: per_device(): pl.pallas_call(functools.partial(late_kernel, float(width), tiles), out_s...]
    dot_general x7 -> x4, matrix products: 47.7 us -> 5.44 us  [attend(): out = jnp.dot(rows, merged, preferred_element_type=jnp.float32)]
    ppermute x0 -> x27, starting transfers between devices: none -> 30.5 us  [exchange(): return lax.ppermute(value, axis, [(i, i ^ offset) for i in range(size)])]
    all_to_all x0 -> x4, waiting for transfers between devices: none -> 22.9 us  [the longest x2 22.9 us: per_device(): lax.all_to_all(slots.reshape(experts, count, part), 'expert', split_axis=...]
    all_to_all x0 -> x4, starting transfers between devices: none -> 18.1 us  [the longest x2 8.1 us: per_device(): lax.all_to_all(slots.reshape(experts, count, part), 'expert', split_axis=...]
  transfers between devices with their start and end apart: 4 -> 31, of which waited for: 4 -> 13; matrix products, arithmetic and copies ran while one was open for 1% -> 20% of each run, Pallas kernels for 0% -> 7%
where the time goes in v2:
time: 227 us; the launch traced here: 226 us
  waiting for transfers between devices  73.4 us (32%)
  Pallas kernels  49.7 us (22%)
  starting transfers between devices  48.6 us (21%)
  local copies, waits for them, and re-layouts  33 us (15%)
  other arithmetic  14.3 us (6%)
  matrix products  5.44 us (2%)
    ppermute x27, waiting for transfers between devices, exchange(): return lax.ppermute(value, axis, [(i, i ^ offset) for i in range(size)])  50.5 us
    pallas_call x1, Pallas kernels, per_device(): pl.pallas_call(functools.partial(late_kernel, float(width), tiles), out_s...  32.4 us
    ppermute x27, starting transfers between devices, exchange(): return lax.ppermute(value, axis, [(i, i ^ offset) for i in range(size)])  30.5 us
    all_to_all x2, waiting for transfers between devices, per_device(): lax.all_to_all(slots.reshape(experts, count, part), 'expert', split_axis=...  22.9 us
    unnamed x43, local copies, waits for them, and re-layouts  17.7 us
    pallas_call x1, Pallas kernels, per_device(): pl.pallas_call(early_kernel, out_shape=(sums, sums, jax.ShapeDtypeStruct(...  12 us
    all_to_all x2, starting transfers between devices, per_device(): lax.all_to_all(slots.reshape(experts, count, part), 'expert', split_axis=...  8.1 us
    add x8, other arithmetic, per_device(): held[c, h] = kept.astype(jnp.float32) + got[h].astype(jnp.float32)  7.08 us
  transfers between devices with their start and end apart: 31, of which 13 were waited for; matrix products, arithmetic and copies ran while one was open for 20% of the time, Pallas kernels for 7%

profile of v2, /device:TPU:0, one launch (start us, length us, event | category | flops | bytes accessed | tf_op | source)
XLA Modules:
  0.0 225.8 jit_solution(1222802599855323532)
XLA Ops:
  2.1 1.7 pad_maximum_fusion.1
  3.8 5.2 %all-to-all-start = ((bf16[4,48,1024]{2,1,0:T(8,128)(2,1)}), bf16[4,48,1024]{2,1,0:T(8,128)(2,1)S(1)}, u32[]{:S(2)}, u32[]{:S(2)}) async-start(bf16[4,48,1024]{2,1,0:T(8,128)(2,1)} %pad_maximum_fusion.1), calls=%async_computation | async-start | bytes 786432 | tf_op jit(solution)/shard_map/all_to_all | solution.py:233
  9.0 4.7 %fusion.47 = (bf16[1,256,4096]{2,1,0:T(8,128)(2,1)}, bf16[1,256,4096]{2,1,0:T(8,128)(2,1)}) fusion(bf16[1,512,4096]{2,1,0:T(8,128)(2,1)} %param.10), kind=kLoop, calls=%fused_computation.92 | loop fusion | bytes 8388608 | tf_op jit(solution)/shard_map/slice | solution.py:274
  13.7 3.3 %copy.27 = bf16[1,256,4096]{1,2,0:T(8,128)(2,1)S(1)} copy(bf16[1,256,4096]{2,1,0:T(8,128)(2,1)} %get-tuple-element.24) | data formatting | bytes 4194304
  17.0 1.1 fusion.48
  18.1 2.4 %constant_dynamic-slice_fusion = (bf16[256,1,2,512]{0,3,2,1:T(8,128)(2,1)}, bf16[256,1,2,512]{0,3,2,1:T(8,128)(2,1)}, bf16[256,1,2,512]{0,3,2,1:T(8,128)(2,1)S(1)}, bf16[256,1,2,512]{0,3,2,1:T(8,128)(2,1)}) fusion(bf16[256,2,2,512]{0,3,2,1:T(8,128)(2,1)} %get-tuple-element.27, s32[]{:T(128)S(6)} %select_n.76, s32[]{:T(128)S(6)} %select_n.77, ...), kind=kLoop, calls=%fused_computation.79 | loop fusion | bytes 4194312 | tf_op jit(solution)/shard_map/jit(dynamic_index_in_dim)/dynamic_slice | solution.py:20
  20.4 1.0 copy.30
  21.5 2.0 collective-permute-start.2
  23.5 3.3 %copy.23 = bf16[1,256,4096]{1,2,0:T(8,128)(2,1)S(1)} copy(bf16[1,256,4096]{2,1,0:T(8,128)(2,1)} %get-tuple-element.25) | data formatting | bytes 4194304
  26.8 1.1 fusion.49
  27.9 2.4 %constant_dynamic-slice_fusion.3 = (bf16[256,2,1,512]{0,3,2,1:T(8,128)(2,1)}, bf16[256,2,1,512]{0,3,2,1:T(8,128)(2,1)}, bf16[256,2,1,512]{0,3,2,1:T(8,128)(2,1)S(1)}, bf16[256,2,1,512]{0,3,2,1:T(8,128)(2,1)S(1)}) fusion(bf16[256,2,2,512]{0,3,2,1:T(8,128)(2,1)} %get-tuple-element.29, s32[]{:T(128)S(6)} %select_n.74, s32[]{:T(128)S(6)} %select_n.75, ...), kind=kLoop, calls=%fused_computation.82 | loop fusion | bytes 4194312 | tf_op jit(solution)/shard_map/jit(dynamic_index_in_dim)/dynamic_slice | solution.py:20
  30.3 1.0 copy.26
  31.3 1.5 collective-permute-start
  33.0 1.0 copy.25
  34.9 4.9 %all-to-all-start.1 = ((bf16[8,48,512]{2,1,0:T(8,128)(2,1)}), bf16[8,48,512]{2,1,0:T(8,128)(2,1)S(1)}, u32[]{:S(2)}, u32[]{:S(2)}) async-start(bf16[8,48,512]{2,1,0:T(8,128)(2,1)} %pad_maximum_fusion.2), calls=%async_computation.1 | async-start | bytes 786432 | tf_op jit(solution)/shard_map/all_to_all | solution.py:244
  39.8 1.2 convert_add_fusion.2
  42.3 2.1 collective-permute-done
  44.4 1.4 convert_add_fusion.3
  46.8 1.0 copy.36
  47.8 1.0 copy.35
  48.8 2.1 copy.32
  50.9 1.0 copy.33
  51.9 2.1 collective-permute-start.4
  54.0 1.2 collective-permute-start.5
  55.2 1.0 bitcast_add_fusion.2
  56.2 1.0 bitcast_add_fusion.3
  58.4 2.6 %collective-permute-start.10 = (bf16[8,32,512]{2,1,0:T(8,128)(2,1)S(1)}, bf16[8,32,512]{2,1,0:T(8,128)(2,1)S(1)}, u32[]{:S(2)}, u32[]{:S(2)}) collective-permute-start(bf16[8,32,512]{2,1,0:T(8,128)(2,1)S(1)} %slice.74), channel_id=1, source_target_pairs={{0,24},{8,16},{16,8},{24,0},{1,25},{9,17},{17,9},{25,1},{2,26},{10... | collective-permute-start | bytes 786440 | tf_op jit(solution)/shard_map/ppermute | solution.py:16
  61.2 6.0 %collective-permute-done.4 = bf16[256,2,512]{2,0,1:T(8,128)(2,1)} collective-permute-done((bf16[256,2,512]{2,0,1:T(8,128)(2,1)}, bf16[256,2,512]{2,0,1:T(8,128)(2,1)}, u32[]{:S(2)}, u32[]{:S(2)}) %collective-permute-start.4) | collective-permute-done | bytes 524320 | tf_op jit(solution)/shard_map/ppermute | solution.py:16
  67.2 1.2 convert_add_fusion.1
  68.3 2.5 %collective-permute-done.5 = bf16[256,2,512]{2,0,1:T(8,128)(2,1)} collective-permute-done((bf16[256,2,512]{2,0,1:T(8,128)(2,1)}, bf16[256,2,512]{2,0,1:T(8,128)(2,1)}, u32[]{:S(2)}, u32[]{:S(2)}) %collective-permute-start.5) | collective-permute-done | bytes 524320 | tf_op jit(solution)/shard_map/ppermute | solution.py:16
  70.8 1.2 convert_add_fusion
  72.1 1.8 collective-permute-start.6
  73.9 5.4 %collective-permute-done.9 = bf16[8,32,512]{2,1,0:T(8,128)(2,1)S(1)} collective-permute-done((bf16[8,32,512]{2,1,0:T(8,128)(2,1)S(1)}, bf16[8,32,512]{2,1,0:T(8,128)(2,1)S(1)}, u32[]{:S(2)}, u32[]{:S(2)}) %collective-permute-start.9) | collective-permute-done | bytes 262176 | tf_op jit(solution)/shard_map/ppermute | solution.py:16
  79.4 1.2 convolution_convert_fusion.1
  80.6 1.5 collective-permute-done.6
  82.4 1.2 convolution_convert_fusion
  83.7 1.5 convert_add_fusion.5
  85.3 1.7 collective-permute-start.12
  87.0 2.4 %collective-permute-start.14 = (bf16[128,512]{1,0:T(8,128)(2,1)S(1)}, bf16[128,512]{1,0:T(8,128)(2,1)}, u32[]{:S(2)}, u32[]{:S(2)}) collective-permute-start(bf16[128,512]{1,0:T(8,128)(2,1)S(1)} %get-tuple-element.34), channel_id=1, source_target_pairs={{0,6},{1,7},{2,4},{3,5},{4,2},{5,3},{6,0},{7,1},{8,14},{9,15},{10,... | collective-permute-start | bytes 393224 | tf_op jit(solution)/shard_map/ppermute | solution.py:16
  89.4 1.5 convert_add_fusion.4
  90.9 1.0 copy-done.2
  91.9 2.0 collective-permute-start.20
  94.0 2.4 %collective-permute-start.22 = (bf16[128,512]{1,0:T(8,128)(2,1)S(1)}, bf16[128,512]{1,0:T(8,128)(2,1)S(1)}, u32[]{:S(2)}, u32[]{:S(2)}) collective-permute-start(bf16[128,512]{1,0:T(8,128)(2,1)S(1)} %get-tuple-element.31), channel_id=1, source_target_pairs={{0,6},{1,7},{2,4},{3,5},{4,2},{5,3},{6,0},{7,1},{8,14},{9,15},{10,... | collective-permute-start | bytes 393224 | tf_op jit(solution)/shard_map/ppermute | solution.py:16
  97.1 10.8 %collective-permute-done.13 = bf16[128,512]{1,0:T(8,128)(2,1)} collective-permute-done((bf16[128,512]{1,0:T(8,128)(2,1)S(1)}, bf16[128,512]{1,0:T(8,128)(2,1)}, u32[]{:S(2)}, u32[]{:S(2)}) %collective-permute-start.13) | collective-permute-done | bytes 131104 | tf_op jit(solution)/shard_map/ppermute | solution.py:16
  107.8 5.1 %collective-permute-done.21 = bf16[128,512]{1,0:T(8,128)(2,1)S(1)} collective-permute-done((bf16[128,512]{1,0:T(8,128)(2,1)S(1)}, bf16[128,512]{1,0:T(8,128)(2,1)S(1)}, u32[]{:S(2)}, u32[]{:S(2)}) %collective-permute-start.21) | collective-permute-done | bytes 131104 | tf_op jit(solution)/shard_map/ppermute | solution.py:16
  113.0 1.3 fusion.28
  114.3 2.7 %collective-permute-start.17 = (bf16[128,512]{1,0:T(8,128)(2,1)S(1)}, bf16[128,512]{1,0:T(8,128)(2,1)S(1)}, u32[]{:S(2)}, u32[]{:S(2)}) collective-permute-start(bf16[128,512]{1,0:T(8,128)(2,1)S(1)} %get-tuple-element.47.refs_0_), channel_id=1, source_target_pairs={{0,6},{1,7},{2,4},{3,5},{4,2},{5,3},{6,0},{7,1},{8,14},{9,15},{10,... | collective-permute-start | bytes 393224 | tf_op jit(solution)/shard_map/ppermute | solution.py:16
  117.0 1.7 collective-permute-start.15
  118.7 3.8 %collective-permute-done.17.refs_3_ = bf16[128,512]{1,0:T(8,128)(2,1)S(1)} collective-permute-done((bf16[128,512]{1,0:T(8,128)(2,1)S(1)}, bf16[128,512]{1,0:T(8,128)(2,1)S(1)}, u32[]{:S(2)}, u32[]{:S(2)}) %collective-permute-start.17) | collective-permute-done | bytes 131104 | tf_op jit(solution)/shard_map/ppermute | solution.py:16
  122.6 4.3 %collective-permute-done.16.refs_2_ = bf16[128,512]{1,0:T(8,128)(2,1)S(1)} collective-permute-done((bf16[128,512]{1,0:T(8,128)(2,1)S(1)}, bf16[128,512]{1,0:T(8,128)(2,1)S(1)}, u32[]{:S(2)}, u32[]{:S(2)}) %collective-permute-start.16) | collective-permute-done | bytes 131104 | tf_op jit(solution)/shard_map/ppermute | solution.py:16
  127.0 2.2 dispatch.2
  129.2 3.6 %all-to-all-start.2 = ((bf16[4,384,512]{2,1,0:T(8,128)(2,1)}), bf16[4,384,512]{2,1,0:T(8,128)(2,1)S(1)}, u32[]{:S(2)}, u32[]{:S(2)}) async-start(bf16[4,384,512]{2,1,0:T(8,128)(2,1)} %bitcast.41), calls=%async_computation.2 | async-start | bytes 3145728 | tf_op jit(solution)/shard_map/all_to_all | solution.py:335
  132.8 2.3 %collective-permute-start.25 = (bf16[128,512]{1,0:T(8,128)(2,1)S(1)}, bf16[128,512]{1,0:T(8,128)(2,1)S(1)}, u32[]{:S(2)}, u32[]{:S(2)}) collective-permute-start(bf16[128,512]{1,0:T(8,128)(2,1)S(1)} %get-tuple-element.46.refs_0_), channel_id=1, source_target_pairs={{0,6},{1,7},{2,4},{3,5},{4,2},{5,3},{6,0},{7,1},{8,14},{9,15},{10,... | collective-permute-start | bytes 393224 | tf_op jit(solution)/shard_map/ppermute | solution.py:16
  135.1 2.1 collective-permute-start.23
  137.2 3.9 %collective-permute-done.25.refs_3_ = bf16[128,512]{1,0:T(8,128)(2,1)S(1)} collective-permute-done((bf16[128,512]{1,0:T(8,128)(2,1)S(1)}, bf16[128,512]{1,0:T(8,128)(2,1)S(1)}, u32[]{:S(2)}, u32[]{:S(2)}) %collective-permute-start.25) | collective-permute-done | bytes 131104 | tf_op jit(solution)/shard_map/ppermute | solution.py:16
  141.1 5.0 %collective-permute-done.24.refs_2_ = bf16[128,512]{1,0:T(8,128)(2,1)S(1)} collective-permute-done((bf16[128,512]{1,0:T(8,128)(2,1)S(1)}, bf16[128,512]{1,0:T(8,128)(2,1)S(1)}, u32[]{:S(2)}, u32[]{:S(2)}) %collective-permute-start.24) | collective-permute-done | bytes 131104 | tf_op jit(solution)/shard_map/ppermute | solution.py:16
  146.2 2.2 dispatch.3
  148.4 4.1 %all-to-all-done.2.own_ref.own0_ref = bf16[4,384,512]{2,1,0:T(8,128)(2,1)S(1)} async-done(((bf16[4,384,512]{2,1,0:T(8,128)(2,1)}), bf16[4,384,512]{2,1,0:T(8,128)(2,1)S(1)}, u32[]{:S(2)}, u32[]{:S(2)}) %all-to-all-start.2) | async-done | bytes 1572896 | tf_op jit(solution)/shard_map/all_to_all | solution.py:335
  152.6 4.5 %all-to-all-start.3 = ((bf16[4,384,512]{2,1,0:T(8,128)(2,1)}), bf16[4,384,512]{2,1,0:T(8,128)(2,1)}, u32[]{:S(2)}, u32[]{:S(2)}) async-start(bf16[4,384,512]{2,1,0:T(8,128)(2,1)} %bitcast.47), calls=%async_computation.3 | async-start | bytes 3145728 | tf_op jit(solution)/shard_map/all_to_all | solution.py:335
  157.2 18.8 %all-to-all-done.3.own1_ref = bf16[4,384,512]{2,1,0:T(8,128)(2,1)} async-done(((bf16[4,384,512]{2,1,0:T(8,128)(2,1)}), bf16[4,384,512]{2,1,0:T(8,128)(2,1)}, u32[]{:S(2)}, u32[]{:S(2)}) %all-to-all-start.3) | async-done | bytes 1572896 | tf_op jit(solution)/shard_map/all_to_all | solution.py:335
  177.7 2.3 %pad_maximum_fusion = bf16[512,1024]{1,0:T(8,128)(2,1)} fusion(bf16[512,512]{1,0:T(8,128)(2,1)} %copy-done.1, bf16[512,512]{1,0:T(8,128)(2,1)} %copy-done), kind=kLoop, calls=%fused_computation.6 | loop fusion | flops 2097152 | bytes 2097152 | tf_op jit(solution)/shard_map/concatenate | solution.py:408
  180.0 12.0 %early.1 = (f32[2,384,1024]{2,1,0:T(8,128)}, f32[2,384,1024]{2,1,0:T(8,128)}, f32[2,384,16]{2,1,0:T(8,128)S(1)}) custom-call(bf16[4,384,512]{2,1,0:T(8,128)(2,1)S(1)} %all-to-all-done.2.own_ref.own0_ref, bf16[4,384,512]{2,1,0:T(8,128)(2,1)S(1)} %collective-permute-done.18.other_ref.other0_ref, bf16[4,16,1024]{2,1,0:T(8,128)(2,1)S(1)} %slice.75.aux_ref, ...), custom_call_target="tpu_custom_call" | custom-call | flops 6442450944 | bytes 8388608 | tf_op jit(solution)/shard_map/early/pallas_call | solution.py:346
  192.0 1.2 copy-done.9
  193.2 32.4 %late.1 = (bf16[4,2,96,1024]{3,2,1,0:T(8,128)(2,1)}, bf16[4,2,512,1024]{3,2,1,0:T(8,128)(2,1)}, bf16[4,2,512,1024]{3,2,1,0:T(8,128)(2,1)}) custom-call(s32[3]{0:T(128)S(1)} %pad_add_fusion.position_ref, bf16[4,384,512]{2,1,0:T(8,128)(2,1)S(1)} %all-to-all-done.2.own_ref.own0_ref, bf16[4,384,512]{2,1,0:T(8,128)(2,1)S(1)} %collective-permute-done.18.other_ref.other0_ref, ...), custom_call_target="tpu_custom_call" | custom-call | tf_op jit(solution)/shard_map/late/pallas_call | solution.py:374
  (95 shorter events, 9.3 us)
Async XLA Ops:
  3.8 30.2 %all-to-all-start = ((bf16[4,48,1024]{2,1,0:T(8,128)(2,1)}), bf16[4,48,1024]{2,1,0:T(8,128)(2,1)S(1)}, u32[]{:S(2)}, u32[]{:S(2)}) async-start(bf16[4,48,1024]{2,1,0:T(8,128)(2,1)} %pad_maximum_fusion.1), calls=%async_computation | async-start | bytes 786432 | tf_op jit(solution)/shard_map/all_to_all | solution.py:233
  21.5 18.3 %collective-permute-start.2 = (bf16[256,2,512]{2,0,1:T(8,128)(2,1)}, bf16[256,2,512]{2,0,1:T(8,128)(2,1)}, u32[]{:S(2)}, u32[]{:S(2)}) collective-permute-start(bf16[256,2,512]{2,0,1:T(8,128)(2,1)} %bitcast.7), channel_id=1, source_target_pairs={{0,16},{8,24},{16,0},{24,8},{1,17},{9,25},{17,1},{25,9},{2,18},{10... | collective-permute-start | bytes 1572872 | tf_op jit(solution)/shard_map/ppermute | solution.py:16
  27.9 4.9 %copy-start.14 = (s32[128,2]{0,1:T(2,128)S(1)}, s32[128,2]{0,1:T(2,128)}, u32[]{:S(2)}) copy-start(s32[128,2]{0,1:T(2,128)} %param.17) | copy-start | bytes 3076
  27.9 4.9 %copy-start.15 = (s32[128,2]{0,1:T(2,128)S(1)}, s32[128,2]{0,1:T(2,128)}, u32[]{:S(2)}) copy-start(s32[128,2]{0,1:T(2,128)} %param.18) | copy-start | bytes 3076
  27.9 4.9 %copy-start.6 = (bf16[256,1,2,512]{0,3,2,1:T(8,128)(2,1)S(1)}, bf16[256,1,2,512]{0,3,2,1:T(8,128)(2,1)}, u32[]{:S(2)}) copy-start(bf16[256,1,2,512]{0,3,2,1:T(8,128)(2,1)} %get-tuple-element.53) | copy-start | bytes 1572868
  31.3 13.1 %collective-permute-start = (bf16[256,2,512]{2,0,1:T(8,128)(2,1)}, bf16[256,2,512]{2,0,1:T(8,128)(2,1)}, u32[]{:S(2)}, u32[]{:S(2)}) collective-permute-start(bf16[256,2,512]{2,0,1:T(8,128)(2,1)} %bitcast.2), channel_id=1, source_target_pairs={{0,8},{8,0},{16,24},{24,16},{1,9},{9,1},{17,25},{25,17},{2,10},{10... | collective-permute-start | bytes 1572872 | tf_op jit(solution)/shard_map/ppermute | solution.py:16
  34.0 0.9 copy-start.10
  34.9 22.5 %all-to-all-start.1 = ((bf16[8,48,512]{2,1,0:T(8,128)(2,1)}), bf16[8,48,512]{2,1,0:T(8,128)(2,1)S(1)}, u32[]{:S(2)}, u32[]{:S(2)}) async-start(bf16[8,48,512]{2,1,0:T(8,128)(2,1)} %pad_maximum_fusion.2), calls=%async_computation.1 | async-start | bytes 786432 | tf_op jit(solution)/shard_map/all_to_all | solution.py:244
  41.0 5.8 %copy-start.4 = (bf16[256,1,2,512]{0,3,2,1:T(8,128)(2,1)S(1)}, bf16[256,1,2,512]{0,3,2,1:T(8,128)(2,1)}, u32[]{:S(2)}) copy-start(bf16[256,1,2,512]{0,3,2,1:T(8,128)(2,1)} %get-tuple-element.40) | copy-start | bytes 1572868
  41.0 6.8 %copy-start.3 = (bf16[256,1,2,512]{0,3,2,1:T(8,128)(2,1)S(1)}, bf16[256,1,2,512]{0,3,2,1:T(8,128)(2,1)}, u32[]{:S(2)}) copy-start(bf16[256,1,2,512]{0,3,2,1:T(8,128)(2,1)} %get-tuple-element.41) | copy-start | bytes 1572868
  41.8 13.4 %collective-permute-start.3 = (bf16[256,512]{1,0:T(8,128)(2,1)}, bf16[256,512]{1,0:T(8,128)(2,1)}, u32[]{:S(2)}, u32[]{:S(2)}) collective-permute-start(bf16[256,512]{1,0:T(8,128)(2,1)} %fusion.21), channel_id=1, source_target_pairs={{0,8},{8,0},{16,24},{24,16},{1,9},{9,1},{17,25},{25,17},{2,10},{10... | collective-permute-start | bytes 786440 | tf_op jit(solution)/shard_map/ppermute | solution.py:16
  46.5 9.7 %collective-permute-start.1 = (bf16[256,512]{1,0:T(8,128)(2,1)}, bf16[256,512]{1,0:T(8,128)(2,1)}, u32[]{:S(2)}, u32[]{:S(2)}) collective-permute-start(bf16[256,512]{1,0:T(8,128)(2,1)} %fusion.20), channel_id=1, source_target_pairs={{0,16},{8,24},{16,0},{24,8},{1,17},{9,25},{17,1},{25,9},{2,18},{10... | collective-permute-start | bytes 786440 | tf_op jit(solution)/shard_map/ppermute | solution.py:16
  47.8 3.1 %copy-start.5 = (bf16[256,2,1,512]{0,3,2,1:T(8,128)(2,1)S(1)}, bf16[256,2,1,512]{0,3,2,1:T(8,128)(2,1)}, u32[]{:S(2)}) copy-start(bf16[256,2,1,512]{0,3,2,1:T(8,128)(2,1)} %get-tuple-element.43) | copy-start | bytes 1572868
  51.9 15.2 %collective-permute-start.4 = (bf16[256,2,512]{2,0,1:T(8,128)(2,1)}, bf16[256,2,512]{2,0,1:T(8,128)(2,1)}, u32[]{:S(2)}, u32[]{:S(2)}) collective-permute-start(bf16[256,2,512]{2,0,1:T(8,128)(2,1)} %bitcast.11), channel_id=1, source_target_pairs={{0,8},{8,0},{16,24},{24,16},{1,9},{9,1},{17,25},{25,17},{2,10},{10... | collective-permute-start | bytes 1572872 | tf_op jit(solution)/shard_map/ppermute | solution.py:16
  54.0 16.8 %collective-permute-start.5 = (bf16[256,2,512]{2,0,1:T(8,128)(2,1)}, bf16[256,2,512]{2,0,1:T(8,128)(2,1)}, u32[]{:S(2)}, u32[]{:S(2)}) collective-permute-start(bf16[256,2,512]{2,0,1:T(8,128)(2,1)} %bitcast.12), channel_id=1, source_target_pairs={{0,16},{8,24},{16,0},{24,8},{1,17},{9,25},{17,1},{25,9},{2,18},{10... | collective-permute-start | bytes 1572872 | tf_op jit(solution)/shard_map/ppermute | solution.py:16
  57.4 26.3 %copy-start = (bf16[512,512]{1,0:T(8,128)(2,1)}, bf16[512,512]{1,0:T(8,128)(2,1)S(1)}, u32[]{:S(2)}) copy-start(bf16[512,512]{1,0:T(8,128)(2,1)S(1)} %fusion) | copy-start | bytes 1572868
  57.4 9.8 %copy-start.8 = (bf16[256,2,1,512]{3,0,1,2:T(8,128)(2,1)S(1)}, bf16[256,2,1,512]{3,0,1,2:T(8,128)(2,1)}, u32[]{:S(2)}) copy-start(bf16[256,2,1,512]{3,0,1,2:T(8,128)(2,1)} %copy.32) | copy-start | bytes 1572868
  57.4 13.4 %copy-start.7 = (bf16[256,1,2,512]{3,0,2,1:T(8,128)(2,1)S(1)}, bf16[256,1,2,512]{3,0,2,1:T(8,128)(2,1)}, u32[]{:S(2)}) copy-start(bf16[256,1,2,512]{3,0,2,1:T(8,128)(2,1)} %copy.36) | copy-start | bytes 1572868
  57.5 21.9 %collective-permute-start.9 = (bf16[8,32,512]{2,1,0:T(8,128)(2,1)S(1)}, bf16[8,32,512]{2,1,0:T(8,128)(2,1)S(1)}, u32[]{:S(2)}, u32[]{:S(2)}) collective-permute-start(bf16[8,32,512]{2,1,0:T(8,128)(2,1)S(1)} %slice.74), channel_id=1, source_target_pairs={{0,16},{8,24},{16,0},{24,8},{1,17},{9,25},{17,1},{25,9},{2,18},{10... | collective-permute-start | bytes 786440 | tf_op jit(solution)/shard_map/ppermute | solution.py:16
  58.4 15.5 %collective-permute-start.8 = (bf16[8,32,512]{2,1,0:T(8,128)(2,1)S(1)}, bf16[8,32,512]{2,1,0:T(8,128)(2,1)S(1)}, u32[]{:S(2)}, u32[]{:S(2)}) collective-permute-start(bf16[8,32,512]{2,1,0:T(8,128)(2,1)S(1)} %slice.74), channel_id=1, source_target_pairs={{0,8},{8,0},{16,24},{24,16},{1,9},{9,1},{17,25},{25,17},{2,10},{10... | collective-permute-start | bytes 786440 | tf_op jit(solution)/shard_map/ppermute | solution.py:16
  58.4 21.0 %collective-permute-start.10 = (bf16[8,32,512]{2,1,0:T(8,128)(2,1)S(1)}, bf16[8,32,512]{2,1,0:T(8,128)(2,1)S(1)}, u32[]{:S(2)}, u32[]{:S(2)}) collective-permute-start(bf16[8,32,512]{2,1,0:T(8,128)(2,1)S(1)} %slice.74), channel_id=1, source_target_pairs={{0,24},{8,16},{16,8},{24,0},{1,25},{9,17},{17,9},{25,1},{2,26},{10... | collective-permute-start | bytes 786440 | tf_op jit(solution)/shard_map/ppermute | solution.py:16
  72.1 10.0 %collective-permute-start.6 = (bf16[256,512]{1,0:T(8,128)(2,1)S(1)}, bf16[256,512]{1,0:T(8,128)(2,1)S(1)}, u32[]{:S(2)}, u32[]{:S(2)}) collective-permute-start(bf16[256,512]{1,0:T(8,128)(2,1)S(1)} %fusion.22), channel_id=1, source_target_pairs={{0,16},{8,24},{16,0},{24,8},{1,17},{9,25},{17,1},{25,9},{2,18},{10... | collective-permute-start | bytes 786440 | tf_op jit(solution)/shard_map/ppermute | solution.py:16
  73.9 8.3 %collective-permute-start.7 = (bf16[256,512]{1,0:T(8,128)(2,1)S(1)}, bf16[256,512]{1,0:T(8,128)(2,1)S(1)}, u32[]{:S(2)}, u32[]{:S(2)}) collective-permute-start(bf16[256,512]{1,0:T(8,128)(2,1)S(1)} %fusion.23), channel_id=1, source_target_pairs={{0,8},{8,0},{16,24},{24,16},{1,9},{9,1},{17,25},{25,17},{2,10},{10... | collective-permute-start | bytes 786440 | tf_op jit(solution)/shard_map/ppermute | solution.py:16
  80.6 3.1 %collective-permute-start.11 = (bf16[4,128,512]{2,1,0:T(8,128)(2,1)}, bf16[4,128,512]{2,1,0:T(8,128)(2,1)}, u32[]{:S(2)}, u32[]{:S(2)}) collective-permute-start(bf16[4,128,512]{2,1,0:T(8,128)(2,1)} %convolution_convert_fusion.1), channel_id=1, source_target_pairs={{0,1},{1,0},{2,3},{3,2},{4,5},{5,4},{6,7},{7,6},{8,9},{9,8},{10,11... | collective-permute-start | bytes 1572872 | tf_op jit(solution)/shard_map/ppermute | solution.py:16
  82.4 7.0 %copy-start.1 = (bf16[512,512]{1,0:T(8,128)(2,1)}, bf16[512,512]{1,0:T(8,128)(2,1)S(1)}, u32[]{:S(2)}) copy-start(bf16[512,512]{1,0:T(8,128)(2,1)S(1)} %fusion.1) | copy-start | bytes 1572868
  83.7 5.8 %collective-permute-start.19 = (bf16[4,128,512]{2,1,0:T(8,128)(2,1)}, bf16[4,128,512]{2,1,0:T(8,128)(2,1)}, u32[]{:S(2)}, u32[]{:S(2)}) collective-permute-start(bf16[4,128,512]{2,1,0:T(8,128)(2,1)} %convolution_convert_fusion), channel_id=1, source_target_pairs={{0,1},{1,0},{2,3},{3,2},{4,5},{5,4},{6,7},{7,6},{8,9},{9,8},{10,11... | collective-permute-start | bytes 1572872 | tf_op jit(solution)/shard_map/ppermute | solution.py:16
  85.2 11.8 %copy-start.13 = (bf16[1024]{0:T(1024)(128)(2,1)S(1)}, bf16[1024]{0:T(1024)(128)(2,1)}, u32[]{:S(2)}) copy-start(bf16[1024]{0:T(1024)(128)(2,1)} %param.13) | copy-start | bytes 6148
  85.2 27.8 %copy-start.11 = (bf16[128,1024]{1,0:T(8,128)(2,1)S(1)}, bf16[128,1024]{1,0:T(8,128)(2,1)}, u32[]{:S(2)}) copy-start(bf16[128,1024]{1,0:T(8,128)(2,1)} %param.12) | copy-start | bytes 786436
  85.3 11.1 %collective-permute-start.12 = (bf16[128,512]{1,0:T(8,128)(2,1)S(1)}, bf16[128,512]{1,0:T(8,128)(2,1)S(1)}, u32[]{:S(2)}, u32[]{:S(2)}) collective-permute-start(bf16[128,512]{1,0:T(8,128)(2,1)S(1)} %get-tuple-element.33), channel_id=1, source_target_pairs={{0,2},{1,3},{2,0},{3,1},{4,6},{5,7},{6,4},{7,5},{8,10},{9,11},{10,... | collective-permute-start | bytes 393224 | tf_op jit(solution)/shard_map/ppermute | solution.py:16
  87.0 10.1 %collective-permute-start.14 = (bf16[128,512]{1,0:T(8,128)(2,1)S(1)}, bf16[128,512]{1,0:T(8,128)(2,1)}, u32[]{:S(2)}, u32[]{:S(2)}) collective-permute-start(bf16[128,512]{1,0:T(8,128)(2,1)S(1)} %get-tuple-element.34), channel_id=1, source_target_pairs={{0,6},{1,7},{2,4},{3,5},{4,2},{5,3},{6,0},{7,1},{8,14},{9,15},{10,... | collective-permute-start | bytes 393224 | tf_op jit(solution)/shard_map/ppermute | solution.py:16
  89.4 18.5 %collective-permute-start.13 = (bf16[128,512]{1,0:T(8,128)(2,1)S(1)}, bf16[128,512]{1,0:T(8,128)(2,1)}, u32[]{:S(2)}, u32[]{:S(2)}) collective-permute-start(bf16[128,512]{1,0:T(8,128)(2,1)S(1)} %get-tuple-element.35), channel_id=1, source_target_pairs={{0,4},{1,5},{2,6},{3,7},{4,0},{5,1},{6,2},{7,3},{8,12},{9,13},{10,... | collective-permute-start | bytes 393224 | tf_op jit(solution)/shard_map/ppermute | solution.py:16
  90.9 1.0 copy-start.2
  91.9 15.9 %collective-permute-start.20 = (bf16[128,512]{1,0:T(8,128)(2,1)S(1)}, bf16[128,512]{1,0:T(8,128)(2,1)S(1)}, u32[]{:S(2)}, u32[]{:S(2)}) collective-permute-start(bf16[128,512]{1,0:T(8,128)(2,1)S(1)} %get-tuple-element.30), channel_id=1, source_target_pairs={{0,2},{1,3},{2,0},{3,1},{4,6},{5,7},{6,4},{7,5},{8,10},{9,11},{10,... | collective-permute-start | bytes 393224 | tf_op jit(solution)/shard_map/ppermute | solution.py:16
  94.0 13.9 %collective-permute-start.22 = (bf16[128,512]{1,0:T(8,128)(2,1)S(1)}, bf16[128,512]{1,0:T(8,128)(2,1)S(1)}, u32[]{:S(2)}, u32[]{:S(2)}) collective-permute-start(bf16[128,512]{1,0:T(8,128)(2,1)S(1)} %get-tuple-element.31), channel_id=1, source_target_pairs={{0,6},{1,7},{2,4},{3,5},{4,2},{5,3},{6,0},{7,1},{8,14},{9,15},{10,... | collective-permute-start | bytes 393224 | tf_op jit(solution)/shard_map/ppermute | solution.py:16
  96.3 0.7 copy-start.12
  96.3 16.6 %collective-permute-start.21 = (bf16[128,512]{1,0:T(8,128)(2,1)S(1)}, bf16[128,512]{1,0:T(8,128)(2,1)S(1)}, u32[]{:S(2)}, u32[]{:S(2)}) collective-permute-start(bf16[128,512]{1,0:T(8,128)(2,1)S(1)} %get-tuple-element.32), channel_id=1, source_target_pairs={{0,4},{1,5},{2,6},{3,7},{4,0},{5,1},{6,2},{7,3},{8,12},{9,13},{10,... | collective-permute-start | bytes 393224 | tf_op jit(solution)/shard_map/ppermute | solution.py:16
  114.3 8.3 %collective-permute-start.17 = (bf16[128,512]{1,0:T(8,128)(2,1)S(1)}, bf16[128,512]{1,0:T(8,128)(2,1)S(1)}, u32[]{:S(2)}, u32[]{:S(2)}) collective-permute-start(bf16[128,512]{1,0:T(8,128)(2,1)S(1)} %get-tuple-element.47.refs_0_), channel_id=1, source_target_pairs={{0,6},{1,7},{2,4},{3,5},{4,2},{5,3},{6,0},{7,1},{8,14},{9,15},{10,... | collective-permute-start | bytes 393224 | tf_op jit(solution)/shard_map/ppermute | solution.py:16
  117.0 10.0 %collective-permute-start.16 = (bf16[128,512]{1,0:T(8,128)(2,1)S(1)}, bf16[128,512]{1,0:T(8,128)(2,1)S(1)}, u32[]{:S(2)}, u32[]{:S(2)}) collective-permute-start(bf16[128,512]{1,0:T(8,128)(2,1)S(1)} %get-tuple-element.47.refs_0_), channel_id=1, source_target_pairs={{0,4},{1,5},{2,6},{3,7},{4,0},{5,1},{6,2},{7,3},{8,12},{9,13},{10,... | collective-permute-start | bytes 393224 | tf_op jit(solution)/shard_map/ppermute | solution.py:16
  117.0 10.0 %collective-permute-start.15 = (bf16[128,512]{1,0:T(8,128)(2,1)S(1)}, bf16[128,512]{1,0:T(8,128)(2,1)S(1)}, u32[]{:S(2)}, u32[]{:S(2)}) collective-permute-start(bf16[128,512]{1,0:T(8,128)(2,1)S(1)} %get-tuple-element.47.refs_0_), channel_id=1, source_target_pairs={{0,2},{1,3},{2,0},{3,1},{4,6},{5,7},{6,4},{7,5},{8,10},{9,11},{10,... | collective-permute-start | bytes 393224 | tf_op jit(solution)/shard_map/ppermute | solution.py:16
  129.2 23.4 %all-to-all-start.2 = ((bf16[4,384,512]{2,1,0:T(8,128)(2,1)}), bf16[4,384,512]{2,1,0:T(8,128)(2,1)S(1)}, u32[]{:S(2)}, u32[]{:S(2)}) async-start(bf16[4,384,512]{2,1,0:T(8,128)(2,1)} %bitcast.41), calls=%async_computation.2 | async-start | bytes 3145728 | tf_op jit(solution)/shard_map/all_to_all | solution.py:335
  132.8 8.3 %collective-permute-start.25 = (bf16[128,512]{1,0:T(8,128)(2,1)S(1)}, bf16[128,512]{1,0:T(8,128)(2,1)S(1)}, u32[]{:S(2)}, u32[]{:S(2)}) collective-permute-start(bf16[128,512]{1,0:T(8,128)(2,1)S(1)} %get-tuple-element.46.refs_0_), channel_id=1, source_target_pairs={{0,6},{1,7},{2,4},{3,5},{4,2},{5,3},{6,0},{7,1},{8,14},{9,15},{10,... | collective-permute-start | bytes 393224 | tf_op jit(solution)/shard_map/ppermute | solution.py:16
  135.1 11.1 %collective-permute-start.24 = (bf16[128,512]{1,0:T(8,128)(2,1)S(1)}, bf16[128,512]{1,0:T(8,128)(2,1)S(1)}, u32[]{:S(2)}, u32[]{:S(2)}) collective-permute-start(bf16[128,512]{1,0:T(8,128)(2,1)S(1)} %get-tuple-element.46.refs_0_), channel_id=1, source_target_pairs={{0,4},{1,5},{2,6},{3,7},{4,0},{5,1},{6,2},{7,3},{8,12},{9,13},{10,... | collective-permute-start | bytes 393224 | tf_op jit(solution)/shard_map/ppermute | solution.py:16
  135.1 11.1 %collective-permute-start.23 = (bf16[128,512]{1,0:T(8,128)(2,1)S(1)}, bf16[128,512]{1,0:T(8,128)(2,1)S(1)}, u32[]{:S(2)}, u32[]{:S(2)}) collective-permute-start(bf16[128,512]{1,0:T(8,128)(2,1)S(1)} %get-tuple-element.46.refs_0_), channel_id=1, source_target_pairs={{0,2},{1,3},{2,0},{3,1},{4,6},{5,7},{6,4},{7,5},{8,10},{9,11},{10,... | collective-permute-start | bytes 393224 | tf_op jit(solution)/shard_map/ppermute | solution.py:16
  152.6 23.4 %all-to-all-start.3 = ((bf16[4,384,512]{2,1,0:T(8,128)(2,1)}), bf16[4,384,512]{2,1,0:T(8,128)(2,1)}, u32[]{:S(2)}, u32[]{:S(2)}) async-start(bf16[4,384,512]{2,1,0:T(8,128)(2,1)} %bitcast.47), calls=%async_computation.3 | async-start | bytes 3145728 | tf_op jit(solution)/shard_map/all_to_all | solution.py:335
  157.1 22.9 %collective-permute-start.18 = (bf16[4,384,512]{2,1,0:T(8,128)(2,1)S(1)}, bf16[4,384,512]{2,1,0:T(8,128)(2,1)S(1)}, u32[]{:S(2)}, u32[]{:S(2)}) collective-permute-start(bf16[4,384,512]{2,1,0:T(8,128)(2,1)S(1)} %all-to-all-done.2.own_ref.own0_ref), channel_id=1, source_target_pairs={{0,1},{1,0},{2,3},{3,2},{4,5},{5,4},{6,7},{7,6},{8,9},{9,8},{10,11... | collective-permute-start | bytes 4718600 | tf_op jit(solution)/shard_map/ppermute | solution.py:16
  176.0 16.0 %collective-permute-start.26 = (bf16[4,384,512]{2,1,0:T(8,128)(2,1)}, bf16[4,384,512]{2,1,0:T(8,128)(2,1)S(1)}, u32[]{:S(2)}, u32[]{:S(2)}) collective-permute-start(bf16[4,384,512]{2,1,0:T(8,128)(2,1)} %all-to-all-done.3.own1_ref), channel_id=1, source_target_pairs={{0,1},{1,0},{2,3},{3,2},{4,5},{5,4},{6,7},{7,6},{8,9},{9,8},{10,11... | collective-permute-start | bytes 4718600 | tf_op jit(solution)/shard_map/ppermute | solution.py:16
  192.0 1.2 copy-start.9

commit v3 on v2

v3 whole, which is shorter than its diff:
```python
import functools

import jax
import jax.numpy as jnp
from jax import lax
from jax.experimental import pallas as pl
from jax.experimental.pallas import tpu as pltpu
from jax.sharding import PartitionSpec as P

CHUNKS = 2
VMEM_LIMIT = 50 * 1024 * 1024


def exchange(value, axis, offset):
    size = lax.axis_size(axis)
    return lax.ppermute(value, axis, [(i, i ^ offset) for i in range(size)])


def pick(value, index, axis):
    return lax.dynamic_index_in_dim(value, index, axis, keepdims=False)


def bits_of(size):
    return size.bit_length() - 1


def whole(shape):
    return pl.BlockSpec(shape, lambda *_: (0,) * len(shape))


def smem():
    return pl.BlockSpec(memory_space=pltpu.SMEM)


def params():
    return pltpu.CompilerParams(vmem_limit_bytes=VMEM_LIMIT)


def signs_kernel(experts, position_ref, ids_ref, out_ref):
    blocks, capacity, lanes = out_ref.shape
    tokens = ids_ref.shape[2]
    expert = position_ref[0]
    slots = lax.broadcasted_iota(jnp.int32, (capacity, tokens), 0)
    rows = lax.broadcasted_iota(jnp.int32, (lanes, tokens), 0)
    last = lax.broadcasted_iota(jnp.int32, (capacity, lanes), 1) == lanes - 1
    for b in range(blocks):
        ids = ids_ref[b]
        e0, e1, s0, s1 = ids[0:1], ids[1:2], ids[2:3], ids[3:4]
        hit0 = jnp.where((e0 == expert) & (s0 == slots), 1.0, 0.0)
        hit1 = jnp.where((e1 == expert) & (s1 == slots), 1.0, 0.0)
        table = jnp.where(e0 == rows - 1, 1.0, 0.0) - jnp.where(e1 == rows - 1, 1.0, 0.0)
        signs = lax.dot_general(
            (hit0 - hit1).astype(jnp.bfloat16),
            table.astype(jnp.bfloat16),
            (((1,), (1,)), ((), ())),
            preferred_element_type=jnp.float32,
        )
        filled = jnp.sum(hit0 + hit1, axis=1, keepdims=True)
        out_ref[b] = jnp.where(last, filled, signs)


def pack_kernel(position_ref, low_ref, high_ref, low_out, high_out):
    low_out[0] = low_ref[...]
    high_out[0] = high_ref[...]


def pack(position, branch, c, experts):
    half = branch.shape[0] // 2
    part = branch.shape[1] // experts // CHUNKS
    others = experts // 2

    def low(j, position_ref):
        return (0, (2 * j + 1 - position_ref[0] % 2) * CHUNKS + c)

    def high(j, position_ref):
        return (1, (j + others * (1 - position_ref[0] // others)) * CHUNKS + c)

    block = pl.BlockSpec((1, half, part), lambda j, position_ref: (j, 0, 0))
    shape = jax.ShapeDtypeStruct((others, half, part), jnp.bfloat16)
    return pl.pallas_call(
        pack_kernel,
        out_shape=(shape, shape),
        grid_spec=pltpu.PrefetchScalarGridSpec(
            num_scalar_prefetch=1,
            grid=(others,),
            in_specs=[pl.BlockSpec((half, part), low), pl.BlockSpec((half, part), high)],
            out_specs=(block, block),
        ),
        compiler_params=params(),
        name="pack",
    )(position, branch, branch)


def spread_kernel(shares_ref, ids_ref, out_ref):
    experts, quarter, columns = shares_ref.shape
    blocks, _, features = out_ref.shape
    per_expert = blocks // experts
    for f in range(blocks):
        start = (f % per_expert) * features
        out_ref[f, :quarter] = shares_ref[f // per_expert, :, start : start + features]
        out_ref[f, quarter:] = ids_ref[...]


def sides_kernel(position_ref, *refs):
    *share_refs, own_ref, other_ref = refs
    quarter = own_ref.shape[2]
    for k, share_ref in enumerate(share_refs):
        place = position_ref[0] ^ k
        for side, out_ref in enumerate((own_ref, other_ref)):
            out_ref[:, place] = share_ref[:, position_ref[2] ^ side, :quarter]


def dispatch_kernel(position_ref, ids_ref, extra_ref, *refs):
    *token_refs, out_ref = refs
    planes = len(token_refs)
    experts, _, part = out_ref.shape
    lanes = extra_ref.shape[0]
    count = out_ref.shape[1] - lanes
    capacity = count // planes
    tokens = ids_ref.shape[2]
    plane, core = position_ref[1], position_ref[2]
    slots = lax.broadcasted_iota(jnp.int32, (experts * capacity, tokens), 0)
    for k in range(planes):
        source = plane ^ k
        ids = ids_ref[source * 2 + core]
        code0 = ids[0:1] * capacity + ids[2:3]
        code1 = ids[1:2] * capacity + ids[3:4]
        one_hot = jnp.where((code0 == slots) | (code1 == slots), 1.0, 0.0).astype(jnp.bfloat16)
        picked = jnp.dot(one_hot, token_refs[k][...], preferred_element_type=jnp.float32)
        rows = pl.ds(pl.multiple_of(source * capacity, 16), capacity)
        out_ref[:, rows] = picked.reshape(experts, capacity, part).astype(jnp.bfloat16)
    for e in range(experts):
        out_ref[e, count:] = extra_ref[...]


def row_stats(rows_ref, aux_ref, count):
    experts, height, part = rows_ref.shape
    squares = jnp.zeros((count, part), jnp.float32)
    logits = jnp.zeros((count, height - count), jnp.float32)
    for e in range(experts):
        rows, aux = rows_ref[e, :count], aux_ref[e, count:]
        ratio = rows.astype(jnp.float32) * (1.0 / aux[0:1].astype(jnp.float32))
        squares = squares + ratio * ratio
        logits = logits + lax.dot_general(
            rows, aux, (((1,), (1,)), ((), ())), preferred_element_type=jnp.float32
        )
    total = jnp.sum(squares, axis=1, keepdims=True)
    return jnp.where(lax.broadcasted_iota(jnp.int32, logits.shape, 1) == 0, total, logits)


def lay_flat(sides, flat_ref):
    count = flat_ref.shape[0] // 2
    part = sides[0].shape[2]
    for side, rows_ref in enumerate(sides):
        for e in range(rows_ref.shape[0]):
            flat_ref[side * count : (side + 1) * count, e * part : (e + 1) * part] = rows_ref[
                e, :count
            ]


def turn(sides, e, out_ref, at):
    count = out_ref.shape[2] // 2
    for side, rows_ref in enumerate(sides):
        out_ref[at, :, side * count : (side + 1) * count] = rows_ref[e, :count].T


def product(flat_ref, weight_ref):
    weight = weight_ref[...].reshape(flat_ref.shape[1], weight_ref.shape[3])
    return jnp.dot(flat_ref[...], weight, preferred_element_type=jnp.float32)


def early_kernel(
    own_ref, other_ref, gate_ref, up_ref, gate_out, up_out, stats_out, turned_out, flat_scratch
):
    count = flat_scratch.shape[0] // 2
    sides = (own_ref, other_ref)

    @pl.when(pl.program_id(0) == 0)
    def _():
        lay_flat(sides, flat_scratch)
        for side, rows_ref in enumerate(sides):
            stats_out[side * count : (side + 1) * count] = row_stats(rows_ref, own_ref, count)

    gate_out[...] = product(flat_scratch, gate_ref)
    up_out[...] = product(flat_scratch, up_ref)
    per_step = turned_out.shape[0]
    first = jnp.minimum(pl.program_id(0) * per_step, own_ref.shape[0] - per_step)
    for j in range(per_step):
        turn(sides, first + j, turned_out, j)


def late_kernel(
    width,
    tiles,
    position_ref,
    own_ref,
    other_ref,
    turned_ref,
    gate_ref,
    up_ref,
    gate_acc,
    up_acc,
    stats_ref,
    signs_ref,
    cot_ref,
    hidden_out,
    grad_gate_out,
    grad_up_out,
    flat_scratch,
    scale_scratch,
    weight_scratch,
    d_gate_scratch,
    d_up_scratch,
    turned_scratch,
):
    step = pl.program_id(0)
    core = position_ref[2]
    planes, _, capacity, tile = hidden_out.shape
    count = planes * capacity
    experts = own_ref.shape[0]
    lanes = stats_ref.shape[1]
    sides = (own_ref, other_ref)
    per_step = max(1, experts // tiles)

    @pl.when(step == 0)
    def _():
        lay_flat(sides, flat_scratch)
        for side, rows_ref in enumerate(sides):
            span = slice(side * count, (side + 1) * count)
            stats = stats_ref[span] + row_stats(rows_ref, own_ref, count)
            inverse = lax.rsqrt(stats[:, 0:1] / width + 1e-05)
            signs = signs_ref[:, pl.ds(core ^ side, 1)].reshape(count, lanes)
            filled = signs[:, lanes - 1 :]
            column = lax.broadcasted_iota(jnp.int32, stats.shape, 1)
            router = (column >= 1) & (column <= experts)
            margin = jnp.sum(jnp.where(router, stats * signs, 0.0), axis=1, keepdims=True)
            prob = jax.nn.sigmoid(margin * inverse).astype(jnp.bfloat16).astype(jnp.float32)
            scale_scratch[span] = inverse
            weight_scratch[span] = jnp.where(filled > 0.0, prob, 0.0)

    @pl.when(step < tiles)
    def _():
        start = pl.multiple_of(step * tile, tile)
        gate_all = gate_acc[...] + product(flat_scratch, gate_ref)
        up_all = up_acc[...] + product(flat_scratch, up_ref)
        first = jnp.minimum(step * per_step, experts - per_step)
        for j in range(per_step):
            turn(sides, first + j, turned_scratch, first + j)
        for side in range(2):
            span = slice(side * count, (side + 1) * count)
            inverse = scale_scratch[span]
            weight = weight_scratch[span]
            gate_pre = inverse * gate_all[span]
            up_pre = inverse * up_all[span]
            sig_gate = jax.nn.sigmoid(gate_pre)
            act_gate = gate_pre * sig_gate
            hidden = (weight * act_gate * up_pre).astype(jnp.bfloat16)
            hidden_out[:, pl.ds(core ^ side, 1)] = hidden.reshape(planes, 1, capacity, tile)
            cot = cot_ref[:, pl.ds(core ^ side, 1)].reshape(count, tile)
            d_pre = cot.astype(jnp.float32) * (weight * inverse)
            d_gate = d_pre * up_pre * sig_gate * (1.0 + gate_pre * (1.0 - sig_gate))
            d_gate_scratch[span, pl.ds(start, tile)] = d_gate.astype(jnp.bfloat16)
            d_up_scratch[span, pl.ds(start, tile)] = (d_pre * act_gate).astype(jnp.bfloat16)

    def gradients(turned):
        for t in range(tiles):
            span = slice(t * tile, (t + 1) * tile)
            for scratch, out in ((d_gate_scratch, grad_gate_out), (d_up_scratch, grad_up_out)):
                out[0, 0, :, span] = jnp.dot(
                    turned, scratch[:, span], preferred_element_type=jnp.float32
                ).astype(jnp.bfloat16)

    @pl.when((step >= tiles) & ((step - tiles) % 2 == 0))
    def _():
        gradients(turned_ref[0])

    @pl.when((step >= tiles) & ((step - tiles) % 2 == 1))
    def _():
        gradients(turned_scratch[(step - tiles) // 2])


def per_device(
    branch_wo,
    context,
    residual,
    norm_gain,
    router_w,
    gate_w,
    up_w,
    expert_ids,
    slot_ids,
    cot_hidden,
):
    experts = lax.axis_size("expert")
    blocks = lax.axis_size("fsdp")
    planes = blocks // 2
    expert = lax.axis_index("expert")
    block = lax.axis_index("fsdp")
    plane, core = block // 2, block % 2
    tokens, columns = context.shape
    width = columns * experts
    features = width // blocks
    capacity = cot_hidden.shape[1] // blocks
    units = cot_hidden.shape[2]
    part = columns // CHUNKS
    quarter = tokens // experts
    count = planes * capacity
    position = jnp.stack([expert, plane, core]).astype(jnp.int32)
    bits = bits_of(experts)

    lanes = experts + 2 + (-(experts + 2)) % 16
    extra = jnp.concatenate([norm_gain[None], router_w.T])
    extra = jnp.pad(extra, ((0, lanes - extra.shape[0]), (0, 0)))
    ids = jnp.concatenate([expert_ids, slot_ids], axis=1).T.astype(jnp.bfloat16)
    id_rows = ids.size // features
    ids = jnp.pad(ids.reshape(id_rows, features), ((0, -id_rows % 16), (0, 0)))

    shares = lax.all_to_all(
        context.reshape(experts, quarter, columns), "expert", split_axis=0, concat_axis=0, tiled=True
    )
    spread_shape = (blocks, quarter + ids.shape[0], features)
    to_blocks = pl.pallas_call(
        spread_kernel,
        out_shape=jax.ShapeDtypeStruct(spread_shape, jnp.bfloat16),
        in_specs=[whole(shares.shape), whole(ids.shape)],
        out_specs=whole(spread_shape),
        grid=(1,),
        compiler_params=params(),
        name="spread",
    )(shares, ids)
    from_blocks = lax.all_to_all(to_blocks, "fsdp", split_axis=0, concat_axis=0, tiled=True)
    ids_all = from_blocks[:, quarter : quarter + id_rows].astype(jnp.int32)
    ids_all = ids_all.reshape(blocks, 4, tokens)
    pieces = [
        (exchange(from_blocks, "expert", k) if k else from_blocks).reshape(
            planes, 2, spread_shape[1], features
        )
        for k in range(experts)
    ]
    side_shape = (planes, experts, quarter, features)
    sides = pl.pallas_call(
        sides_kernel,
        out_shape=(jax.ShapeDtypeStruct(side_shape, jnp.bfloat16),) * 2,
        in_specs=[smem()] + [whole(piece.shape) for piece in pieces],
        out_specs=(whole(side_shape),) * 2,
        grid=(1,),
        compiler_params=params(),
        name="sides",
    )(position, *pieces)
    sides = [side.reshape(planes * tokens, features) for side in sides]

    signs = pl.pallas_call(
        functools.partial(signs_kernel, experts),
        out_shape=jax.ShapeDtypeStruct((blocks, capacity, lanes), jnp.float32),
        in_specs=[smem(), whole(ids_all.shape)],
        out_specs=whole((blocks, capacity, lanes)),
        grid=(1,),
        compiler_params=params(),
        name="signs",
    )(position, ids_all).reshape(planes, 2, capacity, lanes)

    branch = branch_wo[0]
    half = branch.shape[0] // 2
    weights = [1 << (bits - 1 - i) for i in range(bits)]
    own_bits = [(expert // weight) % 2 for weight in weights]

    def start_sum(c, h):
        def value(chosen):
            place = sum(weight * bit for weight, bit in zip(weights, chosen))
            corner = (h * half, (place * CHUNKS + c) * part)
            return lax.dynamic_slice(branch, corner, (half, part)).astype(jnp.float32)

        return value

    def joined(value, got, axis, rest):
        def total(chosen):
            chosen = [own_bits[axis] if i == axis else bit for i, bit in enumerate(chosen)]
            place = 0
            for i in rest:
                place = 2 * place + chosen[i]
            return value(chosen) + pick(got, place, 0).astype(jnp.float32)

        return total

    held = {(c, h): start_sum(c, h) for c in range(CHUNKS) for h in range(2)}
    orders = (list(range(bits))[::-1], list(range(bits)))
    for phase in range(bits):
        before = None
        for c in range(CHUNKS):
            if phase == 0:
                sends = list(pack(position, branch, c, experts))
            else:
                sends = []
                for h, order in enumerate(orders):
                    rest = sorted(order[phase + 1 :])
                    stacked = []
                    for code in range(1 << len(rest)):
                        chosen = [own_bits[i] for i in range(bits)]
                        chosen[order[phase]] = 1 - own_bits[order[phase]]
                        for at, i in enumerate(rest):
                            chosen[i] = (code >> (len(rest) - 1 - at)) & 1
                        stacked.append(held[c, h](chosen).astype(jnp.bfloat16))
                    sends.append(stacked[0][None] if len(stacked) == 1 else jnp.stack(stacked))
            if before is not None:
                sends, before = lax.optimization_barrier((sends, before))
            got = [
                exchange(sends[h], "expert", weights[order[phase]])
                for h, order in enumerate(orders)
            ]
            before = got
            for h, order in enumerate(orders):
                held[c, h] = joined(held[c, h], got[h], order[phase], sorted(order[phase + 1 :]))
    held = {key: value(own_bits) for key, value in held.items()}

    gate_view = gate_w.reshape(experts, CHUNKS, part, units)
    up_view = up_w.reshape(experts, CHUNKS, part, units)
    tile = min(256, units)
    tiles = units // tile
    merged_parts = []
    partial = None
    for c in range(CHUNKS):
        span = slice(c * part, (c + 1) * part)
        merged = jnp.concatenate([held[c, 0], held[c, 1]]) / experts
        merged = merged.astype(jnp.bfloat16)
        merged_parts.append(merged)

        def attend(rows):
            out = jnp.dot(rows, merged, preferred_element_type=jnp.float32)
            return out.reshape(planes, tokens, part)

        swapped = exchange(attend(sides[1]).astype(jnp.bfloat16), "fsdp", 1)
        pair = attend(sides[0]) + swapped.astype(jnp.float32)
        hstate = residual[:, span].astype(jnp.float32) + pick(pair, plane, 0)
        for k in range(1, planes):
            arrived = exchange(pick(pair, plane ^ k, 0).astype(jnp.bfloat16), "fsdp", 2 * k)
            hstate = hstate + arrived.astype(jnp.float32)
        scaled = (hstate * norm_gain[span].astype(jnp.float32)).astype(jnp.bfloat16)
        own_tokens = [exchange(scaled, "fsdp", 2 * k) if k else scaled for k in range(planes)]

        height = count + lanes
        slots = pl.pallas_call(
            dispatch_kernel,
            out_shape=jax.ShapeDtypeStruct((experts, height, part), jnp.bfloat16),
            in_specs=[smem(), whole(ids_all.shape)]
            + [pl.BlockSpec((lanes, part), lambda i, c=c: (0, c))]
            + [whole((tokens, part))] * planes,
            out_specs=whole((experts, height, part)),
            grid=(1,),
            compiler_params=params(),
            name="dispatch",
        )(position, ids_all, extra, *own_tokens)
        rows = lax.all_to_all(slots, "expert", split_axis=0, concat_axis=0, tiled=True)
        if partial is not None:
            rows, partial = lax.optimization_barrier((rows, partial))
        other = exchange(rows, "fsdp", 1)

        if c == 0:
            weight_spec = pl.BlockSpec((experts, 1, part, tile), lambda n: (0, 0, 0, n))
            sums = jax.ShapeDtypeStruct((2 * count, units), jnp.float32)
            sum_spec = pl.BlockSpec((2 * count, tile), lambda n: (0, n))
            per_step = max(1, experts // tiles)
            partial = pl.pallas_call(
                early_kernel,
                out_shape=(
                    sums,
                    sums,
                    jax.ShapeDtypeStruct((2 * count, lanes), jnp.float32),
                    jax.ShapeDtypeStruct((experts, part, 2 * count), jnp.bfloat16),
                ),
                in_specs=[whole(rows.shape)] * 2 + [weight_spec, weight_spec],
                out_specs=(
                    sum_spec,
                    sum_spec,
                    whole((2 * count, lanes)),
                    pl.BlockSpec(
                        (per_step, part, 2 * count),
                        lambda n: (jnp.minimum(n, experts // per_step - 1), 0, 0),
                    ),
                ),
                grid=(tiles,),
                scratch_shapes=[pltpu.VMEM((2 * count, experts * part), jnp.bfloat16)],
                compiler_params=params(),
                cost_estimate=pl.CostEstimate(
                    flops=8 * count * experts * part * units,
                    bytes_accessed=4 * experts * part * units,
                    transcendentals=0,
                ),
                name="early",
            )(rows, other, gate_view, up_view)

    tile_of = lambda i: jnp.minimum(i, tiles - 1)
    place_of = lambda i: jnp.maximum(i - tiles, 0)
    weight_spec = pl.BlockSpec((experts, 1, part, tile), lambda i: (0, 1, 0, tile_of(i)))
    sum_spec = pl.BlockSpec((2 * count, tile), lambda i: (0, tile_of(i)))
    unit_spec = pl.BlockSpec((planes, 2, capacity, tile), lambda i: (0, 0, 0, tile_of(i)))
    grad_spec = pl.BlockSpec((1, 1, part, units), lambda i: (place_of(i) // 2, place_of(i) % 2, 0, 0))
    grad_shape = jax.ShapeDtypeStruct((experts, CHUNKS, part, units), jnp.bfloat16)
    gate_sums, up_sums, stats, turned = partial
    hidden, grad_gate, grad_up = pl.pallas_call(
        functools.partial(late_kernel, float(width), tiles),
        out_shape=(
            jax.ShapeDtypeStruct((planes, 2, capacity, units), jnp.bfloat16),
            grad_shape,
            grad_shape,
        ),
        in_specs=[smem(), whole(rows.shape), whole(rows.shape)]
        + [pl.BlockSpec((1, part, 2 * count), lambda i: (place_of(i) // 2, 0, 0))]
        + [weight_spec, weight_spec, sum_spec, sum_spec]
        + [whole(stats.shape), whole(signs.shape), unit_spec],
        out_specs=(unit_spec, grad_spec, grad_spec),
        grid=(tiles + experts * CHUNKS,),
        scratch_shapes=[
            pltpu.VMEM((2 * count, experts * part), jnp.bfloat16),
            pltpu.VMEM((2 * count, 1), jnp.float32),
            pltpu.VMEM((2 * count, 1), jnp.float32),
            pltpu.VMEM((2 * count, units), jnp.bfloat16),
            pltpu.VMEM((2 * count, units), jnp.bfloat16),
            pltpu.VMEM((experts, part, 2 * count), jnp.bfloat16),
        ],
        compiler_params=params(),
        name="late",
    )(
        position,
        rows,
        other,
        turned,
        gate_view,
        up_view,
        gate_sums,
        up_sums,
        stats,
        signs,
        cot_hidden.reshape(planes, 2, capacity, units),
    )
    return (
        jnp.concatenate(merged_parts, axis=1),
        hidden.reshape(1, -1, units),
        grad_gate.reshape(1, width, units),
        grad_up.reshape(1, width, units),
    )


def solution(mesh):
    placed = (
        P("expert", "fsdp", None),
        P("fsdp", "expert"),
        P("fsdp", "expert"),
        P("expert"),
        P("expert", None),
        P("expert", None, "fsdp"),
        P("expert", None, "fsdp"),
        P("fsdp", None),
        P("fsdp", None),
        P("expert", None, "fsdp"),
    )
    return jax.shard_map(
        per_device,
        mesh=mesh,
        in_specs=placed,
        out_specs=(
            P("fsdp", "expert"),
            P("expert", None, "fsdp"),
            P("expert", None, "fsdp"),
            P("expert", None, "fsdp"),
        ),
        check_vma=False,
    )
```

time: 227 us -> 223 us (0.982)
  local copies, waits for them, and re-layouts: 33 us -> 6.17 us
  blocking collectives: 0 us -> 23.8 us
  other arithmetic: 14.3 us -> 9.72 us
  starting transfers between devices: 48.6 us -> 44.9 us
  Pallas kernels: 49.7 us -> 53.3 us
  waiting for transfers between devices: 73.4 us -> 76.8 us
    all_to_all x0 -> x1, blocking collectives: none -> 23.8 us  [per_device(): lax.all_to_all(slots, 'expert', split_axis=0, concat_axis=0, tiled=True)]
    ppermute x27, waiting for transfers between devices: 50.5 us -> 70.8 us  [exchange(): return lax.ppermute(value, axis, [(i, i ^ offset) for i in range(size)])]
    all_to_all x3 -> x2, waiting for transfers between devices: 22.9 us -> 6.07 us  [the longest x1 6.07 us: per_device(): lax.all_to_all(slots, 'expert', split_axis=0, concat_axis=0, tiled=True)]
    unnamed x43 -> x33, local copies, waits for them, and re-layouts: 17.7 us -> 4.3 us
    slice x5 -> x0, local copies, waits for them, and re-layouts: 7.89 us -> none  [the longest x1 4.73 us: block_view(): branch[h * half:(h + 1) * half].reshape((half,) + (2,) * bits + (columns,))]
    all_to_all x3 -> x2, starting transfers between devices: 13.3 us -> 7.16 us  [the longest x1 3.75 us: per_device(): lax.all_to_all(slots, 'expert', split_axis=0, concat_axis=0, tiled=True)]
    pallas_call x0 -> x4, Pallas kernels: none -> 5.05 us  [the longest x2 3.66 us: pack(): pl.pallas_call(pack_kernel, out_shape=(shape, shape), grid_spec=pltpu.Pre...]
    dynamic_slice x2 -> x0, local copies, waits for them, and re-layouts: 4.76 us -> none  [pick(): return lax.dynamic_index_in_dim(value, index, axis, keepdims=False)]
  transfers between devices with their start and end apart: 31 -> 30, of which waited for: 13 -> 18; matrix products, arithmetic and copies ran while one was open for 20% -> 6% of each run, Pallas kernels for 7% -> 9%
where the time goes in v3:
time: 223 us; the launch traced here: 222 us
  waiting for transfers between devices  76.8 us (34%)
  Pallas kernels  53.3 us (24%)
  starting transfers between devices  44.9 us (20%)
  blocking collectives  23.8 us (11%)
  other arithmetic  9.72 us (4%)
  matrix products  6.45 us (3%)
  local copies, waits for them, and re-layouts  6.17 us (3%)
    ppermute x27, waiting for transfers between devices, exchange(): return lax.ppermute(value, axis, [(i, i ^ offset) for i in range(size)])  70.8 us
    ppermute x27, starting transfers between devices, exchange(): return lax.ppermute(value, axis, [(i, i ^ offset) for i in range(size)])  32.9 us
    pallas_call x1, Pallas kernels, per_device(): pl.pallas_call(functools.partial(late_kernel, float(width), tiles), out_s...  30.7 us
    all_to_all x1, blocking collectives, per_device(): lax.all_to_all(slots, 'expert', split_axis=0, concat_axis=0, tiled=True)  23.8 us
    pallas_call x1, Pallas kernels, per_device(): pl.pallas_call(early_kernel, out_shape=(sums, sums, jax.ShapeDtypeStruct(...  13.4 us
    dot_general x4, matrix products, attend(): out = jnp.dot(rows, merged, preferred_element_type=jnp.float32)  6.45 us
    all_to_all x1, waiting for transfers between devices, per_device(): lax.all_to_all(slots, 'expert', split_axis=0, concat_axis=0, tiled=True)  6.07 us
    all_to_all x1, starting transfers between devices, per_device(): lax.all_to_all(to_blocks, 'fsdp', split_axis=0, concat_axis=0, tiled=True)  4.88 us
  transfers between devices with their start and end apart: 30, of which 18 were waited for; matrix products, arithmetic and copies ran while one was open for 6% of the time, Pallas kernels for 9%

profile of v3, /device:TPU:0, one launch (start us, length us, event | category | flops | bytes accessed | tf_op | source)
XLA Modules:
  0.0 222.1 jit_solution(8728921269721281051)
XLA Ops:
  0.7 1.8 pack.2
  2.6 3.0 %collective-permute-start = (bf16[2,256,512]{2,1,0:T(8,128)(2,1)S(1)}, bf16[2,256,512]{2,1,0:T(8,128)(2,1)}, u32[]{:S(2)}, u32[]{:S(2)}) collective-permute-start(bf16[2,256,512]{2,1,0:T(8,128)(2,1)S(1)} %get-tuple-element.26), channel_id=1, source_target_pairs={{0,8},{8,0},{16,24},{24,16},{1,9},{9,1},{17,25},{25,17},{2,10},{10... | collective-permute-start | bytes 1572872 | tf_op jit(solution)/shard_map/ppermute | solution.py:16
  5.6 1.5 collective-permute-start.2
  7.1 3.4 %all-to-all-start = ((bf16[4,32,1024]{2,1,0:T(8,128)(2,1)}), bf16[4,32,1024]{2,1,0:T(8,128)(2,1)S(1)}, u32[]{:S(2)}, u32[]{:S(2)}) async-start(bf16[4,32,1024]{2,1,0:T(8,128)(2,1)} %bitcast.8), calls=%async_computation | async-start | bytes 524288 | tf_op jit(solution)/shard_map/all_to_all | solution.py:318
  10.5 1.8 pack.3
  12.4 6.1 %collective-permute-done = bf16[2,256,512]{2,1,0:T(8,128)(2,1)} collective-permute-done((bf16[2,256,512]{2,1,0:T(8,128)(2,1)S(1)}, bf16[2,256,512]{2,1,0:T(8,128)(2,1)}, u32[]{:S(2)}, u32[]{:S(2)}) %collective-permute-start) | collective-permute-done | bytes 524320 | tf_op jit(solution)/shard_map/ppermute | solution.py:16
  18.4 2.7 %collective-permute-done.2 = bf16[2,256,512]{2,1,0:T(8,128)(2,1)S(1)} collective-permute-done((bf16[2,256,512]{2,1,0:T(8,128)(2,1)S(1)}, bf16[2,256,512]{2,1,0:T(8,128)(2,1)S(1)}, u32[]{:S(2)}, u32[]{:S(2)}) %collective-permute-start.2) | collective-permute-done | bytes 524320 | tf_op jit(solution)/shard_map/ppermute | solution.py:16
  21.2 1.4 collective-permute-start.5
  22.7 0.8 spread.1
  23.4 4.9 %all-to-all-start.1 = ((bf16[8,48,512]{2,1,0:T(8,128)(2,1)}), bf16[8,48,512]{2,1,0:T(8,128)(2,1)S(1)}, u32[]{:S(2)}, u32[]{:S(2)}) async-start(bf16[8,48,512]{2,1,0:T(8,128)(2,1)} %spread.1), calls=%async_computation.1 | async-start | bytes 786432 | tf_op jit(solution)/shard_map/all_to_all | solution.py:331
  28.3 1.1 add_convert_fusion.3
  29.4 1.4 collective-permute-start.1
  30.8 7.8 %collective-permute-done.1 = bf16[1,256,512]{2,1,0:T(8,128)(2,1)S(1)} collective-permute-done((bf16[1,256,512]{2,1,0:T(8,128)(2,1)S(1)}, bf16[1,256,512]{2,1,0:T(8,128)(2,1)S(1)}, u32[]{:S(2)}, u32[]{:S(2)}) %collective-permute-start.1) | collective-permute-done | bytes 262176 | tf_op jit(solution)/shard_map/ppermute | solution.py:16
  38.6 2.7 %add_bitcast_fusion.3 = (f32[256,512]{1,0:T(8,128)}, bf16[1,256,512]{2,1,0:T(8,128)(2,1)}, bf16[1,256,512]{2,1,0:T(8,128)(2,1)S(1)}, bf16[1,256,512]{2,1,0:T(8,128)(2,1)}) fusion(bf16[1,256,512]{2,1,0:T(8,128)(2,1)S(1)} %collective-permute-done.1, bf16[2,256,512]{2,1,0:T(8,128)(2,1)} %collective-permute-done, s32[]{:T(128)S(6)} %select_n.88, ...), kind=kLoop, calls=%fused_computation.19 | loop fusion | flops 2228224 | bytes 3670044 | tf_op jit(solution)/shard_map/add | solution.py:381
  41.3 1.6 collective-permute-start.3
  43.0 1.4 collective-permute-start.10
  44.3 0.5 collective-permute-start.9
  44.8 1.6 collective-permute-start.8
  46.5 4.1 %collective-permute-done.3 = bf16[1,256,512]{2,1,0:T(8,128)(2,1)S(1)} collective-permute-done((bf16[1,256,512]{2,1,0:T(8,128)(2,1)S(1)}, bf16[1,256,512]{2,1,0:T(8,128)(2,1)S(1)}, u32[]{:S(2)}, u32[]{:S(2)}) %collective-permute-start.3) | collective-permute-done | bytes 262176 | tf_op jit(solution)/shard_map/ppermute | solution.py:16
  50.5 1.6 collective-permute-start.6
  52.1 1.1 collective-permute-start.7
  53.2 6.8 %collective-permute-done.10 = bf16[8,48,512]{2,1,0:T(8,128)(2,1)S(1)} collective-permute-done((bf16[8,48,512]{2,1,0:T(8,128)(2,1)S(1)}, bf16[8,48,512]{2,1,0:T(8,128)(2,1)S(1)}, u32[]{:S(2)}, u32[]{:S(2)}) %collective-permute-start.10) | collective-permute-done | bytes 393248 | tf_op jit(solution)/shard_map/ppermute | solution.py:16
  60.0 4.8 %collective-permute-done.9 = bf16[8,48,512]{2,1,0:T(8,128)(2,1)S(1)} collective-permute-done((bf16[8,48,512]{2,1,0:T(8,128)(2,1)S(1)}, bf16[8,48,512]{2,1,0:T(8,128)(2,1)S(1)}, u32[]{:S(2)}, u32[]{:S(2)}) %collective-permute-start.9) | collective-permute-done | bytes 393248 | tf_op jit(solution)/shard_map/ppermute | solution.py:16
  64.8 2.6 %collective-permute-done.8 = bf16[8,48,512]{2,1,0:T(8,128)(2,1)S(1)} collective-permute-done((bf16[8,48,512]{2,1,0:T(8,128)(2,1)S(1)}, bf16[8,48,512]{2,1,0:T(8,128)(2,1)S(1)}, u32[]{:S(2)}, u32[]{:S(2)}) %collective-permute-start.8) | collective-permute-done | bytes 393248 | tf_op jit(solution)/shard_map/ppermute | solution.py:16
  67.4 0.6 sides.1
  68.4 0.7 copy-done.9
  69.1 2.9 %collective-permute-done.7 = bf16[1,256,512]{2,1,0:T(8,128)(2,1)} collective-permute-done((bf16[1,256,512]{2,1,0:T(8,128)(2,1)}, bf16[1,256,512]{2,1,0:T(8,128)(2,1)}, u32[]{:S(2)}, u32[]{:S(2)}) %collective-permute-start.7) | collective-permute-done | bytes 262176 | tf_op jit(solution)/shard_map/ppermute | solution.py:16
  71.9 1.8 add_bitcast_fusion.2
  73.9 1.2 convolution_convert_fusion
  75.3 1.2 convolution_convert_fusion.1
  76.5 0.5 collective-permute-start.11
  77.4 1.5 convolution_add_fusion
  78.9 0.7 fusion.19
  79.7 1.4 collective-permute-start.19
  81.1 2.6 %collective-permute-start.21 = (bf16[128,512]{1,0:T(8,128)(2,1)}, bf16[128,512]{1,0:T(8,128)(2,1)}, u32[]{:S(2)}, u32[]{:S(2)}) collective-permute-start(bf16[128,512]{1,0:T(8,128)(2,1)} %get-tuple-element.56), channel_id=1, source_target_pairs={{0,6},{1,7},{2,4},{3,5},{4,2},{5,3},{6,0},{7,1},{8,14},{9,15},{10,... | collective-permute-start | bytes 393224 | tf_op jit(solution)/shard_map/ppermute | solution.py:16
  83.7 2.4 %convolution_add_fusion.1 = f32[4,128,512]{2,1,0:T(8,128)} fusion(bf16[4,128,512]{2,1,0:T(8,128)(2,1)S(1)} %bitcast.86, bf16[4,128,512]{2,1,0:T(8,128)(2,1)} %collective-permute-done.11, bf16[512,512]{1,0:T(8,128)(2,1)S(1)} %fusion.1), kind=kOutput, calls=%fused_computation.1 | convolution fusion | flops 268959744 | bytes 2621440 | tf_op jit(solution)/shard_map/dot_general | solution.py:428
  86.1 1.2 fusion.16
  87.3 1.9 collective-permute-start.12
  89.2 2.6 %collective-permute-start.14 = (bf16[128,512]{1,0:T(8,128)(2,1)S(1)}, bf16[128,512]{1,0:T(8,128)(2,1)}, u32[]{:S(2)}, u32[]{:S(2)}) collective-permute-start(bf16[128,512]{1,0:T(8,128)(2,1)S(1)} %get-tuple-element.59), channel_id=1, source_target_pairs={{0,6},{1,7},{2,4},{3,5},{4,2},{5,3},{6,0},{7,1},{8,14},{9,15},{10,... | collective-permute-start | bytes 393224 | tf_op jit(solution)/shard_map/ppermute | solution.py:16
  91.8 0.6 copy-done.11
  92.5 9.9 %collective-permute-done.20 = bf16[128,512]{1,0:T(8,128)(2,1)} collective-permute-done((bf16[128,512]{1,0:T(8,128)(2,1)S(1)}, bf16[128,512]{1,0:T(8,128)(2,1)}, u32[]{:S(2)}, u32[]{:S(2)}) %collective-permute-start.20) | collective-permute-done | bytes 131104 | tf_op jit(solution)/shard_map/ppermute | solution.py:16
  102.4 4.8 %collective-permute-done.13 = bf16[128,512]{1,0:T(8,128)(2,1)} collective-permute-done((bf16[128,512]{1,0:T(8,128)(2,1)S(1)}, bf16[128,512]{1,0:T(8,128)(2,1)}, u32[]{:S(2)}, u32[]{:S(2)}) %collective-permute-start.13) | collective-permute-done | bytes 131104 | tf_op jit(solution)/shard_map/ppermute | solution.py:16
  107.2 1.4 fusion.10
  108.6 2.7 %collective-permute-start.24 = (bf16[128,512]{1,0:T(8,128)(2,1)S(1)}, bf16[128,512]{1,0:T(8,128)(2,1)S(1)}, u32[]{:S(2)}, u32[]{:S(2)}) collective-permute-start(bf16[128,512]{1,0:T(8,128)(2,1)S(1)} %get-tuple-element.61.refs_0_), channel_id=1, source_target_pairs={{0,6},{1,7},{2,4},{3,5},{4,2},{5,3},{6,0},{7,1},{8,14},{9,15},{10,... | collective-permute-start | bytes 393224 | tf_op jit(solution)/shard_map/ppermute | solution.py:16
  111.3 1.7 collective-permute-start.22
  113.1 3.8 %collective-permute-done.24.refs_3_ = bf16[128,512]{1,0:T(8,128)(2,1)S(1)} collective-permute-done((bf16[128,512]{1,0:T(8,128)(2,1)S(1)}, bf16[128,512]{1,0:T(8,128)(2,1)S(1)}, u32[]{:S(2)}, u32[]{:S(2)}) %collective-permute-start.24) | collective-permute-done | bytes 131104 | tf_op jit(solution)/shard_map/ppermute | solution.py:16
  116.9 4.3 %collective-permute-done.23.refs_2_ = bf16[128,512]{1,0:T(8,128)(2,1)S(1)} collective-permute-done((bf16[128,512]{1,0:T(8,128)(2,1)S(1)}, bf16[128,512]{1,0:T(8,128)(2,1)S(1)}, u32[]{:S(2)}, u32[]{:S(2)}) %collective-permute-start.23) | collective-permute-done | bytes 131104 | tf_op jit(solution)/shard_map/ppermute | solution.py:16
  121.2 1.1 dispatch.3
  122.4 23.8 %all_to_all.20.own_ref = bf16[4,400,512]{2,1,0:T(8,128)(2,1)S(1)} all-to-all(bf16[4,400,512]{2,1,0:T(8,128)(2,1)S(1)} %dispatch.3), channel_id=1, replica_groups=mesh['expert'=4,'fsdp'=8] {'expert'}, dimensions={0} | all-to-all | bytes 3276800 | tf_op jit(solution)/shard_map/all_to_all | solution.py:452
  146.1 2.2 collective-permute-start.17
  148.3 2.2 collective-permute-start.15
  150.5 3.8 %collective-permute-done.17.refs_3_ = bf16[128,512]{1,0:T(8,128)(2,1)S(1)} collective-permute-done((bf16[128,512]{1,0:T(8,128)(2,1)S(1)}, bf16[128,512]{1,0:T(8,128)(2,1)S(1)}, u32[]{:S(2)}, u32[]{:S(2)}) %collective-permute-start.17) | collective-permute-done | bytes 131104 | tf_op jit(solution)/shard_map/ppermute | solution.py:16
  154.4 5.1 %collective-permute-done.16.refs_2_ = bf16[128,512]{1,0:T(8,128)(2,1)S(1)} collective-permute-done((bf16[128,512]{1,0:T(8,128)(2,1)S(1)}, bf16[128,512]{1,0:T(8,128)(2,1)S(1)}, u32[]{:S(2)}, u32[]{:S(2)}) %collective-permute-start.16) | collective-permute-done | bytes 131104 | tf_op jit(solution)/shard_map/ppermute | solution.py:16
  159.5 2.3 %dispatch.2 = bf16[4,400,512]{2,1,0:T(8,128)(2,1)} custom-call(s32[3]{0:T(128)S(1)} %pad_add_fusion.position_ref, s32[8,4,128]{2,1,0:T(4,128)S(1)} %bitcast.96, bf16[16,1024]{1,0:T(8,128)(2,1)S(1)} %fusion.24.extra_ref, bf16[128,512]{1,0:T(8,128)(2,1)S(1)} %get-tuple-element.62.refs_0_, bf16[128,512]{1,0:T(8,128)(2,1)S(1)} %collective-permute-done.15.refs_1_, ...), custom_call_target="tpu_custom_call" | custom-call | tf_op jit(solution)/shard_map/dispatch/pallas_call | solution.py:441
  161.8 3.7 %all-to-all-start.2 = ((bf16[4,400,512]{2,1,0:T(8,128)(2,1)}), bf16[4,400,512]{2,1,0:T(8,128)(2,1)S(1)}, u32[]{:S(2)}, u32[]{:S(2)}) async-start(bf16[4,400,512]{2,1,0:T(8,128)(2,1)} %dispatch.2), calls=%async_computation.2 | async-start | bytes 3276800 | tf_op jit(solution)/shard_map/all_to_all | solution.py:452
  165.5 13.4 %early.1 = (f32[768,1024]{1,0:T(8,128)}, f32[768,1024]{1,0:T(8,128)}, f32[768,16]{1,0:T(8,128)S(1)}, bf16[4,512,768]{2,1,0:T(8,128)(2,1)}) custom-call(bf16[4,400,512]{2,1,0:T(8,128)(2,1)S(1)} %all_to_all.20.own_ref, bf16[4,400,512]{2,1,0:T(8,128)(2,1)} %collective-permute-done.25.other_ref, bf16[4,2,512,1024]{3,2,1,0:T(8,128)(2,1)} %bitcast.102, ...), custom_call_target="tpu_custom_call" | custom-call | flops 6442450944 | bytes 8388608 | tf_op jit(solution)/shard_map/early/pallas_call | solution.py:462
  179.0 0.7 copy-done.1
  179.7 6.1 %all-to-all-done.2.own_ref = bf16[4,400,512]{2,1,0:T(8,128)(2,1)S(1)} async-done(((bf16[4,400,512]{2,1,0:T(8,128)(2,1)}), bf16[4,400,512]{2,1,0:T(8,128)(2,1)S(1)}, u32[]{:S(2)}, u32[]{:S(2)}) %all-to-all-start.2) | async-done | bytes 1638432 | tf_op jit(solution)/shard_map/all_to_all | solution.py:452
  185.8 0.8 signs.1
  186.6 2.3 %pad_maximum_fusion = bf16[512,1024]{1,0:T(8,128)(2,1)} fusion(bf16[512,512]{1,0:T(8,128)(2,1)} %copy-done.4, bf16[512,512]{1,0:T(8,128)(2,1)} %copy-done.3), kind=kLoop, calls=%fused_computation.8 | loop fusion | flops 2097152 | bytes 2097152 | tf_op jit(solution)/shard_map/concatenate | solution.py:536
  188.9 0.4 collective-permute-done.26.other_ref
  189.3 1.2 copy-done.6
  190.4 1.0 copy-done.2
  191.4 30.7 %late.1 = (bf16[4,2,96,1024]{3,2,1,0:T(8,128)(2,1)}, bf16[4,2,512,1024]{3,2,1,0:T(8,128)(2,1)}, bf16[4,2,512,1024]{3,2,1,0:T(8,128)(2,1)}) custom-call(s32[3]{0:T(128)S(1)} %pad_add_fusion.position_ref, bf16[4,400,512]{2,1,0:T(8,128)(2,1)S(1)} %all-to-all-done.2.own_ref, bf16[4,400,512]{2,1,0:T(8,128)(2,1)} %copy-done.6, ...), custom_call_target="tpu_custom_call" | custom-call | tf_op jit(solution)/shard_map/late/pallas_call | solution.py:499
  (61 shorter events, 1.2 us)
Async XLA Ops:
  2.6 15.9 %collective-permute-start = (bf16[2,256,512]{2,1,0:T(8,128)(2,1)S(1)}, bf16[2,256,512]{2,1,0:T(8,128)(2,1)}, u32[]{:S(2)}, u32[]{:S(2)}) collective-permute-start(bf16[2,256,512]{2,1,0:T(8,128)(2,1)S(1)} %get-tuple-element.26), channel_id=1, source_target_pairs={{0,8},{8,0},{16,24},{24,16},{1,9},{9,1},{17,25},{25,17},{2,10},{10... | collective-permute-start | bytes 1572872 | tf_op jit(solution)/shard_map/ppermute | solution.py:16
  5.6 15.6 %collective-permute-start.2 = (bf16[2,256,512]{2,1,0:T(8,128)(2,1)S(1)}, bf16[2,256,512]{2,1,0:T(8,128)(2,1)S(1)}, u32[]{:S(2)}, u32[]{:S(2)}) collective-permute-start(bf16[2,256,512]{2,1,0:T(8,128)(2,1)S(1)} %get-tuple-element.27), channel_id=1, source_target_pairs={{0,16},{8,24},{16,0},{24,8},{1,17},{9,25},{17,1},{25,9},{2,18},{10... | collective-permute-start | bytes 1572872 | tf_op jit(solution)/shard_map/ppermute | solution.py:16
  7.1 15.6 %all-to-all-start = ((bf16[4,32,1024]{2,1,0:T(8,128)(2,1)}), bf16[4,32,1024]{2,1,0:T(8,128)(2,1)S(1)}, u32[]{:S(2)}, u32[]{:S(2)}) async-start(bf16[4,32,1024]{2,1,0:T(8,128)(2,1)} %bitcast.8), calls=%async_computation | async-start | bytes 524288 | tf_op jit(solution)/shard_map/all_to_all | solution.py:318
  10.5 12.1 %copy-start.14 = (s32[128,2]{0,1:T(2,128)S(1)}, s32[128,2]{0,1:T(2,128)}, u32[]{:S(2)}) copy-start(s32[128,2]{0,1:T(2,128)} %param.17) | copy-start | bytes 3076
  10.5 12.1 %copy-start.15 = (s32[128,2]{0,1:T(2,128)S(1)}, s32[128,2]{0,1:T(2,128)}, u32[]{:S(2)}) copy-start(s32[128,2]{0,1:T(2,128)} %param.18) | copy-start | bytes 3076
  21.1 46.9 %copy-start.7 = (bf16[2,256,512]{2,1,0:T(8,128)(2,1)}, bf16[2,256,512]{2,1,0:T(8,128)(2,1)S(1)}, u32[]{:S(2)}) copy-start(bf16[2,256,512]{2,1,0:T(8,128)(2,1)S(1)} %collective-permute-done.2) | copy-start | bytes 1572868
  21.1 17.5 %collective-permute-start.4 = (bf16[2,256,512]{2,1,0:T(8,128)(2,1)S(1)}, bf16[2,256,512]{2,1,0:T(8,128)(2,1)S(1)}, u32[]{:S(2)}, u32[]{:S(2)}) collective-permute-start(bf16[2,256,512]{2,1,0:T(8,128)(2,1)S(1)} %get-tuple-element.30), channel_id=1, source_target_pairs={{0,8},{8,0},{16,24},{24,16},{1,9},{9,1},{17,25},{25,17},{2,10},{10... | collective-permute-start | bytes 1572872 | tf_op jit(solution)/shard_map/ppermute | solution.py:16
  21.2 17.5 %collective-permute-start.5 = (bf16[2,256,512]{2,1,0:T(8,128)(2,1)S(1)}, bf16[2,256,512]{2,1,0:T(8,128)(2,1)}, u32[]{:S(2)}, u32[]{:S(2)}) collective-permute-start(bf16[2,256,512]{2,1,0:T(8,128)(2,1)S(1)} %get-tuple-element.31), channel_id=1, source_target_pairs={{0,16},{8,24},{16,0},{24,8},{1,17},{9,25},{17,1},{25,9},{2,18},{10... | collective-permute-start | bytes 1572872 | tf_op jit(solution)/shard_map/ppermute | solution.py:16
  23.4 19.5 %all-to-all-start.1 = ((bf16[8,48,512]{2,1,0:T(8,128)(2,1)}), bf16[8,48,512]{2,1,0:T(8,128)(2,1)S(1)}, u32[]{:S(2)}, u32[]{:S(2)}) async-start(bf16[8,48,512]{2,1,0:T(8,128)(2,1)} %spread.1), calls=%async_computation.1 | async-start | bytes 786432 | tf_op jit(solution)/shard_map/all_to_all | solution.py:331
  29.4 9.2 %collective-permute-start.1 = (bf16[1,256,512]{2,1,0:T(8,128)(2,1)S(1)}, bf16[1,256,512]{2,1,0:T(8,128)(2,1)S(1)}, u32[]{:S(2)}, u32[]{:S(2)}) collective-permute-start(bf16[1,256,512]{2,1,0:T(8,128)(2,1)S(1)} %add_convert_fusion.3), channel_id=1, source_target_pairs={{0,16},{8,24},{16,0},{24,8},{1,17},{9,25},{17,1},{25,9},{2,18},{10... | collective-permute-start | bytes 786440 | tf_op jit(solution)/shard_map/ppermute | solution.py:16
  38.6 5.7 %copy-start.8 = (bf16[2,256,512]{2,1,0:T(8,128)(2,1)}, bf16[2,256,512]{2,1,0:T(8,128)(2,1)S(1)}, u32[]{:S(2)}) copy-start(bf16[2,256,512]{2,1,0:T(8,128)(2,1)S(1)} %collective-permute-done.4) | copy-start | bytes 1572868
  41.3 9.2 %collective-permute-start.3 = (bf16[1,256,512]{2,1,0:T(8,128)(2,1)S(1)}, bf16[1,256,512]{2,1,0:T(8,128)(2,1)S(1)}, u32[]{:S(2)}, u32[]{:S(2)}) collective-permute-start(bf16[1,256,512]{2,1,0:T(8,128)(2,1)S(1)} %get-tuple-element.50), channel_id=1, source_target_pairs={{0,8},{8,0},{16,24},{24,16},{1,9},{9,1},{17,25},{25,17},{2,10},{10... | collective-permute-start | bytes 786440 | tf_op jit(solution)/shard_map/ppermute | solution.py:16
  43.0 17.1 %collective-permute-start.10 = (bf16[8,48,512]{2,1,0:T(8,128)(2,1)S(1)}, bf16[8,48,512]{2,1,0:T(8,128)(2,1)S(1)}, u32[]{:S(2)}, u32[]{:S(2)}) collective-permute-start(bf16[8,48,512]{2,1,0:T(8,128)(2,1)S(1)} %all-to-all-done.1), channel_id=1, source_target_pairs={{0,24},{8,16},{16,8},{24,0},{1,25},{9,17},{17,9},{25,1},{2,26},{10... | collective-permute-start | bytes 1179656 | tf_op jit(solution)/shard_map/ppermute | solution.py:16
  44.3 20.5 %collective-permute-start.9 = (bf16[8,48,512]{2,1,0:T(8,128)(2,1)S(1)}, bf16[8,48,512]{2,1,0:T(8,128)(2,1)S(1)}, u32[]{:S(2)}, u32[]{:S(2)}) collective-permute-start(bf16[8,48,512]{2,1,0:T(8,128)(2,1)S(1)} %all-to-all-done.1), channel_id=1, source_target_pairs={{0,16},{8,24},{16,0},{24,8},{1,17},{9,25},{17,1},{25,9},{2,18},{10... | collective-permute-start | bytes 1179656 | tf_op jit(solution)/shard_map/ppermute | solution.py:16
  44.8 22.6 %collective-permute-start.8 = (bf16[8,48,512]{2,1,0:T(8,128)(2,1)S(1)}, bf16[8,48,512]{2,1,0:T(8,128)(2,1)S(1)}, u32[]{:S(2)}, u32[]{:S(2)}) collective-permute-start(bf16[8,48,512]{2,1,0:T(8,128)(2,1)S(1)} %all-to-all-done.1), channel_id=1, source_target_pairs={{0,8},{8,0},{16,24},{24,16},{1,9},{9,1},{17,25},{25,17},{2,10},{10... | collective-permute-start | bytes 1179656 | tf_op jit(solution)/shard_map/ppermute | solution.py:16
  50.5 17.8 %collective-permute-start.6 = (bf16[1,256,512]{2,1,0:T(8,128)(2,1)}, bf16[1,256,512]{2,1,0:T(8,128)(2,1)S(1)}, u32[]{:S(2)}, u32[]{:S(2)}) collective-permute-start(bf16[1,256,512]{2,1,0:T(8,128)(2,1)} %get-tuple-element.32), channel_id=1, source_target_pairs={{0,16},{8,24},{16,0},{24,8},{1,17},{9,25},{17,1},{25,9},{2,18},{10... | collective-permute-start | bytes 786440 | tf_op jit(solution)/shard_map/ppermute | solution.py:16
  52.1 19.8 %collective-permute-start.7 = (bf16[1,256,512]{2,1,0:T(8,128)(2,1)}, bf16[1,256,512]{2,1,0:T(8,128)(2,1)}, u32[]{:S(2)}, u32[]{:S(2)}) collective-permute-start(bf16[1,256,512]{2,1,0:T(8,128)(2,1)} %get-tuple-element.33), channel_id=1, source_target_pairs={{0,8},{8,0},{16,24},{24,16},{1,9},{9,1},{17,25},{25,17},{2,10},{10... | collective-permute-start | bytes 786440 | tf_op jit(solution)/shard_map/ppermute | solution.py:16
  53.2 20.6 %copy-start.5 = (f32[256,512]{1,0:T(8,128)S(1)}, f32[256,512]{1,0:T(8,128)}, u32[]{:S(2)}) copy-start(f32[256,512]{1,0:T(8,128)} %get-tuple-element.48) | copy-start | bytes 1572868
  68.4 0.7 copy-start.9
  73.9 33.3 %copy-start.3 = (bf16[512,512]{1,0:T(8,128)(2,1)}, bf16[512,512]{1,0:T(8,128)(2,1)S(1)}, u32[]{:S(2)}) copy-start(bf16[512,512]{1,0:T(8,128)(2,1)S(1)} %fusion) | copy-start | bytes 1572868
  75.2 2.3 %collective-permute-start.18 = (bf16[4,128,512]{2,1,0:T(8,128)(2,1)}, bf16[4,128,512]{2,1,0:T(8,128)(2,1)}, u32[]{:S(2)}, u32[]{:S(2)}) collective-permute-start(bf16[4,128,512]{2,1,0:T(8,128)(2,1)} %convolution_convert_fusion), channel_id=1, source_target_pairs={{0,1},{1,0},{2,3},{3,2},{4,5},{5,4},{6,7},{7,6},{8,9},{9,8},{10,11... | collective-permute-start | bytes 1572872 | tf_op jit(solution)/shard_map/ppermute | solution.py:16
  75.3 46.0 %copy-start.4 = (bf16[512,512]{1,0:T(8,128)(2,1)}, bf16[512,512]{1,0:T(8,128)(2,1)S(1)}, u32[]{:S(2)}) copy-start(bf16[512,512]{1,0:T(8,128)(2,1)S(1)} %fusion.1) | copy-start | bytes 1572868
  76.5 7.2 %collective-permute-start.11 = (bf16[4,128,512]{2,1,0:T(8,128)(2,1)}, bf16[4,128,512]{2,1,0:T(8,128)(2,1)}, u32[]{:S(2)}, u32[]{:S(2)}) collective-permute-start(bf16[4,128,512]{2,1,0:T(8,128)(2,1)} %convolution_convert_fusion.1), channel_id=1, source_target_pairs={{0,1},{1,0},{2,3},{3,2},{4,5},{5,4},{6,7},{7,6},{8,9},{9,8},{10,11... | collective-permute-start | bytes 1572872 | tf_op jit(solution)/shard_map/ppermute | solution.py:16
  77.4 15.0 %copy-start.12 = (bf16[1024]{0:T(1024)(128)(2,1)S(1)}, bf16[1024]{0:T(1024)(128)(2,1)}, u32[]{:S(2)}) copy-start(bf16[1024]{0:T(1024)(128)(2,1)} %param.13) | copy-start | bytes 6148
  77.4 15.0 %copy-start.13 = (bf16[1024,4]{0,1:T(4,128)(2,1)S(1)}, bf16[1024,4]{0,1:T(4,128)(2,1)}, u32[]{:S(2)}) copy-start(bf16[1024,4]{0,1:T(4,128)(2,1)} %param.14) | copy-start | bytes 24580
  77.4 29.8 %copy-start.10 = (bf16[128,1024]{1,0:T(8,128)(2,1)S(1)}, bf16[128,1024]{1,0:T(8,128)(2,1)}, u32[]{:S(2)}) copy-start(bf16[128,1024]{1,0:T(8,128)(2,1)} %param.12) | copy-start | bytes 786436
  79.7 12.1 %collective-permute-start.19 = (bf16[128,512]{1,0:T(8,128)(2,1)S(1)}, bf16[128,512]{1,0:T(8,128)(2,1)S(1)}, u32[]{:S(2)}, u32[]{:S(2)}) collective-permute-start(bf16[128,512]{1,0:T(8,128)(2,1)S(1)} %get-tuple-element.55), channel_id=1, source_target_pairs={{0,2},{1,3},{2,0},{3,1},{4,6},{5,7},{6,4},{7,5},{8,10},{9,11},{10,... | collective-permute-start | bytes 393224 | tf_op jit(solution)/shard_map/ppermute | solution.py:16
  81.1 11.4 %collective-permute-start.21 = (bf16[128,512]{1,0:T(8,128)(2,1)}, bf16[128,512]{1,0:T(8,128)(2,1)}, u32[]{:S(2)}, u32[]{:S(2)}) collective-permute-start(bf16[128,512]{1,0:T(8,128)(2,1)} %get-tuple-element.56), channel_id=1, source_target_pairs={{0,6},{1,7},{2,4},{3,5},{4,2},{5,3},{6,0},{7,1},{8,14},{9,15},{10,... | collective-permute-start | bytes 393224 | tf_op jit(solution)/shard_map/ppermute | solution.py:16
  83.7 18.7 %collective-permute-start.20 = (bf16[128,512]{1,0:T(8,128)(2,1)S(1)}, bf16[128,512]{1,0:T(8,128)(2,1)}, u32[]{:S(2)}, u32[]{:S(2)}) collective-permute-start(bf16[128,512]{1,0:T(8,128)(2,1)S(1)} %get-tuple-element.57), channel_id=1, source_target_pairs={{0,4},{1,5},{2,6},{3,7},{4,0},{5,1},{6,2},{7,3},{8,12},{9,13},{10,... | collective-permute-start | bytes 393224 | tf_op jit(solution)/shard_map/ppermute | solution.py:16
  87.3 15.1 %collective-permute-start.12 = (bf16[128,512]{1,0:T(8,128)(2,1)S(1)}, bf16[128,512]{1,0:T(8,128)(2,1)S(1)}, u32[]{:S(2)}, u32[]{:S(2)}) collective-permute-start(bf16[128,512]{1,0:T(8,128)(2,1)S(1)} %get-tuple-element.58), channel_id=1, source_target_pairs={{0,2},{1,3},{2,0},{3,1},{4,6},{5,7},{6,4},{7,5},{8,10},{9,11},{10,... | collective-permute-start | bytes 393224 | tf_op jit(solution)/shard_map/ppermute | solution.py:16
  89.2 13.2 %collective-permute-start.14 = (bf16[128,512]{1,0:T(8,128)(2,1)S(1)}, bf16[128,512]{1,0:T(8,128)(2,1)}, u32[]{:S(2)}, u32[]{:S(2)}) collective-permute-start(bf16[128,512]{1,0:T(8,128)(2,1)S(1)} %get-tuple-element.59), channel_id=1, source_target_pairs={{0,6},{1,7},{2,4},{3,5},{4,2},{5,3},{6,0},{7,1},{8,14},{9,15},{10,... | collective-permute-start | bytes 393224 | tf_op jit(solution)/shard_map/ppermute | solution.py:16
  91.8 0.7 copy-start.11
  91.8 15.4 %collective-permute-start.13 = (bf16[128,512]{1,0:T(8,128)(2,1)S(1)}, bf16[128,512]{1,0:T(8,128)(2,1)}, u32[]{:S(2)}, u32[]{:S(2)}) collective-permute-start(bf16[128,512]{1,0:T(8,128)(2,1)S(1)} %get-tuple-element.60), channel_id=1, source_target_pairs={{0,4},{1,5},{2,6},{3,7},{4,0},{5,1},{6,2},{7,3},{8,12},{9,13},{10,... | collective-permute-start | bytes 393224 | tf_op jit(solution)/shard_map/ppermute | solution.py:16
  108.6 8.3 %collective-permute-start.24 = (bf16[128,512]{1,0:T(8,128)(2,1)S(1)}, bf16[128,512]{1,0:T(8,128)(2,1)S(1)}, u32[]{:S(2)}, u32[]{:S(2)}) collective-permute-start(bf16[128,512]{1,0:T(8,128)(2,1)S(1)} %get-tuple-element.61.refs_0_), channel_id=1, source_target_pairs={{0,6},{1,7},{2,4},{3,5},{4,2},{5,3},{6,0},{7,1},{8,14},{9,15},{10,... | collective-permute-start | bytes 393224 | tf_op jit(solution)/shard_map/ppermute | solution.py:16
  111.3 9.9 %collective-permute-start.23 = (bf16[128,512]{1,0:T(8,128)(2,1)S(1)}, bf16[128,512]{1,0:T(8,128)(2,1)S(1)}, u32[]{:S(2)}, u32[]{:S(2)}) collective-permute-start(bf16[128,512]{1,0:T(8,128)(2,1)S(1)} %get-tuple-element.61.refs_0_), channel_id=1, source_target_pairs={{0,4},{1,5},{2,6},{3,7},{4,0},{5,1},{6,2},{7,3},{8,12},{9,13},{10,... | collective-permute-start | bytes 393224 | tf_op jit(solution)/shard_map/ppermute | solution.py:16
  111.3 9.9 %collective-permute-start.22 = (bf16[128,512]{1,0:T(8,128)(2,1)S(1)}, bf16[128,512]{1,0:T(8,128)(2,1)S(1)}, u32[]{:S(2)}, u32[]{:S(2)}) collective-permute-start(bf16[128,512]{1,0:T(8,128)(2,1)S(1)} %get-tuple-element.61.refs_0_), channel_id=1, source_target_pairs={{0,2},{1,3},{2,0},{3,1},{4,6},{5,7},{6,4},{7,5},{8,10},{9,11},{10,... | collective-permute-start | bytes 393224 | tf_op jit(solution)/shard_map/ppermute | solution.py:16
  146.1 19.4 %collective-permute-start.25 = (bf16[4,400,512]{2,1,0:T(8,128)(2,1)S(1)}, bf16[4,400,512]{2,1,0:T(8,128)(2,1)}, u32[]{:S(2)}, u32[]{:S(2)}) collective-permute-start(bf16[4,400,512]{2,1,0:T(8,128)(2,1)S(1)} %all_to_all.20.own_ref), channel_id=1, source_target_pairs={{0,1},{1,0},{2,3},{3,2},{4,5},{5,4},{6,7},{7,6},{8,9},{9,8},{10,11... | collective-permute-start | bytes 4915208 | tf_op jit(solution)/shard_map/ppermute | solution.py:16
  146.1 8.2 %collective-permute-start.17 = (bf16[128,512]{1,0:T(8,128)(2,1)S(1)}, bf16[128,512]{1,0:T(8,128)(2,1)S(1)}, u32[]{:S(2)}, u32[]{:S(2)}) collective-permute-start(bf16[128,512]{1,0:T(8,128)(2,1)S(1)} %get-tuple-element.62.refs_0_), channel_id=1, source_target_pairs={{0,6},{1,7},{2,4},{3,5},{4,2},{5,3},{6,0},{7,1},{8,14},{9,15},{10,... | collective-permute-start | bytes 393224 | tf_op jit(solution)/shard_map/ppermute | solution.py:16
  148.3 11.2 %collective-permute-start.16 = (bf16[128,512]{1,0:T(8,128)(2,1)S(1)}, bf16[128,512]{1,0:T(8,128)(2,1)S(1)}, u32[]{:S(2)}, u32[]{:S(2)}) collective-permute-start(bf16[128,512]{1,0:T(8,128)(2,1)S(1)} %get-tuple-element.62.refs_0_), channel_id=1, source_target_pairs={{0,4},{1,5},{2,6},{3,7},{4,0},{5,1},{6,2},{7,3},{8,12},{9,13},{10,... | collective-permute-start | bytes 393224 | tf_op jit(solution)/shard_map/ppermute | solution.py:16
  148.3 11.2 %collective-permute-start.15 = (bf16[128,512]{1,0:T(8,128)(2,1)S(1)}, bf16[128,512]{1,0:T(8,128)(2,1)S(1)}, u32[]{:S(2)}, u32[]{:S(2)}) collective-permute-start(bf16[128,512]{1,0:T(8,128)(2,1)S(1)} %get-tuple-element.62.refs_0_), channel_id=1, source_target_pairs={{0,2},{1,3},{2,0},{3,1},{4,6},{5,7},{6,4},{7,5},{8,10},{9,11},{10,... | collective-permute-start | bytes 393224 | tf_op jit(solution)/shard_map/ppermute | solution.py:16
  161.8 24.0 %all-to-all-start.2 = ((bf16[4,400,512]{2,1,0:T(8,128)(2,1)}), bf16[4,400,512]{2,1,0:T(8,128)(2,1)S(1)}, u32[]{:S(2)}, u32[]{:S(2)}) async-start(bf16[4,400,512]{2,1,0:T(8,128)(2,1)} %dispatch.2), calls=%async_computation.2 | async-start | bytes 3276800 | tf_op jit(solution)/shard_map/all_to_all | solution.py:452
  179.0 0.7 copy-start.1
  179.7 10.8 %copy-start = (bf16[1,768,1024]{2,1,0:T(8,128)(2,1)S(1)}, bf16[1,768,1024]{2,1,0:T(8,128)(2,1)}, u32[]{:S(2)}) copy-start(bf16[1,768,1024]{2,1,0:T(8,128)(2,1)} %param.19) | copy-start | bytes 4718596
  185.8 3.5 %collective-permute-start.26 = (bf16[4,400,512]{2,1,0:T(8,128)(2,1)S(1)}, bf16[4,400,512]{2,1,0:T(8,128)(2,1)S(1)}, u32[]{:S(2)}, u32[]{:S(2)}) collective-permute-start(bf16[4,400,512]{2,1,0:T(8,128)(2,1)S(1)} %all-to-all-done.2.own_ref), channel_id=1, source_target_pairs={{0,1},{1,0},{2,3},{3,2},{4,5},{5,4},{6,7},{7,6},{8,9},{9,8},{10,11... | collective-permute-start | bytes 4915208 | tf_op jit(solution)/shard_map/ppermute | solution.py:16
  189.3 1.2 copy-start.6
  190.4 1.0 copy-start.2
